TPU v7x, 32 devices: a whole 2x2x4 slice. The times are simulated.
32 devices in a mesh: slab: 8 (over y, x, core), blk: 4 (over z).
Axes of the slice: x: 2, y: 2, z: 4, core: 2. Of those that a mesh axis runs over, the one named last changes fastest.
Arguments:
- queries: bfloat16 [1024, 768], P(('slab', 'blk')), may hold values from -6 to 6
- passages: bfloat16 [1024, 768], P(('blk', 'slab')), may hold values from -6 to 6
- query_lognorm: float32 [1024], P(('slab', 'blk')), as said below
- passage_lognorm: float32 [1024], P('blk'), as said below
- loss_cotangent: float32 [], replicated, may hold values from 4 to 12
Outputs:
- query_gradient: float32 [1024, 768], P(('slab', 'blk'))
- passage_gradient: float32 [1024, 768], P(('blk', 'slab'))
Inputs may be any that keep to these rules, and one draw needn't show every extreme that they name: `query_lognorm`: every entry lies between log(1024) + 0.5 and log(1024) + 3.5. `passage_lognorm`: every entry lies between log(1024) + 0.5 and log(1024) + 3.5.
All inputs are finite; a program needn't handle non-finite values.
Results may differ from a plain program's by a relative error of at most 0.034.
Values may be sent and summed in bfloat16 or wider, within the bound.
No kernel may reach another device: no remote copies, remote signals or barrier semaphores. Data moves between devices by JAX's collectives and lax.ppermute only.
A program may use at most 64 MiB of HBM per device.

v0:
```python
import math

import jax
import jax.numpy as jnp
from jax import lax
from jax.sharding import PartitionSpec as P


def passed_along(block, axis, distance):
    devices = range(lax.axis_size(axis))
    route = [((i - distance) % len(devices), i) for i in devices]
    return lax.ppermute(block, axis, route)


def tile_gradients(
    query_rows,
    query_norms,
    row_numbers,
    passage_block,
    block_wide,
    block_norms,
    column_start,
    score_scale,
    half_cotangent,
):
    scores = score_scale * lax.dot_general(
        query_rows, passage_block, (((1,), (1,)), ((), ())), preferred_element_type=jnp.float32
    )
    column_numbers = column_start + lax.broadcasted_iota(jnp.int32, scores.shape, 1)
    paired = (row_numbers[:, None] == column_numbers).astype(jnp.float32)
    weights = half_cotangent * (
        jnp.exp(scores - query_norms[:, None])
        + jnp.exp(scores - block_norms[None, :])
        - 2.0 * paired
    )
    rows_wide = query_rows.astype(jnp.float32)
    query_term = score_scale * jnp.dot(
        weights, block_wide, precision=lax.Precision.HIGHEST, preferred_element_type=jnp.float32
    )
    passage_term = score_scale * lax.dot_general(
        weights,
        rows_wide,
        (((0,), (0,)), ((), ())),
        precision=lax.Precision.HIGHEST,
        preferred_element_type=jnp.float32,
    )
    return (query_term, passage_term)


def local(queries, passages, query_lognorm, passage_lognorm, loss_cotangent):
    per_device = queries.shape[0]
    feature_width = queries.shape[1]
    score_scale = 2.0 / math.sqrt(feature_width)
    half_cotangent = 0.5 * loss_cotangent
    cycle_count = lax.axis_size("blk")
    slab_index = lax.axis_index("slab")
    cycle_index = lax.axis_index("blk")
    passage_block = lax.all_gather(passages, "slab", axis=0, tiled=True)
    block_wide = passage_block.astype(jnp.float32)
    column_start = cycle_index * passage_block.shape[0]
    local_index = lax.broadcasted_iota(jnp.int32, (per_device,), 0)
    block_start = jnp.zeros(passage_block.shape, jnp.float32)

    def owner_offset(source_index):
        return (slab_index * cycle_count + source_index) * per_device

    def advance(cycle_turn, state_carry):
        query_rows, query_norms, carried_sum, block_total = state_carry
        source_index = (cycle_index - cycle_turn) % cycle_count
        query_term, passage_term = tile_gradients(
            query_rows,
            query_norms,
            owner_offset(source_index) + local_index,
            passage_block,
            block_wide,
            passage_lognorm,
            column_start,
            score_scale,
            half_cotangent,
        )
        query_rows = passed_along(query_rows, "blk", 1)
        query_norms, carried_sum = passed_along((query_norms, carried_sum + query_term), "blk", 1)
        return (query_rows, query_norms, carried_sum, block_total + passage_term)

    state_carry = (queries, query_lognorm, jnp.zeros(queries.shape, jnp.float32), block_start)
    state_carry = lax.fori_loop(0, cycle_count, advance, state_carry)
    query_gradient = state_carry[2]
    block_total = state_carry[3]
    passage_gradient = lax.psum_scatter(block_total, "slab", scatter_dimension=0, tiled=True)
    return (query_gradient, passage_gradient)


def solution(mesh):
    return jax.shard_map(
        local,
        mesh=mesh,
        in_specs=(
            P(("slab", "blk"), None),
            P(("blk", "slab"), None),
            P(("slab", "blk")),
            P("blk"),
            P(),
        ),
        out_specs=(P(("slab", "blk"), None), P(("blk", "slab"), None)),
        check_vma=False,
    )
```

profile of v0, /device:TPU:0, one launch (start us, length us, event | category | flops | bytes accessed | tf_op | source)
XLA Modules:
  0.0 99.4 jit_solution(8065582783891211725)
XLA Ops:
  7.2 0.0 reduce-scatter.2.cloned.1.call-start
  7.9 0.1 copy-done.2
  8.0 11.0 %all_gather.3 = bf16[256,768]{1,0:T(8,128)(2,1)S(1)} all-gather(bf16[32,768]{1,0:T(8,128)(2,1)S(1)} %copy-done.2), channel_id=1, replica_groups=mesh['slab'=8,'blk'=4] {'slab'}, dimensions={0}, use_global_device_ids=true | all-gather | bytes 442368 | tf_op jit(solution)/shard_map/all_gather | solution.py:58
  19.0 0.1 convert_element_type.9
  19.1 0.0 copy-start.1
  19.1 0.0 copy-start.3
  19.1 0.0 copy-start.4
  19.1 0.7 copy-done.1
  19.9 36.8 %while.22 = (s32[]{:T(128)}, bf16[32,768]{1,0:T(8,128)(2,1)S(1)}, f32[32]{0:T(128)S(1)}, f32[32,768]{1,0:T(8,128)S(1)}, f32[256,768]{1,0:T(8,128)S(1)}, /*index=...) while((s32[]{:T(128)}, bf16[32,768]{1,0:T(8,128)(2,1)S(1)}, ...), condition=%wide.region_1.2_spmd.clone, body=%wide.region_0.1_spmd.clone.sunk | while | flops 164282672 | bytes 3838524 | solution.py:86
  19.9 1.6 %collective-permute-start.1 = (f32[32]{0:T(128)S(1)}, f32[32]{0:T(128)S(1)}, u32[]{:S(2)}, u32[]{:S(2)}) collective-permute-start(f32[32]{0:T(128)S(1)} %copy.14), channel_id=1, source_target_pairs={{3,0},{0,1},{1,2},{2,3},{7,4},{4,5},{5,6},{6,7},{11,8},{8,9},{9,10... | collective-permute-start | bytes 392 | tf_op jit(solution)/shard_map/while/body/eval_jaxpr/ppermute | solution.py:12
  21.5 1.6 %collective-permute-start = (bf16[32,768]{1,0:T(8,128)(2,1)S(1)}, bf16[32,768]{1,0:T(8,128)(2,1)S(1)}, u32[]{:S(2)}, u32[]{:S(2)}) collective-permute-start(bf16[32,768]{1,0:T(8,128)(2,1)S(1)} %copy.13), channel_id=1, source_target_pairs={{3,0},{0,1},{1,2},{2,3},{7,4},{4,5},{5,6},{6,7},{11,8},{8,9},{9,10... | collective-permute-start | bytes 147464 | tf_op jit(solution)/shard_map/while/body/eval_jaxpr/ppermute | solution.py:12
  23.1 0.3 subtract_multiply_fusion.2
  23.4 0.6 fusion.24
  24.0 1.6 %collective-permute-start.2 = (f32[32,768]{1,0:T(8,128)S(1)}, f32[32,768]{1,0:T(8,128)S(1)}, u32[]{:S(2)}, u32[]{:S(2)}) collective-permute-start(f32[32,768]{1,0:T(8,128)S(1)} %fusion.24), channel_id=1, source_target_pairs={{3,0},{0,1},{1,2},{2,3},{7,4},{4,5},{5,6},{6,7},{11,8},{8,9},{9,10... | collective-permute-start | bytes 294920 | tf_op jit(solution)/shard_map/while/body/eval_jaxpr/ppermute | solution.py:12
  25.6 0.7 fusion.25
  26.3 0.0 collective-permute-done.1
  26.3 1.1 %collective-permute-done = bf16[32,768]{1,0:T(8,128)(2,1)S(1)} collective-permute-done((bf16[32,768]{1,0:T(8,128)(2,1)S(1)}, bf16[32,768]{1,0:T(8,128)(2,1)S(1)}, u32[]{:S(2)}, u32[]{:S(2)}) %collective-permute-start) | collective-permute-done | bytes 49184 | tf_op jit(solution)/shard_map/while/body/eval_jaxpr/ppermute | solution.py:12
  27.4 3.0 %collective-permute-done.2 = f32[32,768]{1,0:T(8,128)S(1)} collective-permute-done((f32[32,768]{1,0:T(8,128)S(1)}, f32[32,768]{1,0:T(8,128)S(1)}, u32[]{:S(2)}, u32[]{:S(2)}) %collective-permute-start.2) | collective-permute-done | bytes 98336 | tf_op jit(solution)/shard_map/while/body/eval_jaxpr/ppermute | solution.py:12
  30.4 0.0 collective-permute-start.1
  30.4 0.4 collective-permute-start
  30.9 0.3 subtract_multiply_fusion.2
  31.2 0.6 fusion.24
  31.7 1.2 %collective-permute-start.2 = (f32[32,768]{1,0:T(8,128)S(1)}, f32[32,768]{1,0:T(8,128)S(1)}, u32[]{:S(2)}, u32[]{:S(2)}) collective-permute-start(f32[32,768]{1,0:T(8,128)S(1)} %fusion.24), channel_id=1, source_target_pairs={{3,0},{0,1},{1,2},{2,3},{7,4},{4,5},{5,6},{6,7},{11,8},{8,9},{9,10... | collective-permute-start | bytes 294920 | tf_op jit(solution)/shard_map/while/body/eval_jaxpr/ppermute | solution.py:12
  32.9 0.7 fusion.25
  33.6 2.1 %collective-permute-done.1 = f32[32]{0:T(128)S(1)} collective-permute-done((f32[32]{0:T(128)S(1)}, f32[32]{0:T(128)S(1)}, u32[]{:S(2)}, u32[]{:S(2)}) %collective-permute-start.1) | collective-permute-done | bytes 160 | tf_op jit(solution)/shard_map/while/body/eval_jaxpr/ppermute | solution.py:12
  35.8 0.9 collective-permute-done
  36.7 1.5 %collective-permute-done.2 = f32[32,768]{1,0:T(8,128)S(1)} collective-permute-done((f32[32,768]{1,0:T(8,128)S(1)}, f32[32,768]{1,0:T(8,128)S(1)}, u32[]{:S(2)}, u32[]{:S(2)}) %collective-permute-start.2) | collective-permute-done | bytes 98336 | tf_op jit(solution)/shard_map/while/body/eval_jaxpr/ppermute | solution.py:12
  38.2 0.7 collective-permute-start.1
  38.9 2.5 %collective-permute-start = (bf16[32,768]{1,0:T(8,128)(2,1)S(1)}, bf16[32,768]{1,0:T(8,128)(2,1)S(1)}, u32[]{:S(2)}, u32[]{:S(2)}) collective-permute-start(bf16[32,768]{1,0:T(8,128)(2,1)S(1)} %copy.13), channel_id=1, source_target_pairs={{3,0},{0,1},{1,2},{2,3},{7,4},{4,5},{5,6},{6,7},{11,8},{8,9},{9,10... | collective-permute-start | bytes 147464 | tf_op jit(solution)/shard_map/while/body/eval_jaxpr/ppermute | solution.py:12
  41.4 0.3 subtract_multiply_fusion.2
  41.7 0.6 fusion.24
  42.2 0.1 collective-permute-start.2
  42.4 0.7 fusion.25
  43.1 0.5 collective-permute-done.1
  43.6 1.2 %collective-permute-done = bf16[32,768]{1,0:T(8,128)(2,1)S(1)} collective-permute-done((bf16[32,768]{1,0:T(8,128)(2,1)S(1)}, bf16[32,768]{1,0:T(8,128)(2,1)S(1)}, u32[]{:S(2)}, u32[]{:S(2)}) %collective-permute-start) | collective-permute-done | bytes 49184 | tf_op jit(solution)/shard_map/while/body/eval_jaxpr/ppermute | solution.py:12
  44.8 4.4 %collective-permute-done.2 = f32[32,768]{1,0:T(8,128)S(1)} collective-permute-done((f32[32,768]{1,0:T(8,128)S(1)}, f32[32,768]{1,0:T(8,128)S(1)}, u32[]{:S(2)}, u32[]{:S(2)}) %collective-permute-start.2) | collective-permute-done | bytes 98336 | tf_op jit(solution)/shard_map/while/body/eval_jaxpr/ppermute | solution.py:12
  49.3 0.1 collective-permute-start
  49.4 0.3 subtract_multiply_fusion.2
  49.7 0.6 fusion.24
  50.2 0.6 collective-permute-start.2
  50.8 0.7 fusion.25
  51.5 3.0 %collective-permute-done.1 = f32[32]{0:T(128)S(1)} collective-permute-done((f32[32]{0:T(128)S(1)}, f32[32]{0:T(128)S(1)}, u32[]{:S(2)}, u32[]{:S(2)}) %collective-permute-start.1) | collective-permute-done | bytes 160 | tf_op jit(solution)/shard_map/while/body/eval_jaxpr/ppermute | solution.py:12
  54.6 0.6 collective-permute-done
  55.2 1.5 %collective-permute-done.2 = f32[32,768]{1,0:T(8,128)S(1)} collective-permute-done((f32[32,768]{1,0:T(8,128)S(1)}, f32[32,768]{1,0:T(8,128)S(1)}, u32[]{:S(2)}, u32[]{:S(2)}) %collective-permute-start.2) | collective-permute-done | bytes 98336 | tf_op jit(solution)/shard_map/while/body/eval_jaxpr/ppermute | solution.py:12
  56.7 0.9 copy-done
  57.6 0.0 reduce-scatter.2.cloned.1.call-update
  57.6 34.3 %reduce-scatter.2.cloned.1.call-done = f32[32,768]{1,0:T(8,128)} async-done(((f32[256,768]{1,0:T(8,128)}), f32[32,768]{1,0:T(8,128)}) %reduce-scatter.2.cloned.1.call-update) | async-done | bytes 98320 | tf_op jit(solution)/shard_map/reduce_scatter | solution.py:89
  91.9 0.6 copy.28
  (23 shorter events, 0.1 us)
Async XLA Ops:
  7.2 84.7 %reduce-scatter.2.cloned.1.call-start = ((), (), s32[]{:S(2)}) async-start(), calls=%async_computation.1 | async-start | bytes 884736 | tf_op jit(solution)/shard_map/reduce_scatter | solution.py:89
  7.2 0.8 copy-start.2
  19.1 0.8 copy-start.1
  19.1 0.8 copy-start.3
  19.1 0.8 copy-start.4
  19.9 6.4 %collective-permute-start.1 = (f32[32]{0:T(128)S(1)}, f32[32]{0:T(128)S(1)}, u32[]{:S(2)}, u32[]{:S(2)}) collective-permute-start(f32[32]{0:T(128)S(1)} %copy.14), channel_id=1, source_target_pairs={{3,0},{0,1},{1,2},{2,3},{7,4},{4,5},{5,6},{6,7},{11,8},{8,9},{9,10... | collective-permute-start | bytes 392 | tf_op jit(solution)/shard_map/while/body/eval_jaxpr/ppermute | solution.py:12
  21.5 5.9 %collective-permute-start = (bf16[32,768]{1,0:T(8,128)(2,1)S(1)}, bf16[32,768]{1,0:T(8,128)(2,1)S(1)}, u32[]{:S(2)}, u32[]{:S(2)}) collective-permute-start(bf16[32,768]{1,0:T(8,128)(2,1)S(1)} %copy.13), channel_id=1, source_target_pairs={{3,0},{0,1},{1,2},{2,3},{7,4},{4,5},{5,6},{6,7},{11,8},{8,9},{9,10... | collective-permute-start | bytes 147464 | tf_op jit(solution)/shard_map/while/body/eval_jaxpr/ppermute | solution.py:12
  24.0 6.5 %collective-permute-start.2 = (f32[32,768]{1,0:T(8,128)S(1)}, f32[32,768]{1,0:T(8,128)S(1)}, u32[]{:S(2)}, u32[]{:S(2)}) collective-permute-start(f32[32,768]{1,0:T(8,128)S(1)} %fusion.24), channel_id=1, source_target_pairs={{3,0},{0,1},{1,2},{2,3},{7,4},{4,5},{5,6},{6,7},{11,8},{8,9},{9,10... | collective-permute-start | bytes 294920 | tf_op jit(solution)/shard_map/while/body/eval_jaxpr/ppermute | solution.py:12
  30.4 5.3 %collective-permute-start.1 = (f32[32]{0:T(128)S(1)}, f32[32]{0:T(128)S(1)}, u32[]{:S(2)}, u32[]{:S(2)}) collective-permute-start(f32[32]{0:T(128)S(1)} %copy.14), channel_id=1, source_target_pairs={{3,0},{0,1},{1,2},{2,3},{7,4},{4,5},{5,6},{6,7},{11,8},{8,9},{9,10... | collective-permute-start | bytes 392 | tf_op jit(solution)/shard_map/while/body/eval_jaxpr/ppermute | solution.py:12
  30.4 6.3 %collective-permute-start = (bf16[32,768]{1,0:T(8,128)(2,1)S(1)}, bf16[32,768]{1,0:T(8,128)(2,1)S(1)}, u32[]{:S(2)}, u32[]{:S(2)}) collective-permute-start(bf16[32,768]{1,0:T(8,128)(2,1)S(1)} %copy.13), channel_id=1, source_target_pairs={{3,0},{0,1},{1,2},{2,3},{7,4},{4,5},{5,6},{6,7},{11,8},{8,9},{9,10... | collective-permute-start | bytes 147464 | tf_op jit(solution)/shard_map/while/body/eval_jaxpr/ppermute | solution.py:12
  31.7 6.5 %collective-permute-start.2 = (f32[32,768]{1,0:T(8,128)S(1)}, f32[32,768]{1,0:T(8,128)S(1)}, u32[]{:S(2)}, u32[]{:S(2)}) collective-permute-start(f32[32,768]{1,0:T(8,128)S(1)} %fusion.24), channel_id=1, source_target_pairs={{3,0},{0,1},{1,2},{2,3},{7,4},{4,5},{5,6},{6,7},{11,8},{8,9},{9,10... | collective-permute-start | bytes 294920 | tf_op jit(solution)/shard_map/while/body/eval_jaxpr/ppermute | solution.py:12
  38.2 5.3 %collective-permute-start.1 = (f32[32]{0:T(128)S(1)}, f32[32]{0:T(128)S(1)}, u32[]{:S(2)}, u32[]{:S(2)}) collective-permute-start(f32[32]{0:T(128)S(1)} %copy.14), channel_id=1, source_target_pairs={{3,0},{0,1},{1,2},{2,3},{7,4},{4,5},{5,6},{6,7},{11,8},{8,9},{9,10... | collective-permute-start | bytes 392 | tf_op jit(solution)/shard_map/while/body/eval_jaxpr/ppermute | solution.py:12
  38.9 5.9 %collective-permute-start = (bf16[32,768]{1,0:T(8,128)(2,1)S(1)}, bf16[32,768]{1,0:T(8,128)(2,1)S(1)}, u32[]{:S(2)}, u32[]{:S(2)}) collective-permute-start(bf16[32,768]{1,0:T(8,128)(2,1)S(1)} %copy.13), channel_id=1, source_target_pairs={{3,0},{0,1},{1,2},{2,3},{7,4},{4,5},{5,6},{6,7},{11,8},{8,9},{9,10... | collective-permute-start | bytes 147464 | tf_op jit(solution)/shard_map/while/body/eval_jaxpr/ppermute | solution.py:12
  42.2 7.0 %collective-permute-start.2 = (f32[32,768]{1,0:T(8,128)S(1)}, f32[32,768]{1,0:T(8,128)S(1)}, u32[]{:S(2)}, u32[]{:S(2)}) collective-permute-start(f32[32,768]{1,0:T(8,128)S(1)} %fusion.24), channel_id=1, source_target_pairs={{3,0},{0,1},{1,2},{2,3},{7,4},{4,5},{5,6},{6,7},{11,8},{8,9},{9,10... | collective-permute-start | bytes 294920 | tf_op jit(solution)/shard_map/while/body/eval_jaxpr/ppermute | solution.py:12
  49.2 5.3 %collective-permute-start.1 = (f32[32]{0:T(128)S(1)}, f32[32]{0:T(128)S(1)}, u32[]{:S(2)}, u32[]{:S(2)}) collective-permute-start(f32[32]{0:T(128)S(1)} %copy.14), channel_id=1, source_target_pairs={{3,0},{0,1},{1,2},{2,3},{7,4},{4,5},{5,6},{6,7},{11,8},{8,9},{9,10... | collective-permute-start | bytes 392 | tf_op jit(solution)/shard_map/while/body/eval_jaxpr/ppermute | solution.py:12
  49.3 5.9 %collective-permute-start = (bf16[32,768]{1,0:T(8,128)(2,1)S(1)}, bf16[32,768]{1,0:T(8,128)(2,1)S(1)}, u32[]{:S(2)}, u32[]{:S(2)}) collective-permute-start(bf16[32,768]{1,0:T(8,128)(2,1)S(1)} %copy.13), channel_id=1, source_target_pairs={{3,0},{0,1},{1,2},{2,3},{7,4},{4,5},{5,6},{6,7},{11,8},{8,9},{9,10... | collective-permute-start | bytes 147464 | tf_op jit(solution)/shard_map/while/body/eval_jaxpr/ppermute | solution.py:12
  50.2 6.5 %collective-permute-start.2 = (f32[32,768]{1,0:T(8,128)S(1)}, f32[32,768]{1,0:T(8,128)S(1)}, u32[]{:S(2)}, u32[]{:S(2)}) collective-permute-start(f32[32,768]{1,0:T(8,128)S(1)} %fusion.24), channel_id=1, source_target_pairs={{3,0},{0,1},{1,2},{2,3},{7,4},{4,5},{5,6},{6,7},{11,8},{8,9},{9,10... | collective-permute-start | bytes 294920 | tf_op jit(solution)/shard_map/while/body/eval_jaxpr/ppermute | solution.py:12
  56.7 0.9 copy-start
Sparse Core Ops, SparseCore 0:
  57.7 34.1 reduce-scatter.1
where the time goes:
time: 99.6 us; the launch traced here: 99.4 us
  waiting for transfers between devices  54.3 us (55%)
  between operations  14.7 us (15%)
  blocking collectives  11 us (11%)
  starting transfers between devices  10.4 us (10%)
  matrix products  6.13 us (6%)
  local copies, waits for them, and re-layouts  2.44 us (2%)
    reduce_scatter x1, waiting for transfers between devices, local(): lax.psum_scatter(block_total, 'slab', scatter_dimension=0, tiled=True)  34.3 us
    ppermute x12, waiting for transfers between devices, passed_along(): return lax.ppermute(block, axis, route)  20 us
    all_gather x1, blocking collectives, local(): passage_block = lax.all_gather(passages, 'slab', axis=0, tiled=True)  11 us
    ppermute x12, starting transfers between devices, passed_along(): return lax.ppermute(block, axis, route)  10.4 us
    dot_general x4, matrix products, tile_gradients(): lax.dot_general(weights, rows_wide, (((0,), (0,)), ((), ())), precision=l...  2.81 us
    unnamed x11, local copies, waits for them, and re-layouts  2.41 us
    dot_general x4, matrix products, tile_gradients(): jnp.dot(weights, block_wide, precision=lax.Precision.HIGHEST, preferred_e...  2.22 us
  transfers between devices with their start and end apart: 13, of which 12 were waited for; matrix products, arithmetic and copies ran while one was open for 6% of the time, Pallas kernels for 0%

commit v1 on v0

v1 whole, which is shorter than its diff:
```python
import functools
import math

import jax
import jax.numpy as jnp
from jax import lax
from jax.experimental import pallas as pl
from jax.experimental.pallas import tpu as pltpu
from jax.sharding import PartitionSpec as P

AXES = ("slab", "blk")
TAIL = 128


def split_three(values):
    high = values.astype(jnp.bfloat16)
    rest = values - high.astype(jnp.float32)
    middle = rest.astype(jnp.bfloat16)
    low = (rest - middle.astype(jnp.float32)).astype(jnp.bfloat16)
    return high, middle, low


def peer(index, step, count):
    if count & (count - 1) == 0:
        return index ^ step
    return (index + step) % count


class Plan:
    def __init__(self, slab_count, blk_count):
        self.blk_count = blk_count
        self.chip_count = slab_count // 2
        self.group_size = max(self.chip_count, blk_count)

    def device(self, chip, core, blk):
        return (2 * chip + core) * self.blk_count + blk

    def each(self):
        for chip in range(self.chip_count):
            for blk in range(self.blk_count):
                yield chip, blk

    def core_pairs(self):
        return [
            (self.device(chip, core, blk), self.device(chip, 1 - core, blk))
            for chip, blk in self.each()
            for core in (0, 1)
        ]

    def one_way(self, core):
        return [
            (self.device(chip, core, blk), self.device(chip, 1 - core, blk))
            for chip, blk in self.each()
        ]

    def group_pairs(self, step):
        pairs = []
        for chip, blk in self.each():
            if step < self.chip_count:
                other = peer(chip, step, self.chip_count)
                pairs.append((self.device(chip, 0, blk), self.device(other, 0, blk)))
            if step < self.blk_count:
                other = peer(blk, step, self.blk_count)
                pairs.append((self.device(chip, 1, blk), self.device(chip, 1, other)))
        return pairs


def pack_kernel(core_ref, q_ref, p_ref, got_q_ref, got_p_ref, norms_ref, out_ref):
    rows, width = q_ref.shape
    is_query = core_ref[0] == 1
    out_ref[:rows, :width] = jnp.where(is_query, q_ref[...], p_ref[...])
    out_ref[rows:, :width] = jnp.where(is_query, got_q_ref[...], got_p_ref[...])
    high, middle, low = split_three(norms_ref[...])
    lane = lax.broadcasted_iota(jnp.int32, (2 * rows, TAIL), 1)
    spread = functools.partial(jnp.broadcast_to, shape=(2 * rows, TAIL))
    out_ref[:, width:] = jnp.where(
        lane == 0,
        spread(high.astype(jnp.float32)),
        jnp.where(
            lane == 1,
            spread(middle.astype(jnp.float32)),
            jnp.where(lane == 2, spread(low.astype(jnp.float32)), 0.0),
        ),
    ).astype(jnp.bfloat16)


def tile_kernel(count, half_ref, row_ref, column_ref, *refs):
    a_refs, b_refs, out_refs = refs[:count], refs[count : 2 * count], refs[2 * count :]
    rows, wide = a_refs[0].shape
    width = wide - TAIL
    scale = 2.0 / math.sqrt(width)
    a = jnp.concatenate([r[...] for r in a_refs], axis=0)
    b = jnp.concatenate([r[...] for r in b_refs], axis=0)
    contract = (((1,), (1,)), ((), ()))
    scores = scale * lax.dot_general(
        a[:, :width], b[:, :width], contract, preferred_element_type=jnp.float32
    )
    tail = a[:, width:].astype(jnp.float32)
    a_norm = tail[:, 0:1] + tail[:, 1:2] + tail[:, 2:3]
    ones = jnp.ones((16, TAIL), jnp.bfloat16)
    b_norm = lax.dot_general(ones, b[:, width:], contract, preferred_element_type=jnp.float32)[0:1]
    paired = (row_ref[...] == column_ref[...]).astype(jnp.float32)
    weights = half_ref[0] * (
        jnp.exp(scores - a_norm) + jnp.exp(scores - b_norm) - 2.0 * paired
    )
    high = weights.astype(jnp.bfloat16)
    low = (weights - high.astype(jnp.float32)).astype(jnp.bfloat16)
    total = jnp.dot(high, b[:, :width], preferred_element_type=jnp.float32) + jnp.dot(
        low, b[:, :width], preferred_element_type=jnp.float32
    )
    total = scale * total
    for i, out_ref in enumerate(out_refs):
        out_ref[...] = total[i * rows : (i + 1) * rows]


VMEM = pl.BlockSpec(memory_space=pltpu.VMEM)
SMEM = pl.BlockSpec(memory_space=pltpu.SMEM)


def local(plan, queries, passages, query_lognorm, passage_lognorm, loss_cotangent):
    rows, width = queries.shape
    wide = width + TAIL
    count = plan.group_size
    slab = lax.axis_index("slab")
    blk = lax.axis_index("blk")
    chip, core = slab // 2, slab % 2

    got_q = lax.ppermute(queries, AXES, plan.one_way(0))
    got_p = lax.ppermute(passages, AXES, plan.one_way(1))
    got_norm = lax.ppermute(query_lognorm, AXES, plan.one_way(0))
    p_norms = passage_lognorm.reshape(-1, rows)
    own_first = jnp.stack([p_norms[slab], p_norms[slab ^ 1]]).reshape(-1)
    norms = jnp.where(core == 1, jnp.concatenate([query_lognorm, got_norm]), own_first)
    mine = pl.pallas_call(
        pack_kernel,
        out_shape=jax.ShapeDtypeStruct((2 * rows, wide), jnp.bfloat16),
        in_specs=[SMEM] + [VMEM] * 5,
        out_specs=VMEM,
        name="pack",
    )(core.reshape(1), queries, passages, got_q, got_p, norms[:, None])

    a_parts, b_parts = [mine], []
    for step in range(1, count):
        back = [(to, at) for at, to in plan.group_pairs(step)]
        a_parts.append(lax.ppermute(mine, AXES, back))
    b_parts = [lax.ppermute(part, AXES, plan.core_pairs()) for part in a_parts]

    def numbers(role):
        at = lax.broadcasted_iota(jnp.int32, (count, 2, rows), 0)
        of = lax.broadcasted_iota(jnp.int32, (count, 2, rows), 1) ^ role
        within = lax.broadcasted_iota(jnp.int32, (count, 2, rows), 2)
        p_shard = blk * (2 * plan.chip_count) + 2 * peer(chip, at, plan.chip_count) + of
        q_shard = (2 * chip + of) * plan.blk_count + peer(blk, at, plan.blk_count)
        p_number = jnp.where(at < plan.chip_count, p_shard * rows + within, -1)
        q_number = jnp.where(at < plan.blk_count, q_shard * rows + within, -2)
        return jnp.where(role == 0, p_number, q_number).reshape(-1)

    partials = pl.pallas_call(
        functools.partial(tile_kernel, count),
        out_shape=[jax.ShapeDtypeStruct((2 * rows, width), jnp.float32)] * count,
        in_specs=[SMEM] + [VMEM] * (2 * count + 2),
        out_specs=[VMEM] * count,
        name="tile",
        compiler_params=pltpu.CompilerParams(vmem_limit_bytes=48 * 1024 * 1024),
    )(
        (0.5 * loss_cotangent).reshape(1),
        numbers(core)[:, None],
        numbers(1 - core)[None, :],
        *a_parts,
        *b_parts,
    )

    total = partials[0]
    for step in range(1, count):
        total = total + lax.ppermute(partials[step], AXES, plan.group_pairs(step))
    own = total[:rows]
    got = lax.ppermute(total[rows:], AXES, plan.core_pairs())
    return jnp.where(core == 1, own, got), jnp.where(core == 1, got, own)


def solution(mesh):
    plan = Plan(mesh.shape["slab"], mesh.shape["blk"])
    return jax.shard_map(
        functools.partial(local, plan),
        mesh=mesh,
        in_specs=(
            P(("slab", "blk"), None),
            P(("blk", "slab"), None),
            P(("slab", "blk")),
            P("blk"),
            P(),
        ),
        out_specs=(P(("slab", "blk"), None), P(("blk", "slab"), None)),
        check_vma=False,
    )
```

time: 99.6 us -> 36 us (0.36)
  waiting for transfers between devices: 54.3 us -> 8.49 us
  between operations: 14.7 us -> 1.47 us
  blocking collectives: 11 us -> 0 us
  starting transfers between devices: 10.4 us -> 19.1 us
  matrix products: 6.13 us -> 0 us
  Pallas kernels: 0 us -> 2.52 us
  other arithmetic: 0.08 us -> 1.54 us
    reduce_scatter x1 -> x0, waiting for transfers between devices: 34.3 us -> none  [local(): lax.psum_scatter(block_total, 'slab', scatter_dimension=0, tiled=True)]
    ppermute x12 -> x14, waiting for transfers between devices: 20 us -> 8.49 us  [the longest x3 6.09 us: local(): total = total + lax.ppermute(partials[step], AXES, plan.group_pairs(step))]
    all_gather x1 -> x0, blocking collectives: 11 us -> none  [local(): passage_block = lax.all_gather(passages, 'slab', axis=0, tiled=True)]
    ppermute x12 -> x14, starting transfers between devices: 10.4 us -> 19.1 us  [the longest x4 5.53 us: local(): b_parts = [lax.ppermute(part, AXES, plan.core_pairs()) for part in a_parts]]
    dot_general x12 -> x0, matrix products: 6.13 us -> none  [the longest x4 2.81 us: tile_gradients(): lax.dot_general(weights, rows_wide, (((0,), (0,)), ((), ())), precision=l...]
    pallas_call x0 -> x2, Pallas kernels: none -> 2.52 us  [the longest x1 1.59 us: local(): pl.pallas_call(pack_kernel, out_shape=jax.ShapeDtypeStruct((2 * rows, wid...]
    select_n x0 -> x3, other arithmetic: none -> 1.39 us  [the longest x1 0.69 us: local(): return (jnp.where(core == 1, own, got), jnp.where(core == 1, got, own))]
    unnamed x11 -> x10, local copies, waits for them, and re-layouts: 2.41 us -> 1.94 us
  transfers between devices with their start and end apart: 13 -> 14, of which waited for: 12 -> 7; matrix products, arithmetic and copies ran while one was open for 6% -> 4% of each run, Pallas kernels for 0% -> 0%
where the time goes in v1:
time: 36 us; the launch traced here: 35.6 us
  starting transfers between devices  19.1 us (53%)
  waiting for transfers between devices  8.49 us (24%)
  Pallas kernels  2.52 us (7%)
  local copies, waits for them, and re-layouts  2.45 us (7%)
  other arithmetic  1.54 us (4%)
  between operations  1.47 us (4%)
    ppermute x3, waiting for transfers between devices, local(): total = total + lax.ppermute(partials[step], AXES, plan.group_pairs(step))  6.09 us
    ppermute x4, starting transfers between devices, local(): b_parts = [lax.ppermute(part, AXES, plan.core_pairs()) for part in a_parts]  5.53 us
    ppermute x3, starting transfers between devices, local(): a_parts.append(lax.ppermute(mine, AXES, back))  3.84 us
    ppermute x3, starting transfers between devices, local(): total = total + lax.ppermute(partials[step], AXES, plan.group_pairs(step))  3.55 us
    ppermute x1, starting transfers between devices, local(): got_norm = lax.ppermute(query_lognorm, AXES, plan.one_way(0))  2.36 us
    unnamed x10, local copies, waits for them, and re-layouts  1.94 us
    pallas_call x1, Pallas kernels, local(): pl.pallas_call(pack_kernel, out_shape=jax.ShapeDtypeStruct((2 * rows, wid...  1.59 us
    ppermute x1, starting transfers between devices, local(): got_q = lax.ppermute(queries, AXES, plan.one_way(0))  1.29 us
  transfers between devices with their start and end apart: 14, of which 7 were waited for; matrix products, arithmetic and copies ran while one was open for 4% of the time, Pallas kernels for 0%

profile of v1, /device:TPU:0, one launch (start us, length us, event | category | flops | bytes accessed | tf_op | source)
XLA Modules:
  0.0 35.6 jit_solution(15818024690355974487)
XLA Ops:
  0.6 2.4 %collective-permute-start.2 = (f32[32]{0:T(128)}, f32[32]{0:T(128)S(1)}, u32[]{:S(2)}, u32[]{:S(2)}) collective-permute-start(f32[32]{0:T(128)} %param.7), channel_id=1, source_target_pairs={{0,4},{1,5},{2,6},{3,7},{8,12},{9,13},{10,14},{11,15},{16,20},{17,... | collective-permute-start | bytes 392 | tf_op jit(solution)/shard_map/ppermute | solution.py:130
  3.0 1.3 %collective-permute-start = (bf16[32,768]{1,0:T(8,128)(2,1)}, bf16[32,768]{1,0:T(8,128)(2,1)S(1)}, u32[]{:S(2)}, u32[]{:S(2)}) collective-permute-start(bf16[32,768]{1,0:T(8,128)(2,1)} %q_ref.1), channel_id=1, source_target_pairs={{0,4},{1,5},{2,6},{3,7},{8,12},{9,13},{10,14},{11,15},{16,20},{17,... | collective-permute-start | bytes 147464 | tf_op jit(solution)/shard_map/ppermute | solution.py:128
  4.3 1.3 %collective-permute-start.1 = (bf16[32,768]{1,0:T(8,128)(2,1)}, bf16[32,768]{1,0:T(8,128)(2,1)S(1)}, u32[]{:S(2)}, u32[]{:S(2)}) collective-permute-start(bf16[32,768]{1,0:T(8,128)(2,1)} %p_ref.1), channel_id=1, source_target_pairs={{4,0},{5,1},{6,2},{7,3},{12,8},{13,9},{14,10},{15,11},{20,16},{21,... | collective-permute-start | bytes 147464 | tf_op jit(solution)/shard_map/ppermute | solution.py:129
  5.6 0.0 copy-start.3
  5.6 0.7 %copy-done.3 = f32[256]{0:T(256)S(1)} copy-done((f32[256]{0:T(256)S(1)}, f32[256]{0:T(256)}, u32[]{:S(2)}) %copy-start.3) | copy-done | bytes 1048
  6.3 0.1 reshape.283
  6.4 0.1 reshape.298
  6.5 0.0 collective-permute-done.2
  6.5 0.0 copy-start.4
  6.5 0.6 %copy-done.4 = f32[32]{0:T(128)S(1)} copy-done((f32[32]{0:T(128)S(1)}, f32[32]{0:T(128)}, u32[]{:S(2)}) %copy-start.4) | copy-done | bytes 152
  7.2 0.1 pad_maximum_fusion.1
  7.3 0.1 copy.14
  7.4 0.6 %broadcast_select_fusion.norms_ref = f32[64,1]{1,0:T(8,128)} fusion(f32[64,1]{1,0:T(8,128)S(1)} %copy.14, f32[64,1]{1,0:T(8,128)S(1)} %reshape.298, pred[]{:T(512)S(6)} %eq.13), kind=kLoop, calls=%fused_computation.3 | loop fusion | flops 64 | bytes 769 | tf_op jit(solution)/shard_map/jit(_where)/select_n | solution.py:133
  8.0 0.0 collective-permute-done.got_q_ref
  8.0 0.0 collective-permute-done.1.got_p_ref
  8.0 0.0 copy-start.2
  8.0 0.6 %copy-done.1 = bf16[32,768]{1,0:T(8,128)(2,1)} copy-done((bf16[32,768]{1,0:T(8,128)(2,1)}, bf16[32,768]{1,0:T(8,128)(2,1)S(1)}, u32[]{:S(2)}) %copy-start.1) | copy-done | bytes 49176
  8.6 0.0 copy-done.2
  8.6 1.6 %pack.1.refs_0_ = bf16[64,896]{1,0:T(8,128)(2,1)} custom-call(s32[1]{0:T(128)} %bitcast.1.core_ref, bf16[32,768]{1,0:T(8,128)(2,1)} %q_ref.1, bf16[32,768]{1,0:T(8,128)(2,1)} %p_ref.1, bf16[32,768]{1,0:T(8,128)(2,1)} %copy-done.1, bf16[32,768]{1,0:T(8,128)(2,1)} %copy-done.2, f32[64,1]{1,0:T(8,128)} %broadcast_select_fusion.norms_ref), custom_call_target="tpu_custom_call" | custom-call | tf_op jit(solution)/shard_map/pack/pallas_call | solution.py:134
  10.2 3.3 %collective-permute-start.5 = (bf16[64,896]{1,0:T(8,128)(2,1)}, bf16[64,896]{1,0:T(8,128)(2,1)S(1)}, u32[]{:S(2)}, u32[]{:S(2)}) collective-permute-start(bf16[64,896]{1,0:T(8,128)(2,1)} %pack.1.refs_0_), channel_id=1, source_target_pairs={{24,0},{7,4},{25,1},{6,5},{26,2},{5,6},{27,3},{4,7},{16,8},{15,12}... | collective-permute-start | bytes 344072 | tf_op jit(solution)/shard_map/ppermute | solution.py:145
  13.5 0.5 %collective-permute-start.4 = (bf16[64,896]{1,0:T(8,128)(2,1)}, bf16[64,896]{1,0:T(8,128)(2,1)S(1)}, u32[]{:S(2)}, u32[]{:S(2)}) collective-permute-start(bf16[64,896]{1,0:T(8,128)(2,1)} %pack.1.refs_0_), channel_id=1, source_target_pairs={{16,0},{6,4},{17,1},{7,5},{18,2},{4,6},{19,3},{5,7},{24,8},{14,12}... | collective-permute-start | bytes 344072 | tf_op jit(solution)/shard_map/ppermute | solution.py:145
  14.0 0.1 collective-permute-start.3
  14.7 1.8 %collective-permute-start.6 = (bf16[64,896]{1,0:T(8,128)(2,1)}, bf16[64,896]{1,0:T(8,128)(2,1)S(1)}, u32[]{:S(2)}, u32[]{:S(2)}) collective-permute-start(bf16[64,896]{1,0:T(8,128)(2,1)} %pack.1.refs_0_), channel_id=1, source_target_pairs={{0,4},{4,0},{1,5},{5,1},{2,6},{6,2},{3,7},{7,3},{8,12},{12,8},{9,1... | collective-permute-start | bytes 344072 | tf_op jit(solution)/shard_map/ppermute | solution.py:146
  16.5 0.0 collective-permute-done.5.refs_3_
  16.5 1.5 %collective-permute-start.9 = (bf16[64,896]{1,0:T(8,128)(2,1)S(1)}, bf16[64,896]{1,0:T(8,128)(2,1)S(1)}, u32[]{:S(2)}, u32[]{:S(2)}) collective-permute-start(bf16[64,896]{1,0:T(8,128)(2,1)S(1)} %collective-permute-done.5.refs_3_), channel_id=1, source_target_pairs={{0,4},{4,0},{1,5},{5,1},{2,6},{6,2},{3,7},{7,3},{8,12},{12,8},{9,1... | collective-permute-start | bytes 344072 | tf_op jit(solution)/shard_map/ppermute | solution.py:146
  18.1 0.4 %collective-permute-done.4.refs_2_ = bf16[64,896]{1,0:T(8,128)(2,1)S(1)} collective-permute-done((bf16[64,896]{1,0:T(8,128)(2,1)}, bf16[64,896]{1,0:T(8,128)(2,1)S(1)}, u32[]{:S(2)}, u32[]{:S(2)}) %collective-permute-start.4) | collective-permute-done | bytes 114720 | tf_op jit(solution)/shard_map/ppermute | solution.py:145
  18.5 2.2 %collective-permute-start.8 = (bf16[64,896]{1,0:T(8,128)(2,1)S(1)}, bf16[64,896]{1,0:T(8,128)(2,1)S(1)}, u32[]{:S(2)}, u32[]{:S(2)}) collective-permute-start(bf16[64,896]{1,0:T(8,128)(2,1)S(1)} %collective-permute-done.4.refs_2_), channel_id=1, source_target_pairs={{0,4},{4,0},{1,5},{5,1},{2,6},{6,2},{3,7},{7,3},{8,12},{12,8},{9,1... | collective-permute-start | bytes 344072 | tf_op jit(solution)/shard_map/ppermute | solution.py:146
  20.7 0.0 collective-permute-done.3.refs_1_
  20.7 0.0 collective-permute-start.7
  20.7 0.1 select_select_fusion
  20.8 0.1 reshape.296.column_ref
  20.9 0.1 reshape.297.row_ref
  21.1 0.0 collective-permute-done.6.refs_4_
  21.1 0.0 collective-permute-done.9.refs_7_
  21.1 0.6 %collective-permute-done.8.refs_6_ = bf16[64,896]{1,0:T(8,128)(2,1)S(1)} collective-permute-done((bf16[64,896]{1,0:T(8,128)(2,1)S(1)}, bf16[64,896]{1,0:T(8,128)(2,1)S(1)}, u32[]{:S(2)}, u32[]{:S(2)}) %collective-permute-start.8) | collective-permute-done | bytes 114720 | tf_op jit(solution)/shard_map/ppermute | solution.py:146
  21.7 0.4 %collective-permute-done.7.refs_5_ = bf16[64,896]{1,0:T(8,128)(2,1)S(1)} collective-permute-done((bf16[64,896]{1,0:T(8,128)(2,1)S(1)}, bf16[64,896]{1,0:T(8,128)(2,1)S(1)}, u32[]{:S(2)}, u32[]{:S(2)}) %collective-permute-start.7) | collective-permute-done | bytes 114720 | tf_op jit(solution)/shard_map/ppermute | solution.py:146
  22.1 0.0 copy-done
  22.1 0.9 %tile.1 = (f32[64,768]{1,0:T(8,128)S(1)}, f32[64,768]{1,0:T(8,128)S(1)}, f32[64,768]{1,0:T(8,128)S(1)}, f32[64,768]{1,0:T(8,128)S(1)}) custom-call(f32[1]{0:T(128)} %bitcast.half_ref, s32[256,1]{1,0:T(8,128)S(1)} %reshape.297.row_ref, s32[1,256]{1,0:T(1,128)S(1)} %reshape.296.column_ref, bf16[64,896]{1,0:T(8,128)(2,1)S(1)} %copy-done, ...), custom_call_target="tpu_custom_call" | custom-call | tf_op jit(solution)/shard_map/tile/pallas_call | solution.py:158
  23.0 1.6 %collective-permute-start.10 = (f32[64,768]{1,0:T(8,128)S(1)}, f32[64,768]{1,0:T(8,128)S(1)}, u32[]{:S(2)}, u32[]{:S(2)}) collective-permute-start(f32[64,768]{1,0:T(8,128)S(1)} %get-tuple-element.7), channel_id=1, source_target_pairs={{0,8},{4,5},{1,9},{5,4},{2,10},{6,7},{3,11},{7,6},{8,0},{12,13},{9... | collective-permute-start | bytes 589832 | tf_op jit(solution)/shard_map/ppermute | solution.py:175
  24.6 1.5 %collective-permute-start.11 = (f32[64,768]{1,0:T(8,128)S(1)}, f32[64,768]{1,0:T(8,128)S(1)}, u32[]{:S(2)}, u32[]{:S(2)}) collective-permute-start(f32[64,768]{1,0:T(8,128)S(1)} %get-tuple-element.8), channel_id=1, source_target_pairs={{0,16},{4,6},{1,17},{5,7},{2,18},{6,4},{3,19},{7,5},{8,24},{12,14}... | collective-permute-start | bytes 589832 | tf_op jit(solution)/shard_map/ppermute | solution.py:175
  26.1 0.5 %collective-permute-start.12 = (f32[64,768]{1,0:T(8,128)S(1)}, f32[64,768]{1,0:T(8,128)S(1)}, u32[]{:S(2)}, u32[]{:S(2)}) collective-permute-start(f32[64,768]{1,0:T(8,128)S(1)} %get-tuple-element.9), channel_id=1, source_target_pairs={{0,24},{4,7},{1,25},{5,6},{2,26},{6,5},{3,27},{7,4},{8,16},{12,15}... | collective-permute-start | bytes 589832 | tf_op jit(solution)/shard_map/ppermute | solution.py:175
  26.5 2.2 %collective-permute-done.10 = f32[64,768]{1,0:T(8,128)S(1)} collective-permute-done((f32[64,768]{1,0:T(8,128)S(1)}, f32[64,768]{1,0:T(8,128)S(1)}, u32[]{:S(2)}, u32[]{:S(2)}) %collective-permute-start.10) | collective-permute-done | bytes 196640 | tf_op jit(solution)/shard_map/ppermute | solution.py:175
  28.7 2.7 %collective-permute-done.11 = f32[64,768]{1,0:T(8,128)S(1)} collective-permute-done((f32[64,768]{1,0:T(8,128)S(1)}, f32[64,768]{1,0:T(8,128)S(1)}, u32[]{:S(2)}, u32[]{:S(2)}) %collective-permute-start.11) | collective-permute-done | bytes 196640 | tf_op jit(solution)/shard_map/ppermute | solution.py:175
  31.4 1.2 %collective-permute-done.12 = f32[64,768]{1,0:T(8,128)S(1)} collective-permute-done((f32[64,768]{1,0:T(8,128)S(1)}, f32[64,768]{1,0:T(8,128)S(1)}, u32[]{:S(2)}, u32[]{:S(2)}) %collective-permute-start.12) | collective-permute-done | bytes 196640 | tf_op jit(solution)/shard_map/ppermute | solution.py:175
  32.6 0.1 add_add_fusion
  32.7 1.3 %collective-permute-start.13 = (f32[32,768]{1,0:T(8,128)S(1)}, f32[32,768]{1,0:T(8,128)S(1)}, u32[]{:S(2)}, u32[]{:S(2)}) collective-permute-start(f32[32,768]{1,0:T(8,128)S(1)} %slice.9), channel_id=1, source_target_pairs={{0,4},{4,0},{1,5},{5,1},{2,6},{6,2},{3,7},{7,3},{8,12},{12,8},{9,1... | collective-permute-start | bytes 294920 | tf_op jit(solution)/shard_map/ppermute | solution.py:177
  34.0 0.9 %collective-permute-done.13 = f32[32,768]{1,0:T(8,128)S(1)} collective-permute-done((f32[32,768]{1,0:T(8,128)S(1)}, f32[32,768]{1,0:T(8,128)S(1)}, u32[]{:S(2)}, u32[]{:S(2)}) %collective-permute-start.13) | collective-permute-done | bytes 98336 | tf_op jit(solution)/shard_map/ppermute | solution.py:177
  34.9 0.7 %slice_select_fusion = (f32[32,768]{1,0:T(8,128)}, f32[32,768]{1,0:T(8,128)}) fusion(f32[32,768]{1,0:T(8,128)S(1)} %collective-permute-done.13, f32[64,768]{1,0:T(8,128)S(1)} %add_add_fusion, pred[]{:T(512)S(6)} %eq.13), kind=kLoop, calls=%fused_computation.1 | loop fusion | flops 49152 | bytes 393217 | tf_op jit(solution)/shard_map/jit(_where)/select_n | solution.py:178
  (9 shorter events, 0.0 us)
Async XLA Ops:
  0.6 5.9 %collective-permute-start.2 = (f32[32]{0:T(128)}, f32[32]{0:T(128)S(1)}, u32[]{:S(2)}, u32[]{:S(2)}) collective-permute-start(f32[32]{0:T(128)} %param.7), channel_id=1, source_target_pairs={{0,4},{1,5},{2,6},{3,7},{8,12},{9,13},{10,14},{11,15},{16,20},{17,... | collective-permute-start | bytes 392 | tf_op jit(solution)/shard_map/ppermute | solution.py:130
  3.0 5.0 %collective-permute-start = (bf16[32,768]{1,0:T(8,128)(2,1)}, bf16[32,768]{1,0:T(8,128)(2,1)S(1)}, u32[]{:S(2)}, u32[]{:S(2)}) collective-permute-start(bf16[32,768]{1,0:T(8,128)(2,1)} %q_ref.1), channel_id=1, source_target_pairs={{0,4},{1,5},{2,6},{3,7},{8,12},{9,13},{10,14},{11,15},{16,20},{17,... | collective-permute-start | bytes 147464 | tf_op jit(solution)/shard_map/ppermute | solution.py:128
  4.3 3.7 %collective-permute-start.1 = (bf16[32,768]{1,0:T(8,128)(2,1)}, bf16[32,768]{1,0:T(8,128)(2,1)S(1)}, u32[]{:S(2)}, u32[]{:S(2)}) collective-permute-start(bf16[32,768]{1,0:T(8,128)(2,1)} %p_ref.1), channel_id=1, source_target_pairs={{4,0},{5,1},{6,2},{7,3},{12,8},{13,9},{14,10},{15,11},{20,16},{21,... | collective-permute-start | bytes 147464 | tf_op jit(solution)/shard_map/ppermute | solution.py:129
  5.6 0.7 %copy-start.3 = (f32[256]{0:T(256)S(1)}, f32[256]{0:T(256)}, u32[]{:S(2)}) copy-start(f32[256]{0:T(256)} %param.8) | copy-start | bytes 3076
  6.5 0.7 %copy-start.4 = (f32[32]{0:T(128)S(1)}, f32[32]{0:T(128)}, u32[]{:S(2)}) copy-start(f32[32]{0:T(128)} %param.7) | copy-start | bytes 388
  8.0 0.6 %copy-start.1 = (bf16[32,768]{1,0:T(8,128)(2,1)}, bf16[32,768]{1,0:T(8,128)(2,1)S(1)}, u32[]{:S(2)}) copy-start(bf16[32,768]{1,0:T(8,128)(2,1)S(1)} %collective-permute-done.got_q_ref) | copy-start | bytes 147460
  8.0 0.6 %copy-start.2 = (bf16[32,768]{1,0:T(8,128)(2,1)}, bf16[32,768]{1,0:T(8,128)(2,1)S(1)}, u32[]{:S(2)}) copy-start(bf16[32,768]{1,0:T(8,128)(2,1)S(1)} %collective-permute-done.1.got_p_ref) | copy-start | bytes 147460
  10.2 11.8 %copy-start = (bf16[64,896]{1,0:T(8,128)(2,1)S(1)}, bf16[64,896]{1,0:T(8,128)(2,1)}, u32[]{:S(2)}) copy-start(bf16[64,896]{1,0:T(8,128)(2,1)} %pack.1.refs_0_) | copy-start | bytes 344068
  10.2 6.3 %collective-permute-start.5 = (bf16[64,896]{1,0:T(8,128)(2,1)}, bf16[64,896]{1,0:T(8,128)(2,1)S(1)}, u32[]{:S(2)}, u32[]{:S(2)}) collective-permute-start(bf16[64,896]{1,0:T(8,128)(2,1)} %pack.1.refs_0_), channel_id=1, source_target_pairs={{24,0},{7,4},{25,1},{6,5},{26,2},{5,6},{27,3},{4,7},{16,8},{15,12}... | collective-permute-start | bytes 344072 | tf_op jit(solution)/shard_map/ppermute | solution.py:145
  13.5 5.0 %collective-permute-start.4 = (bf16[64,896]{1,0:T(8,128)(2,1)}, bf16[64,896]{1,0:T(8,128)(2,1)S(1)}, u32[]{:S(2)}, u32[]{:S(2)}) collective-permute-start(bf16[64,896]{1,0:T(8,128)(2,1)} %pack.1.refs_0_), channel_id=1, source_target_pairs={{16,0},{6,4},{17,1},{7,5},{18,2},{4,6},{19,3},{5,7},{24,8},{14,12}... | collective-permute-start | bytes 344072 | tf_op jit(solution)/shard_map/ppermute | solution.py:145
  14.0 6.7 %collective-permute-start.3 = (bf16[64,896]{1,0:T(8,128)(2,1)}, bf16[64,896]{1,0:T(8,128)(2,1)S(1)}, u32[]{:S(2)}, u32[]{:S(2)}) collective-permute-start(bf16[64,896]{1,0:T(8,128)(2,1)} %pack.1.refs_0_), channel_id=1, source_target_pairs={{8,0},{5,4},{9,1},{4,5},{10,2},{7,6},{11,3},{6,7},{0,8},{13,12},{1... | collective-permute-start | bytes 344072 | tf_op jit(solution)/shard_map/ppermute | solution.py:145
  14.7 6.3 %collective-permute-start.6 = (bf16[64,896]{1,0:T(8,128)(2,1)}, bf16[64,896]{1,0:T(8,128)(2,1)S(1)}, u32[]{:S(2)}, u32[]{:S(2)}) collective-permute-start(bf16[64,896]{1,0:T(8,128)(2,1)} %pack.1.refs_0_), channel_id=1, source_target_pairs={{0,4},{4,0},{1,5},{5,1},{2,6},{6,2},{3,7},{7,3},{8,12},{12,8},{9,1... | collective-permute-start | bytes 344072 | tf_op jit(solution)/shard_map/ppermute | solution.py:146
  16.5 4.5 %collective-permute-start.9 = (bf16[64,896]{1,0:T(8,128)(2,1)S(1)}, bf16[64,896]{1,0:T(8,128)(2,1)S(1)}, u32[]{:S(2)}, u32[]{:S(2)}) collective-permute-start(bf16[64,896]{1,0:T(8,128)(2,1)S(1)} %collective-permute-done.5.refs_3_), channel_id=1, source_target_pairs={{0,4},{4,0},{1,5},{5,1},{2,6},{6,2},{3,7},{7,3},{8,12},{12,8},{9,1... | collective-permute-start | bytes 344072 | tf_op jit(solution)/shard_map/ppermute | solution.py:146
  18.5 3.2 %collective-permute-start.8 = (bf16[64,896]{1,0:T(8,128)(2,1)S(1)}, bf16[64,896]{1,0:T(8,128)(2,1)S(1)}, u32[]{:S(2)}, u32[]{:S(2)}) collective-permute-start(bf16[64,896]{1,0:T(8,128)(2,1)S(1)} %collective-permute-done.4.refs_2_), channel_id=1, source_target_pairs={{0,4},{4,0},{1,5},{5,1},{2,6},{6,2},{3,7},{7,3},{8,12},{12,8},{9,1... | collective-permute-start | bytes 344072 | tf_op jit(solution)/shard_map/ppermute | solution.py:146
  20.7 1.3 %collective-permute-start.7 = (bf16[64,896]{1,0:T(8,128)(2,1)S(1)}, bf16[64,896]{1,0:T(8,128)(2,1)S(1)}, u32[]{:S(2)}, u32[]{:S(2)}) collective-permute-start(bf16[64,896]{1,0:T(8,128)(2,1)S(1)} %collective-permute-done.3.refs_1_), channel_id=1, source_target_pairs={{0,4},{4,0},{1,5},{5,1},{2,6},{6,2},{3,7},{7,3},{8,12},{12,8},{9,1... | collective-permute-start | bytes 344072 | tf_op jit(solution)/shard_map/ppermute | solution.py:146
  23.0 5.7 %collective-permute-start.10 = (f32[64,768]{1,0:T(8,128)S(1)}, f32[64,768]{1,0:T(8,128)S(1)}, u32[]{:S(2)}, u32[]{:S(2)}) collective-permute-start(f32[64,768]{1,0:T(8,128)S(1)} %get-tuple-element.7), channel_id=1, source_target_pairs={{0,8},{4,5},{1,9},{5,4},{2,10},{6,7},{3,11},{7,6},{8,0},{12,13},{9... | collective-permute-start | bytes 589832 | tf_op jit(solution)/shard_map/ppermute | solution.py:175
  24.6 6.8 %collective-permute-start.11 = (f32[64,768]{1,0:T(8,128)S(1)}, f32[64,768]{1,0:T(8,128)S(1)}, u32[]{:S(2)}, u32[]{:S(2)}) collective-permute-start(f32[64,768]{1,0:T(8,128)S(1)} %get-tuple-element.8), channel_id=1, source_target_pairs={{0,16},{4,6},{1,17},{5,7},{2,18},{6,4},{3,19},{7,5},{8,24},{12,14}... | collective-permute-start | bytes 589832 | tf_op jit(solution)/shard_map/ppermute | solution.py:175
  26.1 6.6 %collective-permute-start.12 = (f32[64,768]{1,0:T(8,128)S(1)}, f32[64,768]{1,0:T(8,128)S(1)}, u32[]{:S(2)}, u32[]{:S(2)}) collective-permute-start(f32[64,768]{1,0:T(8,128)S(1)} %get-tuple-element.9), channel_id=1, source_target_pairs={{0,24},{4,7},{1,25},{5,6},{2,26},{6,5},{3,27},{7,4},{8,16},{12,15}... | collective-permute-start | bytes 589832 | tf_op jit(solution)/shard_map/ppermute | solution.py:175
  32.7 2.2 %collective-permute-start.13 = (f32[32,768]{1,0:T(8,128)S(1)}, f32[32,768]{1,0:T(8,128)S(1)}, u32[]{:S(2)}, u32[]{:S(2)}) collective-permute-start(f32[32,768]{1,0:T(8,128)S(1)} %slice.9), channel_id=1, source_target_pairs={{0,4},{4,0},{1,5},{5,1},{2,6},{6,2},{3,7},{7,3},{8,12},{12,8},{9,1... | collective-permute-start | bytes 294920 | tf_op jit(solution)/shard_map/ppermute | solution.py:177

commit v2 on v1

v2 whole, which is shorter than its diff:
```python
import functools
import math

import jax
import jax.numpy as jnp
from jax import lax
from jax.experimental import pallas as pl
from jax.experimental.pallas import tpu as pltpu
from jax.sharding import PartitionSpec as P

AXES = ("slab", "blk")
TAIL = 128


def split_three(values):
    high = values.astype(jnp.bfloat16)
    rest = values - high.astype(jnp.float32)
    middle = rest.astype(jnp.bfloat16)
    low = (rest - middle.astype(jnp.float32)).astype(jnp.bfloat16)
    return high, middle, low


def peer(index, step, count):
    if count & (count - 1) == 0:
        return index ^ step
    return (index + step) % count


class Plan:
    def __init__(self, slab_count, blk_count):
        self.blk_count = blk_count
        self.chip_count = slab_count // 2
        self.group_size = max(self.chip_count, blk_count)

    def device(self, chip, core, blk):
        return (2 * chip + core) * self.blk_count + blk

    def each(self):
        for chip in range(self.chip_count):
            for blk in range(self.blk_count):
                yield chip, blk

    def core_pairs(self):
        return [
            (self.device(chip, core, blk), self.device(chip, 1 - core, blk))
            for chip, blk in self.each()
            for core in (0, 1)
        ]

    def group_pairs(self, step):
        pairs = []
        for chip, blk in self.each():
            if step < self.chip_count:
                other = peer(chip, step, self.chip_count)
                pairs.append((self.device(chip, 0, blk), self.device(other, 0, blk)))
            if step < self.blk_count:
                other = peer(blk, step, self.blk_count)
                pairs.append((self.device(chip, 1, blk), self.device(chip, 1, other)))
        return pairs


def column(values, first, rows):
    shape = (rows, values.shape[1])
    lane = lax.broadcasted_iota(jnp.int32, shape, 1)
    row = lax.broadcasted_iota(jnp.int32, shape, 0)
    picked = jnp.where(lane == row + first, jnp.broadcast_to(values, shape), 0.0)
    return jnp.sum(picked, axis=1, keepdims=True)


def with_tail(out_ref, start, block, norms):
    rows, width = block.shape
    high, middle, low = (
        jnp.broadcast_to(part.astype(jnp.float32), (rows, TAIL)) for part in split_three(norms)
    )
    lane = lax.broadcasted_iota(jnp.int32, (rows, TAIL), 1)
    tail = jnp.where(lane == 0, high, jnp.where(lane == 1, middle, low))
    out_ref[start : start + rows, :width] = block
    out_ref[start : start + rows, width:] = jnp.where(lane < 3, tail, 0.0).astype(jnp.bfloat16)


def pack_kernel(
    slab_ref, q_ref, p_ref, got_q_ref, got_p_ref, norm_ref, got_norm_ref, p_norm_ref, a_ref, b_ref
):
    rows = q_ref.shape[0]
    slab = slab_ref[0]
    is_query = (slab & 1) == 1
    own_q = column(norm_ref[...], 0, rows)
    got_q = column(got_norm_ref[...], 0, rows)
    own_p = column(p_norm_ref[...], slab * rows, rows)
    got_p = column(p_norm_ref[...], (slab ^ 1) * rows, rows)
    pick = functools.partial(jnp.where, is_query)
    with_tail(a_ref, 0, pick(q_ref[...], p_ref[...]), pick(own_q, own_p))
    with_tail(a_ref, rows, pick(got_q_ref[...], got_p_ref[...]), pick(got_q, got_p))
    with_tail(b_ref, 0, pick(got_p_ref[...], got_q_ref[...]), pick(got_p, got_q))
    with_tail(b_ref, rows, pick(p_ref[...], q_ref[...]), pick(own_p, own_q))


def row_numbers(plan, slab, blk, role, rows, place):
    chip = slab >> 1
    number = place
    for step in range(plan.group_size):
        for other in (0, 1):
            core = role ^ other
            p_shard = blk * (2 * plan.chip_count) + 2 * peer(chip, step, plan.chip_count) + core
            q_shard = (2 * chip + core) * plan.blk_count + peer(blk, step, plan.blk_count)
            p_base = p_shard * rows if step < plan.chip_count else -(1 << 24)
            q_base = q_shard * rows if step < plan.blk_count else -(1 << 25)
            start = (2 * step + other) * rows
            base = jnp.where(role == 0, p_base, q_base) - start
            number = jnp.where(place >= start, place + base, number)
    return number


def tile_kernel(plan, slab_ref, blk_ref, loss_ref, *refs):
    count = plan.group_size
    a_refs, b_refs, out_refs = refs[:count], refs[count : 2 * count], refs[2 * count :]
    rows, wide = a_refs[0].shape
    width = wide - TAIL
    scale = 2.0 / math.sqrt(width)
    a = jnp.concatenate([r[...] for r in a_refs], axis=0)
    b = jnp.concatenate([r[...] for r in b_refs], axis=0)
    contract = (((1,), (1,)), ((), ()))
    scores = scale * lax.dot_general(
        a[:, :width], b[:, :width], contract, preferred_element_type=jnp.float32
    )
    tail = a[:, width:].astype(jnp.float32)
    a_norm = tail[:, 0:1] + tail[:, 1:2] + tail[:, 2:3]
    ones = jnp.ones((16, TAIL), jnp.bfloat16)
    b_norm = lax.dot_general(ones, b[:, width:], contract, preferred_element_type=jnp.float32)[0:1]
    slab, blk = slab_ref[0], blk_ref[0]
    role = slab & 1
    numbers = functools.partial(row_numbers, plan, slab, blk, rows=rows // 2)
    a_number = numbers(role, place=lax.broadcasted_iota(jnp.int32, (count * rows, 1), 0))
    b_number = numbers(1 - role, place=lax.broadcasted_iota(jnp.int32, (1, count * rows), 1))
    paired = (a_number == b_number).astype(jnp.float32)
    weights = (0.5 * loss_ref[0]) * (
        jnp.exp(scores - a_norm) + jnp.exp(scores - b_norm) - 2.0 * paired
    )
    high = weights.astype(jnp.bfloat16)
    low = (weights - high.astype(jnp.float32)).astype(jnp.bfloat16)
    total = jnp.dot(high, b[:, :width], preferred_element_type=jnp.float32) + jnp.dot(
        low, b[:, :width], preferred_element_type=jnp.float32
    )
    total = scale * total
    for i, out_ref in enumerate(out_refs):
        out_ref[...] = total[i * rows : (i + 1) * rows]


VMEM = pl.BlockSpec(memory_space=pltpu.VMEM)
SMEM = pl.BlockSpec(memory_space=pltpu.SMEM)


def local(plan, queries, passages, query_lognorm, passage_lognorm, loss_cotangent):
    rows, width = queries.shape
    wide = width + TAIL
    count = plan.group_size
    slab = lax.axis_index("slab")
    blk = lax.axis_index("blk")
    core = slab & 1

    def swapped(block):
        return lax.ppermute(block, AXES, plan.core_pairs())

    packed = jax.ShapeDtypeStruct((2 * rows, wide), jnp.bfloat16)
    mine, others = pl.pallas_call(
        pack_kernel,
        out_shape=[packed, packed],
        in_specs=[SMEM] + [VMEM] * 7,
        out_specs=[VMEM, VMEM],
        name="pack",
        compiler_params=pltpu.CompilerParams(vmem_limit_bytes=4 * 1024 * 1024),
    )(
        slab.reshape(1),
        queries,
        passages,
        swapped(queries),
        swapped(passages),
        query_lognorm.reshape(1, -1),
        swapped(query_lognorm).reshape(1, -1),
        passage_lognorm.reshape(1, -1),
    )

    a_parts, b_parts = [mine], [others]
    for step in range(1, count):
        back = [(to, at) for at, to in plan.group_pairs(step)]
        a_parts.append(lax.ppermute(mine, AXES, back))
        b_parts.append(swapped(a_parts[-1]))

    partials = pl.pallas_call(
        functools.partial(tile_kernel, plan),
        out_shape=[jax.ShapeDtypeStruct((2 * rows, width), jnp.float32)] * count,
        in_specs=[SMEM] * 3 + [VMEM] * (2 * count),
        out_specs=[VMEM] * count,
        name="tile",
        compiler_params=pltpu.CompilerParams(vmem_limit_bytes=3 * count * 1024 * 1024),
    )(slab.reshape(1), blk.reshape(1), loss_cotangent.reshape(1), *a_parts, *b_parts)

    total = partials[0]
    for step in range(1, count):
        total = total + lax.ppermute(partials[step], AXES, plan.group_pairs(step))
    own = total[:rows]
    got = swapped(total[rows:])
    return jnp.where(core == 1, own, got), jnp.where(core == 1, got, own)


def solution(mesh):
    plan = Plan(mesh.shape["slab"], mesh.shape["blk"])
    return jax.shard_map(
        functools.partial(local, plan),
        mesh=mesh,
        in_specs=(
            P(("slab", "blk"), None),
            P(("blk", "slab"), None),
            P(("slab", "blk")),
            P("blk"),
            P(),
        ),
        out_specs=(P(("slab", "blk"), None), P(("blk", "slab"), None)),
        check_vma=False,
    )
```

time: 36 us -> 31.1 us (0.86)
  starting transfers between devices: 19.1 us -> 12.8 us
  waiting for transfers between devices: 8.49 us -> 12.7 us
  Pallas kernels: 2.52 us -> 1.04 us
  other arithmetic: 1.54 us -> 0.73 us
    ppermute x8 -> x7, starting transfers between devices: 11.7 us -> 4.84 us  [swapped(): return lax.ppermute(block, AXES, plan.core_pairs())]
    ppermute x3, waiting for transfers between devices: 0.46 us -> 4.67 us  [local(): a_parts.append(lax.ppermute(mine, AXES, back))]
    pallas_call x2, Pallas kernels: 2.52 us -> 1.04 us  [the longest x1 0.92 us: local(): pl.pallas_call(functools.partial(tile_kernel, plan), out_shape=[jax.Shape...]
    select_n x2 -> x0, other arithmetic: 0.7 us -> none  [the longest x1 0.62 us: local(): jnp.where(core == 1, jnp.concatenate([query_lognorm, got_norm]), own_first)]
    ppermute x3, starting transfers between devices: 3.84 us -> 4.39 us  [local(): a_parts.append(lax.ppermute(mine, AXES, back))]
    unnamed x10 -> x8, local copies, waits for them, and re-layouts: 1.94 us -> 2.27 us
    ppermute x8 -> x7, waiting for transfers between devices: 1.93 us -> 2.2 us  [swapped(): return lax.ppermute(block, AXES, plan.core_pairs())]
  transfers between devices with their start and end apart: 14 -> 13, of which waited for: 7 -> 9; matrix products, arithmetic and copies ran while one was open for 4% -> 0% of each run, Pallas kernels for 0% -> 0%
where the time goes in v2:
time: 31.1 us; the launch traced here: 30.8 us
  starting transfers between devices  12.8 us (41%)
  waiting for transfers between devices  12.7 us (41%)
  local copies, waits for them, and re-layouts  2.28 us (7%)
  between operations  1.34 us (4%)
  Pallas kernels  1.04 us (3%)
  other arithmetic  0.73 us (2%)
    ppermute x3, waiting for transfers between devices, local(): total = total + lax.ppermute(partials[step], AXES, plan.group_pairs(step))  5.8 us
    ppermute x7, starting transfers between devices, swapped(): return lax.ppermute(block, AXES, plan.core_pairs())  4.84 us
    ppermute x3, waiting for transfers between devices, local(): a_parts.append(lax.ppermute(mine, AXES, back))  4.67 us
    ppermute x3, starting transfers between devices, local(): a_parts.append(lax.ppermute(mine, AXES, back))  4.39 us
    ppermute x3, starting transfers between devices, local(): total = total + lax.ppermute(partials[step], AXES, plan.group_pairs(step))  3.55 us
    unnamed x8, local copies, waits for them, and re-layouts  2.27 us
    ppermute x7, waiting for transfers between devices, swapped(): return lax.ppermute(block, AXES, plan.core_pairs())  2.2 us
    pallas_call x1, Pallas kernels, local(): pl.pallas_call(functools.partial(tile_kernel, plan), out_shape=[jax.Shape...  0.92 us
  transfers between devices with their start and end apart: 13, of which 9 were waited for; matrix products, arithmetic and copies ran while one was open for 0% of the time, Pallas kernels for 0%

profile of v2, /device:TPU:0, one launch (start us, length us, event | category | flops | bytes accessed | tf_op | source)
XLA Modules:
  0.0 30.8 jit_solution(12240523970816237861)
XLA Ops:
  0.6 0.5 %collective-permute-start = (bf16[32,768]{1,0:T(8,128)(2,1)}, bf16[32,768]{1,0:T(8,128)(2,1)S(1)}, u32[]{:S(2)}, u32[]{:S(2)}) collective-permute-start(bf16[32,768]{1,0:T(8,128)(2,1)} %q_ref.1), channel_id=1, source_target_pairs={{0,4},{4,0},{1,5},{5,1},{2,6},{6,2},{3,7},{7,3},{8,12},{12,8},{9,1... | collective-permute-start | bytes 147464 | tf_op jit(solution)/shard_map/ppermute | solution.py:162
  1.1 0.1 collective-permute-start.1
  1.2 0.4 %collective-permute-start.2 = (f32[32]{0:T(128)}, f32[32]{0:T(128)S(1)}, u32[]{:S(2)}, u32[]{:S(2)}) collective-permute-start(f32[32]{0:T(128)} %param.7), channel_id=1, source_target_pairs={{0,4},{4,0},{1,5},{5,1},{2,6},{6,2},{3,7},{7,3},{8,12},{12,8},{9,1... | collective-permute-start | bytes 392 | tf_op jit(solution)/shard_map/ppermute | solution.py:162
  1.7 1.0 %collective-permute-done.2 = f32[32]{0:T(128)S(1)} collective-permute-done((f32[32]{0:T(128)}, f32[32]{0:T(128)S(1)}, u32[]{:S(2)}, u32[]{:S(2)}) %collective-permute-start.2) | collective-permute-done | bytes 160 | tf_op jit(solution)/shard_map/ppermute | solution.py:162
  2.6 0.0 collective-permute-done.got_q_ref
  2.6 0.0 collective-permute-done.1.got_p_ref
  2.6 0.0 copy-start.2
  2.6 0.0 copy-start.3
  2.6 0.7 %copy-done.2 = f32[256]{0:T(256)S(1)} copy-done((f32[256]{0:T(256)S(1)}, f32[256]{0:T(256)}, u32[]{:S(2)}) %copy-start.2) | copy-done | bytes 1048
  3.3 0.0 copy-done.3
  3.3 0.0 copy-start
  3.3 0.8 %copy-done = bf16[32,768]{1,0:T(8,128)(2,1)S(1)} copy-done((bf16[32,768]{1,0:T(8,128)(2,1)S(1)}, bf16[32,768]{1,0:T(8,128)(2,1)}, u32[]{:S(2)}) %copy-start) | copy-done | bytes 49176
  4.1 0.0 copy-start.1
  4.1 0.8 %copy-done.1 = bf16[32,768]{1,0:T(8,128)(2,1)S(1)} copy-done((bf16[32,768]{1,0:T(8,128)(2,1)S(1)}, bf16[32,768]{1,0:T(8,128)(2,1)}, u32[]{:S(2)}) %copy-start.1) | copy-done | bytes 49176
  4.9 0.1 pack.1
  5.0 2.9 %collective-permute-start.3 = (bf16[64,896]{1,0:T(8,128)(2,1)S(1)}, bf16[64,896]{1,0:T(8,128)(2,1)S(1)}, u32[]{:S(2)}, u32[]{:S(2)}) collective-permute-start(bf16[64,896]{1,0:T(8,128)(2,1)S(1)} %get-tuple-element.8.refs_0_), channel_id=1, source_target_pairs={{8,0},{5,4},{9,1},{4,5},{10,2},{7,6},{11,3},{6,7},{0,8},{13,12},{1... | collective-permute-start | bytes 344072 | tf_op jit(solution)/shard_map/ppermute | solution.py:186
  7.9 1.5 %collective-permute-start.4 = (bf16[64,896]{1,0:T(8,128)(2,1)S(1)}, bf16[64,896]{1,0:T(8,128)(2,1)S(1)}, u32[]{:S(2)}, u32[]{:S(2)}) collective-permute-start(bf16[64,896]{1,0:T(8,128)(2,1)S(1)} %get-tuple-element.8.refs_0_), channel_id=1, source_target_pairs={{16,0},{6,4},{17,1},{7,5},{18,2},{4,6},{19,3},{5,7},{24,8},{14,12}... | collective-permute-start | bytes 344072 | tf_op jit(solution)/shard_map/ppermute | solution.py:186
  9.4 0.0 collective-permute-start.5
  9.4 1.2 %collective-permute-done.3.refs_1_ = bf16[64,896]{1,0:T(8,128)(2,1)S(1)} collective-permute-done((bf16[64,896]{1,0:T(8,128)(2,1)S(1)}, bf16[64,896]{1,0:T(8,128)(2,1)S(1)}, u32[]{:S(2)}, u32[]{:S(2)}) %collective-permute-start.3) | collective-permute-done | bytes 114720 | tf_op jit(solution)/shard_map/ppermute | solution.py:186
  10.6 0.0 collective-permute-start.6
  10.6 2.0 %collective-permute-done.4.refs_2_ = bf16[64,896]{1,0:T(8,128)(2,1)S(1)} collective-permute-done((bf16[64,896]{1,0:T(8,128)(2,1)S(1)}, bf16[64,896]{1,0:T(8,128)(2,1)S(1)}, u32[]{:S(2)}, u32[]{:S(2)}) %collective-permute-start.4) | collective-permute-done | bytes 114720 | tf_op jit(solution)/shard_map/ppermute | solution.py:186
  12.7 1.0 %collective-permute-start.7 = (bf16[64,896]{1,0:T(8,128)(2,1)S(1)}, bf16[64,896]{1,0:T(8,128)(2,1)S(1)}, u32[]{:S(2)}, u32[]{:S(2)}) collective-permute-start(bf16[64,896]{1,0:T(8,128)(2,1)S(1)} %collective-permute-done.4.refs_2_), channel_id=1, source_target_pairs={{0,4},{4,0},{1,5},{5,1},{2,6},{6,2},{3,7},{7,3},{8,12},{12,8},{9,1... | collective-permute-start | bytes 344072 | tf_op jit(solution)/shard_map/ppermute | solution.py:162
  13.7 1.4 %collective-permute-done.5.refs_3_ = bf16[64,896]{1,0:T(8,128)(2,1)S(1)} collective-permute-done((bf16[64,896]{1,0:T(8,128)(2,1)S(1)}, bf16[64,896]{1,0:T(8,128)(2,1)S(1)}, u32[]{:S(2)}, u32[]{:S(2)}) %collective-permute-start.5) | collective-permute-done | bytes 114720 | tf_op jit(solution)/shard_map/ppermute | solution.py:186
  15.1 0.7 %collective-permute-start.8 = (bf16[64,896]{1,0:T(8,128)(2,1)S(1)}, bf16[64,896]{1,0:T(8,128)(2,1)S(1)}, u32[]{:S(2)}, u32[]{:S(2)}) collective-permute-start(bf16[64,896]{1,0:T(8,128)(2,1)S(1)} %collective-permute-done.5.refs_3_), channel_id=1, source_target_pairs={{0,4},{4,0},{1,5},{5,1},{2,6},{6,2},{3,7},{7,3},{8,12},{12,8},{9,1... | collective-permute-start | bytes 344072 | tf_op jit(solution)/shard_map/ppermute | solution.py:162
  16.4 0.0 collective-permute-done.6.refs_5_
  16.4 0.0 collective-permute-done.7.refs_6_
  16.4 0.3 collective-permute-done.8.refs_7_
  16.7 0.9 %tile.1 = (f32[64,768]{1,0:T(8,128)S(1)}, f32[64,768]{1,0:T(8,128)S(1)}, f32[64,768]{1,0:T(8,128)S(1)}, f32[64,768]{1,0:T(8,128)S(1)}) custom-call(s32[1]{0:T(128)} %bitcast.slab_ref, s32[1]{0:T(128)} %bitcast.1.blk_ref, f32[1]{0:T(128)} %bitcast.6.loss_ref, bf16[64,896]{1,0:T(8,128)(2,1)S(1)} %get-tuple-element.8.refs_0_, ...), custom_call_target="tpu_custom_call" | custom-call | tf_op jit(solution)/shard_map/tile/pallas_call | solution.py:189
  17.6 1.6 %collective-permute-start.10 = (f32[64,768]{1,0:T(8,128)S(1)}, f32[64,768]{1,0:T(8,128)S(1)}, u32[]{:S(2)}, u32[]{:S(2)}) collective-permute-start(f32[64,768]{1,0:T(8,128)S(1)} %get-tuple-element.12), channel_id=1, source_target_pairs={{0,16},{4,6},{1,17},{5,7},{2,18},{6,4},{3,19},{7,5},{8,24},{12,14}... | collective-permute-start | bytes 589832 | tf_op jit(solution)/shard_map/ppermute | solution.py:200
  19.2 1.4 %collective-permute-start.11 = (f32[64,768]{1,0:T(8,128)S(1)}, f32[64,768]{1,0:T(8,128)S(1)}, u32[]{:S(2)}, u32[]{:S(2)}) collective-permute-start(f32[64,768]{1,0:T(8,128)S(1)} %get-tuple-element.13), channel_id=1, source_target_pairs={{0,24},{4,7},{1,25},{5,6},{2,26},{6,5},{3,27},{7,4},{8,16},{12,15}... | collective-permute-start | bytes 589832 | tf_op jit(solution)/shard_map/ppermute | solution.py:200
  20.7 0.5 %collective-permute-start.9 = (f32[64,768]{1,0:T(8,128)S(1)}, f32[64,768]{1,0:T(8,128)S(1)}, u32[]{:S(2)}, u32[]{:S(2)}) collective-permute-start(f32[64,768]{1,0:T(8,128)S(1)} %get-tuple-element.11), channel_id=1, source_target_pairs={{0,8},{4,5},{1,9},{5,4},{2,10},{6,7},{3,11},{7,6},{8,0},{12,13},{9... | collective-permute-start | bytes 589832 | tf_op jit(solution)/shard_map/ppermute | solution.py:200
  21.2 3.4 %collective-permute-done.10 = f32[64,768]{1,0:T(8,128)S(1)} collective-permute-done((f32[64,768]{1,0:T(8,128)S(1)}, f32[64,768]{1,0:T(8,128)S(1)}, u32[]{:S(2)}, u32[]{:S(2)}) %collective-permute-start.10) | collective-permute-done | bytes 196640 | tf_op jit(solution)/shard_map/ppermute | solution.py:200
  24.6 1.2 %collective-permute-done.11 = f32[64,768]{1,0:T(8,128)S(1)} collective-permute-done((f32[64,768]{1,0:T(8,128)S(1)}, f32[64,768]{1,0:T(8,128)S(1)}, u32[]{:S(2)}, u32[]{:S(2)}) %collective-permute-start.11) | collective-permute-done | bytes 196640 | tf_op jit(solution)/shard_map/ppermute | solution.py:200
  25.8 1.2 %collective-permute-done.9 = f32[64,768]{1,0:T(8,128)S(1)} collective-permute-done((f32[64,768]{1,0:T(8,128)S(1)}, f32[64,768]{1,0:T(8,128)S(1)}, u32[]{:S(2)}, u32[]{:S(2)}) %collective-permute-start.9) | collective-permute-done | bytes 196640 | tf_op jit(solution)/shard_map/ppermute | solution.py:200
  27.1 2.2 %collective-permute-start.12 = (f32[32,768]{1,0:T(8,128)S(1)}, f32[32,768]{1,0:T(8,128)S(1)}, u32[]{:S(2)}, u32[]{:S(2)}) collective-permute-start(f32[32,768]{1,0:T(8,128)S(1)} %slice.9), channel_id=1, source_target_pairs={{0,4},{4,0},{1,5},{5,1},{2,6},{6,2},{3,7},{7,3},{8,12},{12,8},{9,1... | collective-permute-start | bytes 294920 | tf_op jit(solution)/shard_map/ppermute | solution.py:162
  29.2 0.9 %collective-permute-done.12 = f32[32,768]{1,0:T(8,128)S(1)} collective-permute-done((f32[32,768]{1,0:T(8,128)S(1)}, f32[32,768]{1,0:T(8,128)S(1)}, u32[]{:S(2)}, u32[]{:S(2)}) %collective-permute-start.12) | collective-permute-done | bytes 98336 | tf_op jit(solution)/shard_map/ppermute | solution.py:162
  30.2 0.7 %slice_select_fusion = (f32[32,768]{1,0:T(8,128)}, f32[32,768]{1,0:T(8,128)}) fusion(f32[32,768]{1,0:T(8,128)S(1)} %collective-permute-done.12, f32[64,768]{1,0:T(8,128)S(1)} %add_add_fusion, pred[]{:T(512)S(6)} %eq.4), kind=kLoop, calls=%fused_computation.1 | loop fusion | flops 49152 | bytes 393217 | tf_op jit(solution)/shard_map/jit(_where)/select_n | solution.py:203
  (2 shorter events, 0.0 us)
Async XLA Ops:
  0.6 2.0 %collective-permute-start = (bf16[32,768]{1,0:T(8,128)(2,1)}, bf16[32,768]{1,0:T(8,128)(2,1)S(1)}, u32[]{:S(2)}, u32[]{:S(2)}) collective-permute-start(bf16[32,768]{1,0:T(8,128)(2,1)} %q_ref.1), channel_id=1, source_target_pairs={{0,4},{4,0},{1,5},{5,1},{2,6},{6,2},{3,7},{7,3},{8,12},{12,8},{9,1... | collective-permute-start | bytes 147464 | tf_op jit(solution)/shard_map/ppermute | solution.py:162
  1.1 1.5 %collective-permute-start.1 = (bf16[32,768]{1,0:T(8,128)(2,1)}, bf16[32,768]{1,0:T(8,128)(2,1)S(1)}, u32[]{:S(2)}, u32[]{:S(2)}) collective-permute-start(bf16[32,768]{1,0:T(8,128)(2,1)} %p_ref.1), channel_id=1, source_target_pairs={{0,4},{4,0},{1,5},{5,1},{2,6},{6,2},{3,7},{7,3},{8,12},{12,8},{9,1... | collective-permute-start | bytes 147464 | tf_op jit(solution)/shard_map/ppermute | solution.py:162
  1.2 1.4 %collective-permute-start.2 = (f32[32]{0:T(128)}, f32[32]{0:T(128)S(1)}, u32[]{:S(2)}, u32[]{:S(2)}) collective-permute-start(f32[32]{0:T(128)} %param.7), channel_id=1, source_target_pairs={{0,4},{4,0},{1,5},{5,1},{2,6},{6,2},{3,7},{7,3},{8,12},{12,8},{9,1... | collective-permute-start | bytes 392 | tf_op jit(solution)/shard_map/ppermute | solution.py:162
  2.6 0.7 %copy-start.2 = (f32[256]{0:T(256)S(1)}, f32[256]{0:T(256)}, u32[]{:S(2)}) copy-start(f32[256]{0:T(256)} %param.8) | copy-start | bytes 3076
  2.6 0.7 %copy-start.3 = (f32[32]{0:T(128)S(1)}, f32[32]{0:T(128)}, u32[]{:S(2)}) copy-start(f32[32]{0:T(128)} %param.7) | copy-start | bytes 388
  3.3 0.8 %copy-start = (bf16[32,768]{1,0:T(8,128)(2,1)S(1)}, bf16[32,768]{1,0:T(8,128)(2,1)}, u32[]{:S(2)}) copy-start(bf16[32,768]{1,0:T(8,128)(2,1)} %q_ref.1) | copy-start | bytes 147460
  4.1 0.8 %copy-start.1 = (bf16[32,768]{1,0:T(8,128)(2,1)S(1)}, bf16[32,768]{1,0:T(8,128)(2,1)}, u32[]{:S(2)}) copy-start(bf16[32,768]{1,0:T(8,128)(2,1)} %p_ref.1) | copy-start | bytes 147460
  5.0 5.6 %collective-permute-start.3 = (bf16[64,896]{1,0:T(8,128)(2,1)S(1)}, bf16[64,896]{1,0:T(8,128)(2,1)S(1)}, u32[]{:S(2)}, u32[]{:S(2)}) collective-permute-start(bf16[64,896]{1,0:T(8,128)(2,1)S(1)} %get-tuple-element.8.refs_0_), channel_id=1, source_target_pairs={{8,0},{5,4},{9,1},{4,5},{10,2},{7,6},{11,3},{6,7},{0,8},{13,12},{1... | collective-permute-start | bytes 344072 | tf_op jit(solution)/shard_map/ppermute | solution.py:186
  7.9 4.8 %collective-permute-start.4 = (bf16[64,896]{1,0:T(8,128)(2,1)S(1)}, bf16[64,896]{1,0:T(8,128)(2,1)S(1)}, u32[]{:S(2)}, u32[]{:S(2)}) collective-permute-start(bf16[64,896]{1,0:T(8,128)(2,1)S(1)} %get-tuple-element.8.refs_0_), channel_id=1, source_target_pairs={{16,0},{6,4},{17,1},{7,5},{18,2},{4,6},{19,3},{5,7},{24,8},{14,12}... | collective-permute-start | bytes 344072 | tf_op jit(solution)/shard_map/ppermute | solution.py:186
  9.4 5.7 %collective-permute-start.5 = (bf16[64,896]{1,0:T(8,128)(2,1)S(1)}, bf16[64,896]{1,0:T(8,128)(2,1)S(1)}, u32[]{:S(2)}, u32[]{:S(2)}) collective-permute-start(bf16[64,896]{1,0:T(8,128)(2,1)S(1)} %get-tuple-element.8.refs_0_), channel_id=1, source_target_pairs={{24,0},{7,4},{25,1},{6,5},{26,2},{5,6},{27,3},{4,7},{16,8},{15,12}... | collective-permute-start | bytes 344072 | tf_op jit(solution)/shard_map/ppermute | solution.py:186
  10.6 5.8 %collective-permute-start.6 = (bf16[64,896]{1,0:T(8,128)(2,1)S(1)}, bf16[64,896]{1,0:T(8,128)(2,1)S(1)}, u32[]{:S(2)}, u32[]{:S(2)}) collective-permute-start(bf16[64,896]{1,0:T(8,128)(2,1)S(1)} %collective-permute-done.3.refs_1_), channel_id=1, source_target_pairs={{0,4},{4,0},{1,5},{5,1},{2,6},{6,2},{3,7},{7,3},{8,12},{12,8},{9,1... | collective-permute-start | bytes 344072 | tf_op jit(solution)/shard_map/ppermute | solution.py:162
  12.7 3.7 %collective-permute-start.7 = (bf16[64,896]{1,0:T(8,128)(2,1)S(1)}, bf16[64,896]{1,0:T(8,128)(2,1)S(1)}, u32[]{:S(2)}, u32[]{:S(2)}) collective-permute-start(bf16[64,896]{1,0:T(8,128)(2,1)S(1)} %collective-permute-done.4.refs_2_), channel_id=1, source_target_pairs={{0,4},{4,0},{1,5},{5,1},{2,6},{6,2},{3,7},{7,3},{8,12},{12,8},{9,1... | collective-permute-start | bytes 344072 | tf_op jit(solution)/shard_map/ppermute | solution.py:162
  15.1 1.6 %collective-permute-start.8 = (bf16[64,896]{1,0:T(8,128)(2,1)S(1)}, bf16[64,896]{1,0:T(8,128)(2,1)S(1)}, u32[]{:S(2)}, u32[]{:S(2)}) collective-permute-start(bf16[64,896]{1,0:T(8,128)(2,1)S(1)} %collective-permute-done.5.refs_3_), channel_id=1, source_target_pairs={{0,4},{4,0},{1,5},{5,1},{2,6},{6,2},{3,7},{7,3},{8,12},{12,8},{9,1... | collective-permute-start | bytes 344072 | tf_op jit(solution)/shard_map/ppermute | solution.py:162
  17.6 6.9 %collective-permute-start.10 = (f32[64,768]{1,0:T(8,128)S(1)}, f32[64,768]{1,0:T(8,128)S(1)}, u32[]{:S(2)}, u32[]{:S(2)}) collective-permute-start(f32[64,768]{1,0:T(8,128)S(1)} %get-tuple-element.12), channel_id=1, source_target_pairs={{0,16},{4,6},{1,17},{5,7},{2,18},{6,4},{3,19},{7,5},{8,24},{12,14}... | collective-permute-start | bytes 589832 | tf_op jit(solution)/shard_map/ppermute | solution.py:200
  19.2 6.6 %collective-permute-start.11 = (f32[64,768]{1,0:T(8,128)S(1)}, f32[64,768]{1,0:T(8,128)S(1)}, u32[]{:S(2)}, u32[]{:S(2)}) collective-permute-start(f32[64,768]{1,0:T(8,128)S(1)} %get-tuple-element.13), channel_id=1, source_target_pairs={{0,24},{4,7},{1,25},{5,6},{2,26},{6,5},{3,27},{7,4},{8,16},{12,15}... | collective-permute-start | bytes 589832 | tf_op jit(solution)/shard_map/ppermute | solution.py:200
  20.7 6.3 %collective-permute-start.9 = (f32[64,768]{1,0:T(8,128)S(1)}, f32[64,768]{1,0:T(8,128)S(1)}, u32[]{:S(2)}, u32[]{:S(2)}) collective-permute-start(f32[64,768]{1,0:T(8,128)S(1)} %get-tuple-element.11), channel_id=1, source_target_pairs={{0,8},{4,5},{1,9},{5,4},{2,10},{6,7},{3,11},{7,6},{8,0},{12,13},{9... | collective-permute-start | bytes 589832 | tf_op jit(solution)/shard_map/ppermute | solution.py:200
  27.1 3.1 %collective-permute-start.12 = (f32[32,768]{1,0:T(8,128)S(1)}, f32[32,768]{1,0:T(8,128)S(1)}, u32[]{:S(2)}, u32[]{:S(2)}) collective-permute-start(f32[32,768]{1,0:T(8,128)S(1)} %slice.9), channel_id=1, source_target_pairs={{0,4},{4,0},{1,5},{5,1},{2,6},{6,2},{3,7},{7,3},{8,12},{12,8},{9,1... | collective-permute-start | bytes 294920 | tf_op jit(solution)/shard_map/ppermute | solution.py:162

commit v3 on v2

v3 whole, which is shorter than its diff:
```python
import functools
import math

import jax
import jax.numpy as jnp
from jax import lax
from jax.experimental import pallas as pl
from jax.experimental.pallas import tpu as pltpu
from jax.sharding import PartitionSpec as P

AXES = ("slab", "blk")
LANES = 128
NORM_ROWS = 16
SIZE_ROWS = 8
ORDER = ((3, 2, 1), (3, 2, 1))
BACK_ORDER = ((1, 2, 3), (1, 2, 3))


def peer(index, step, count):
    if count & (count - 1) == 0:
        return index ^ step
    return (index + step) % count


class Plan:
    def __init__(self, slab_count, blk_count):
        self.blk_count = blk_count
        self.chip_count = slab_count // 2
        self.group_size = max(self.chip_count, blk_count)

    def device(self, chip, core, blk):
        return (2 * chip + core) * self.blk_count + blk

    def each(self):
        for chip in range(self.chip_count):
            for blk in range(self.blk_count):
                yield chip, blk

    def core_pairs(self):
        return [
            (self.device(chip, core, blk), self.device(chip, 1 - core, blk))
            for chip, blk in self.each()
            for core in (0, 1)
        ]

    def group_pairs(self, step):
        pairs = []
        for chip, blk in self.each():
            if step < self.chip_count:
                other = peer(chip, step, self.chip_count)
                pairs.append((self.device(chip, 0, blk), self.device(other, 0, blk)))
            if step < self.blk_count:
                other = peer(blk, step, self.blk_count)
                pairs.append((self.device(chip, 1, blk), self.device(chip, 1, other)))
        return pairs


def column(values, first, rows):
    shape = (rows, values.shape[1])
    lane = lax.broadcasted_iota(jnp.int32, shape, 1)
    row = lax.broadcasted_iota(jnp.int32, shape, 0)
    picked = jnp.where(lane == row + first, jnp.broadcast_to(values, shape), 0.0)
    return jnp.sum(picked, axis=1, keepdims=True)


def as_row(values, lanes):
    shape = (values.shape[0], lanes)
    lane = lax.broadcasted_iota(jnp.int32, shape, 1)
    row = lax.broadcasted_iota(jnp.int32, shape, 0)
    picked = jnp.where(lane == row, jnp.broadcast_to(values, shape), 0.0)
    return jnp.sum(picked, axis=0, keepdims=True)


def split_three(values):
    high = values.astype(jnp.bfloat16).astype(jnp.float32)
    middle = (values - high).astype(jnp.bfloat16).astype(jnp.float32)
    return high, middle, values - high - middle


def write_block(out_ref, halves, norms):
    rows, width = halves[0].shape
    for chunk in range(width // LANES):
        for half in (0, 1):
            start = (2 * chunk + half) * rows
            out_ref[start : start + rows] = halves[half][:, chunk * LANES : (chunk + 1) * LANES]
    shape = (NORM_ROWS, LANES)
    row = lax.broadcasted_iota(jnp.int32, shape, 0)
    tail = jnp.zeros(shape, jnp.float32)
    for half in (0, 1):
        for i, part in enumerate(split_three(as_row(norms[half], LANES))):
            tail = jnp.where(row == 3 * half + i, jnp.broadcast_to(part, shape), tail)
    out_ref[2 * rows * (width // LANES) :] = tail.astype(jnp.bfloat16)


def read_block(ref, rows):
    chunks = (ref.shape[0] - NORM_ROWS) // (2 * rows)
    block = jnp.concatenate(
        [ref[2 * rows * i : 2 * rows * (i + 1)] for i in range(chunks)], axis=1
    )
    tail = ref[2 * rows * chunks :].astype(jnp.float32)
    norms = [
        column(tail[i : i + 1] + tail[i + 1 : i + 2] + tail[i + 2 : i + 3], 0, rows) for i in (0, 3)
    ]
    return block, jnp.concatenate(norms, axis=0)


def pack_kernel(
    slab_ref, role_ref, other_ref, got_q_ref, got_p_ref, norm_ref, got_norm_ref, a_ref, b_ref
):
    rows = role_ref.shape[0]
    slab = slab_ref[0]
    pick = functools.partial(jnp.where, (slab & 1) == 1)
    own_q = column(norm_ref[...], 0, rows)
    got_q = column(got_norm_ref[...], 0, rows)
    own_p = column(norm_ref[...], (1 + slab) * rows, rows)
    got_p = column(norm_ref[...], (1 + (slab ^ 1)) * rows, rows)
    write_block(
        a_ref,
        (role_ref[...], pick(got_q_ref[...], got_p_ref[...])),
        (pick(own_q, own_p), pick(got_q, got_p)),
    )
    write_block(
        b_ref,
        (pick(got_p_ref[...], got_q_ref[...]), other_ref[...]),
        (pick(got_p, got_q), pick(own_p, own_q)),
    )


def row_numbers(plan, slab, blk, role, rows, place):
    chip = slab >> 1
    number = place
    for step in range(plan.group_size):
        for other in (0, 1):
            core = role ^ other
            p_shard = blk * (2 * plan.chip_count) + 2 * peer(chip, step, plan.chip_count) + core
            q_shard = (2 * chip + core) * plan.blk_count + peer(blk, step, plan.blk_count)
            p_base = p_shard * rows if step < plan.chip_count else -(1 << 24)
            q_base = q_shard * rows if step < plan.blk_count else -(1 << 25)
            start = (2 * step + other) * rows
            base = jnp.where(role == 0, p_base, q_base) - start
            number = jnp.where(place >= start, place + base, number)
    return number


def tile_kernel(plan, rows, slab_ref, blk_ref, loss_ref, *refs):
    count = plan.group_size
    a_refs, b_refs, out_refs = refs[:count], refs[count : 2 * count], refs[2 * count :]
    a, a_norm = (jnp.concatenate(x, axis=0) for x in zip(*(read_block(r, rows) for r in a_refs)))
    b, b_norm = (jnp.concatenate(x, axis=0) for x in zip(*(read_block(r, rows) for r in b_refs)))
    b_norm = as_row(b_norm, b_norm.shape[0])
    scale = 2.0 / math.sqrt(a.shape[1])
    scores = scale * lax.dot_general(
        a, b, (((1,), (1,)), ((), ())), preferred_element_type=jnp.float32
    )
    slab, blk = slab_ref[0], blk_ref[0]
    role = slab & 1
    numbers = functools.partial(row_numbers, plan, slab, blk, rows=rows)
    a_number = numbers(role, place=lax.broadcasted_iota(jnp.int32, (a.shape[0], 1), 0))
    b_number = numbers(1 - role, place=lax.broadcasted_iota(jnp.int32, (1, b.shape[0]), 1))
    paired = (a_number == b_number).astype(jnp.float32)
    weights = (0.5 * loss_ref[0]) * (
        jnp.exp(scores - a_norm) + jnp.exp(scores - b_norm) - 2.0 * paired
    )
    high = weights.astype(jnp.bfloat16)
    low = (weights - high.astype(jnp.float32)).astype(jnp.bfloat16)
    total = jnp.dot(high, b, preferred_element_type=jnp.float32) + jnp.dot(
        low, b, preferred_element_type=jnp.float32
    )
    total = scale * total
    out_refs[0][...] = total[: 2 * rows]
    for i in range(1, count):
        write_partial(out_refs[i], total[2 * rows * i : 2 * rows * (i + 1)])


def write_partial(ref, block):
    rows, width = block.shape
    largest = jnp.maximum(jnp.max(jnp.abs(block), keepdims=True), 1e-30)
    power = jnp.ceil(jnp.log2(largest)) - 10.0
    block = block * jnp.exp2(-power)
    for chunk in range(width // LANES):
        ref[chunk * rows : (chunk + 1) * rows] = block[:, chunk * LANES : (chunk + 1) * LANES]
    ref[rows * (width // LANES) :] = jnp.broadcast_to(power, (SIZE_ROWS, LANES))


def sum_kernel(own_ref, *refs):
    partial_refs, (keep_ref, give_ref) = refs[:-2], refs[-2:]
    rows, width = own_ref.shape
    tail = rows * (width // LANES)
    factors = [jnp.exp2(ref[tail : tail + 1]) for ref in partial_refs]
    for chunk in range(width // LANES):
        lanes = slice(chunk * LANES, (chunk + 1) * LANES)
        total = own_ref[:, lanes]
        for ref, factor in zip(partial_refs, factors):
            total = total + ref[chunk * rows : (chunk + 1) * rows] * factor
        keep_ref[:, lanes] = total[: rows // 2]
        give_ref[:, lanes] = total[rows // 2 :]


VMEM = pl.BlockSpec(memory_space=pltpu.VMEM)
SMEM = pl.BlockSpec(memory_space=pltpu.SMEM)


def call(kernel, name, scalars, arrays, out_shape, mebibytes):
    return pl.pallas_call(
        kernel,
        out_shape=out_shape,
        in_specs=[SMEM] * len(scalars) + [VMEM] * len(arrays),
        out_specs=[VMEM] * len(out_shape),
        name=name,
        compiler_params=pltpu.CompilerParams(vmem_limit_bytes=mebibytes * 1024 * 1024),
    )(*(x.reshape(1) for x in scalars), *arrays)


def local(plan, queries, passages, query_lognorm, passage_lognorm, loss_cotangent):
    rows, width = queries.shape
    count = plan.group_size
    chunk_rows = 2 * rows * (width // LANES)
    slab = lax.axis_index("slab")
    blk = lax.axis_index("blk")
    core = slab & 1

    def swapped(block):
        return lax.ppermute(block, AXES, plan.core_pairs())

    packed = jax.ShapeDtypeStruct((chunk_rows + NORM_ROWS, LANES), jnp.bfloat16)
    mine, others = call(
        pack_kernel,
        "pack",
        (slab,),
        (
            jnp.where(core == 1, queries, passages),
            jnp.where(core == 1, passages, queries),
            swapped(queries),
            swapped(passages),
            jnp.concatenate([query_lognorm, passage_lognorm]).reshape(1, -1),
            swapped(query_lognorm).reshape(1, -1),
        ),
        [packed, packed],
        4,
    )

    a_parts, b_parts = [mine], [others]
    for step in range(1, count):
        back = [(to, at) for at, to in plan.group_pairs(step)]
        a_parts.append(lax.ppermute(mine, AXES, back))
        b_parts.append(swapped(a_parts[-1]))

    whole = jax.ShapeDtypeStruct((2 * rows, width), jnp.float32)
    half = jax.ShapeDtypeStruct((rows, width), jnp.float32)
    partial = jax.ShapeDtypeStruct((chunk_rows + SIZE_ROWS, LANES), jnp.float32)
    own, *partials = call(
        functools.partial(tile_kernel, plan, rows),
        "tile",
        (slab, blk, loss_cotangent),
        (*a_parts, *b_parts),
        [whole] + [partial] * (count - 1),
        3 * count,
    )

    arrived = [
        lax.ppermute(x.astype(jnp.float16), AXES, plan.group_pairs(1 + i)).astype(jnp.float32)
        for i, x in enumerate(partials)
    ]
    keep, give = call(sum_kernel, "sum", (), (own, *arrived), [half, half], 2 * count)
    got = swapped(give)
    return jnp.where(core == 1, keep, got), jnp.where(core == 1, got, keep)


def solution(mesh):
    plan = Plan(mesh.shape["slab"], mesh.shape["blk"])
    return jax.shard_map(
        functools.partial(local, plan),
        mesh=mesh,
        in_specs=(
            P(("slab", "blk"), None),
            P(("blk", "slab"), None),
            P(("slab", "blk")),
            P("blk"),
            P(),
        ),
        out_specs=(P(("slab", "blk"), None), P(("blk", "slab"), None)),
        check_vma=False,
    )
```

time: 31.1 us -> 24.8 us (0.80)
  waiting for transfers between devices: 12.7 us -> 9.58 us
  local copies, waits for them, and re-layouts: 2.28 us -> 0.01 us
  starting transfers between devices: 12.8 us -> 10.8 us
  other arithmetic: 0.73 us -> 1.72 us
    unnamed x8 -> x4, local copies, waits for them, and re-layouts: 2.27 us -> 0.01 us
    ppermute x7, starting transfers between devices: 4.84 us -> 2.64 us  [swapped(): return lax.ppermute(block, AXES, plan.core_pairs())]
    ppermute x3, waiting for transfers between devices: 5.8 us -> 4.06 us  [local(): lax.ppermute(x.astype(jnp.float16), AXES, plan.group_pairs(1 + i))]
    ppermute x3, waiting for transfers between devices: 4.67 us -> 3.47 us  [local(): a_parts.append(lax.ppermute(mine, AXES, back))]
    select_n x1 -> x2, other arithmetic: 0.69 us -> 1.55 us  [the longest x1 0.86 us: local(): jnp.where(core == 1, passages, queries)]
    pallas_call x2 -> x3, Pallas kernels: 1.04 us -> 1.22 us  [call(): pl.pallas_call(kernel, out_shape=out_shape, in_specs=[SMEM] * len(scalars...]
  transfers between devices with their start and end apart: 13 -> 13, of which waited for: 9 -> 9; matrix products, arithmetic and copies ran while one was open for 0% -> 4% of each run, Pallas kernels for 0% -> 0%
where the time goes in v3:
time: 24.8 us; the launch traced here: 24.7 us
  starting transfers between devices  10.8 us (44%)
  waiting for transfers between devices  9.58 us (39%)
  other arithmetic  1.72 us (7%)
  between operations  1.37 us (6%)
  Pallas kernels  1.22 us (5%)
    ppermute x3, starting transfers between devices, local(): a_parts.append(lax.ppermute(mine, AXES, back))  4.5 us
    ppermute x3, waiting for transfers between devices, local(): lax.ppermute(x.astype(jnp.float16), AXES, plan.group_pairs(1 + i))  4.06 us
    ppermute x3, starting transfers between devices, local(): lax.ppermute(x.astype(jnp.float16), AXES, plan.group_pairs(1 + i))  3.62 us
    ppermute x3, waiting for transfers between devices, local(): a_parts.append(lax.ppermute(mine, AXES, back))  3.47 us
    ppermute x7, starting transfers between devices, swapped(): return lax.ppermute(block, AXES, plan.core_pairs())  2.64 us
    ppermute x7, waiting for transfers between devices, swapped(): return lax.ppermute(block, AXES, plan.core_pairs())  2.05 us
    pallas_call x3, Pallas kernels, call(): pl.pallas_call(kernel, out_shape=out_shape, in_specs=[SMEM] * len(scalars...  1.22 us
    select_n x1, other arithmetic, local(): jnp.where(core == 1, passages, queries)  0.86 us
  transfers between devices with their start and end apart: 13, of which 9 were waited for; matrix products, arithmetic and copies ran while one was open for 4% of the time, Pallas kernels for 0%

profile of v3, /device:TPU:0, one launch (start us, length us, event | category | flops | bytes accessed | tf_op | source)
XLA Modules:
  0.0 24.7 jit_solution(16075729035696609671)
XLA Ops:
  0.6 0.5 %collective-permute-start.2 = (f32[32]{0:T(128)}, f32[32]{0:T(128)S(1)}, u32[]{:S(2)}, u32[]{:S(2)}) collective-permute-start(f32[32]{0:T(128)} %param.7), channel_id=1, source_target_pairs={{0,4},{4,0},{1,5},{5,1},{2,6},{6,2},{3,7},{7,3},{8,12},{12,8},{9,1... | collective-permute-start | bytes 392 | tf_op jit(solution)/shard_map/ppermute | solution.py:223
  1.1 0.1 collective-permute-start
  1.2 0.4 %collective-permute-start.1 = (bf16[32,768]{1,0:T(8,128)(2,1)}, bf16[32,768]{1,0:T(8,128)(2,1)S(1)}, u32[]{:S(2)}, u32[]{:S(2)}) collective-permute-start(bf16[32,768]{1,0:T(8,128)(2,1)} %param.6), channel_id=1, source_target_pairs={{0,4},{4,0},{1,5},{5,1},{2,6},{6,2},{3,7},{7,3},{8,12},{12,8},{9,1... | collective-permute-start | bytes 147464 | tf_op jit(solution)/shard_map/ppermute | solution.py:223
  1.7 0.0 copy-start
  1.7 0.0 copy-start.1
  1.7 0.9 %broadcast_select_fusion.2 = (bf16[32,768]{1,0:T(8,128)(2,1)S(1)}, bf16[32,768]{1,0:T(8,128)(2,1)S(1)}) fusion(bf16[32,768]{1,0:T(8,128)(2,1)} %param.6, bf16[32,768]{1,0:T(8,128)(2,1)} %param.5, pred[]{:T(512)S(6)} %eq.2), kind=kLoop, calls=%fused_computation.2 | loop fusion | flops 49152 | bytes 196609 | tf_op jit(solution)/shard_map/jit(_where)/select_n | solution.py:232
  2.5 0.0 copy-done
  2.5 0.0 copy-done.1
  2.5 0.1 pad_maximum_fusion
  2.6 0.0 collective-permute-done.2
  2.6 0.0 collective-permute-done.got_q_ref
  2.6 0.1 collective-permute-done.1.got_p_ref
  2.8 0.1 pack.1
  2.9 3.9 %collective-permute-start.5 = (bf16[400,128]{1,0:T(8,128)(2,1)S(1)}, bf16[400,128]{1,0:T(8,128)(2,1)S(1)}, u32[]{:S(2)}, u32[]{:S(2)}) collective-permute-start(bf16[400,128]{1,0:T(8,128)(2,1)S(1)} %get-tuple-element.10.refs_0_), channel_id=1, source_target_pairs={{24,0},{7,4},{25,1},{6,5},{26,2},{5,6},{27,3},{4,7},{16,8},{15,12}... | collective-permute-start | bytes 307208 | tf_op jit(solution)/shard_map/ppermute | solution.py:245
  6.7 0.5 %collective-permute-start.4 = (bf16[400,128]{1,0:T(8,128)(2,1)S(1)}, bf16[400,128]{1,0:T(8,128)(2,1)S(1)}, u32[]{:S(2)}, u32[]{:S(2)}) collective-permute-start(bf16[400,128]{1,0:T(8,128)(2,1)S(1)} %get-tuple-element.10.refs_0_), channel_id=1, source_target_pairs={{16,0},{6,4},{17,1},{7,5},{18,2},{4,6},{19,3},{5,7},{24,8},{14,12}... | collective-permute-start | bytes 307208 | tf_op jit(solution)/shard_map/ppermute | solution.py:245
  7.3 0.1 collective-permute-start.3
  7.4 2.0 %collective-permute-done.5.refs_3_ = bf16[400,128]{1,0:T(8,128)(2,1)S(1)} collective-permute-done((bf16[400,128]{1,0:T(8,128)(2,1)S(1)}, bf16[400,128]{1,0:T(8,128)(2,1)S(1)}, u32[]{:S(2)}, u32[]{:S(2)}) %collective-permute-start.5) | collective-permute-done | bytes 102432 | tf_op jit(solution)/shard_map/ppermute | solution.py:245
  9.4 0.6 %collective-permute-start.8 = (bf16[400,128]{1,0:T(8,128)(2,1)S(1)}, bf16[400,128]{1,0:T(8,128)(2,1)S(1)}, u32[]{:S(2)}, u32[]{:S(2)}) collective-permute-start(bf16[400,128]{1,0:T(8,128)(2,1)S(1)} %collective-permute-done.5.refs_3_), channel_id=1, source_target_pairs={{0,4},{4,0},{1,5},{5,1},{2,6},{6,2},{3,7},{7,3},{8,12},{12,8},{9,1... | collective-permute-start | bytes 307208 | tf_op jit(solution)/shard_map/ppermute | solution.py:223
  9.9 1.5 %collective-permute-done.4.refs_2_ = bf16[400,128]{1,0:T(8,128)(2,1)S(1)} collective-permute-done((bf16[400,128]{1,0:T(8,128)(2,1)S(1)}, bf16[400,128]{1,0:T(8,128)(2,1)S(1)}, u32[]{:S(2)}, u32[]{:S(2)}) %collective-permute-start.4) | collective-permute-done | bytes 102432 | tf_op jit(solution)/shard_map/ppermute | solution.py:245
  11.4 1.0 %collective-permute-start.7 = (bf16[400,128]{1,0:T(8,128)(2,1)S(1)}, bf16[400,128]{1,0:T(8,128)(2,1)S(1)}, u32[]{:S(2)}, u32[]{:S(2)}) collective-permute-start(bf16[400,128]{1,0:T(8,128)(2,1)S(1)} %collective-permute-done.4.refs_2_), channel_id=1, source_target_pairs={{0,4},{4,0},{1,5},{5,1},{2,6},{6,2},{3,7},{7,3},{8,12},{12,8},{9,1... | collective-permute-start | bytes 307208 | tf_op jit(solution)/shard_map/ppermute | solution.py:223
  12.4 0.0 collective-permute-done.3.refs_1_
  12.4 0.0 collective-permute-start.6
  13.0 0.0 collective-permute-done.8.refs_7_
  13.1 0.3 %collective-permute-done.7.refs_6_ = bf16[400,128]{1,0:T(8,128)(2,1)S(1)} collective-permute-done((bf16[400,128]{1,0:T(8,128)(2,1)S(1)}, bf16[400,128]{1,0:T(8,128)(2,1)S(1)}, u32[]{:S(2)}, u32[]{:S(2)}) %collective-permute-start.7) | collective-permute-done | bytes 102432 | tf_op jit(solution)/shard_map/ppermute | solution.py:223
  13.3 0.4 %collective-permute-done.6.refs_5_ = bf16[400,128]{1,0:T(8,128)(2,1)S(1)} collective-permute-done((bf16[400,128]{1,0:T(8,128)(2,1)S(1)}, bf16[400,128]{1,0:T(8,128)(2,1)S(1)}, u32[]{:S(2)}, u32[]{:S(2)}) %collective-permute-start.6) | collective-permute-done | bytes 102432 | tf_op jit(solution)/shard_map/ppermute | solution.py:223
  13.7 1.0 %tile.1 = (f32[64,768]{1,0:T(8,128)S(1)}, f32[392,128]{1,0:T(8,128)S(1)}, f32[392,128]{1,0:T(8,128)S(1)}, f32[392,128]{1,0:T(8,128)S(1)}) custom-call(s32[1]{0:T(128)} %bitcast.slab_ref, s32[1]{0:T(128)} %bitcast.1.blk_ref, f32[1]{0:T(128)} %bitcast.4.loss_ref, bf16[400,128]{1,0:T(8,128)(2,1)S(1)} %get-tuple-element.10.refs_0_, ...), custom_call_target="tpu_custom_call" | custom-call | tf_op jit(solution)/shard_map/tile/pallas_call | solution.py:204
  14.8 2.5 %collective-permute-start.11 = (f16[392,128]{1,0:T(8,128)(2,1)S(1)}, f16[392,128]{1,0:T(8,128)(2,1)S(1)}, u32[]{:S(2)}, u32[]{:S(2)}) collective-permute-start(f16[392,128]{1,0:T(8,128)(2,1)S(1)} %convert_element_type.22), channel_id=1, source_target_pairs={{0,24},{4,7},{1,25},{5,6},{2,26},{6,5},{3,27},{7,4},{8,16},{12,15}... | collective-permute-start | bytes 301064 | tf_op jit(solution)/shard_map/ppermute | solution.py:261
  17.3 0.5 %collective-permute-start.10 = (f16[392,128]{1,0:T(8,128)(2,1)S(1)}, f16[392,128]{1,0:T(8,128)(2,1)S(1)}, u32[]{:S(2)}, u32[]{:S(2)}) collective-permute-start(f16[392,128]{1,0:T(8,128)(2,1)S(1)} %convert_element_type.20), channel_id=1, source_target_pairs={{0,16},{4,6},{1,17},{5,7},{2,18},{6,4},{3,19},{7,5},{8,24},{12,14}... | collective-permute-start | bytes 301064 | tf_op jit(solution)/shard_map/ppermute | solution.py:261
  17.8 0.6 %collective-permute-start.9 = (f16[392,128]{1,0:T(8,128)(2,1)S(1)}, f16[392,128]{1,0:T(8,128)(2,1)S(1)}, u32[]{:S(2)}, u32[]{:S(2)}) collective-permute-start(f16[392,128]{1,0:T(8,128)(2,1)S(1)} %convert_element_type.18), channel_id=1, source_target_pairs={{0,8},{4,5},{1,9},{5,4},{2,10},{6,7},{3,11},{7,6},{8,0},{12,13},{9... | collective-permute-start | bytes 301064 | tf_op jit(solution)/shard_map/ppermute | solution.py:261
  18.4 2.0 %collective-permute-done.11 = f16[392,128]{1,0:T(8,128)(2,1)S(1)} collective-permute-done((f16[392,128]{1,0:T(8,128)(2,1)S(1)}, f16[392,128]{1,0:T(8,128)(2,1)S(1)}, u32[]{:S(2)}, u32[]{:S(2)}) %collective-permute-start.11) | collective-permute-done | bytes 100384 | tf_op jit(solution)/shard_map/ppermute | solution.py:261
  20.4 1.5 %collective-permute-done.10 = f16[392,128]{1,0:T(8,128)(2,1)S(1)} collective-permute-done((f16[392,128]{1,0:T(8,128)(2,1)S(1)}, f16[392,128]{1,0:T(8,128)(2,1)S(1)}, u32[]{:S(2)}, u32[]{:S(2)}) %collective-permute-start.10) | collective-permute-done | bytes 100384 | tf_op jit(solution)/shard_map/ppermute | solution.py:261
  21.9 0.6 %collective-permute-done.9 = f16[392,128]{1,0:T(8,128)(2,1)S(1)} collective-permute-done((f16[392,128]{1,0:T(8,128)(2,1)S(1)}, f16[392,128]{1,0:T(8,128)(2,1)S(1)}, u32[]{:S(2)}, u32[]{:S(2)}) %collective-permute-start.9) | collective-permute-done | bytes 100384 | tf_op jit(solution)/shard_map/ppermute | solution.py:261
  22.5 0.1 sum.1
  22.6 0.1 collective-permute-start.12
  22.7 1.3 %collective-permute-done.12 = f32[32,768]{1,0:T(8,128)S(1)} collective-permute-done((f32[32,768]{1,0:T(8,128)S(1)}, f32[32,768]{1,0:T(8,128)S(1)}, u32[]{:S(2)}, u32[]{:S(2)}) %collective-permute-start.12) | collective-permute-done | bytes 98336 | tf_op jit(solution)/shard_map/ppermute | solution.py:223
  24.0 0.7 %broadcast_select_fusion = (f32[32,768]{1,0:T(8,128)}, f32[32,768]{1,0:T(8,128)}) fusion(f32[32,768]{1,0:T(8,128)S(1)} %collective-permute-done.12, f32[32,768]{1,0:T(8,128)S(1)} %get-tuple-element.16, pred[]{:T(512)S(6)} %eq.2), kind=kLoop, calls=%fused_computation | loop fusion | flops 49152 | bytes 393217 | tf_op jit(solution)/shard_map/jit(_where)/select_n | solution.py:266
  (7 shorter events, 0.1 us)
Async XLA Ops:
  0.6 2.0 %collective-permute-start.2 = (f32[32]{0:T(128)}, f32[32]{0:T(128)S(1)}, u32[]{:S(2)}, u32[]{:S(2)}) collective-permute-start(f32[32]{0:T(128)} %param.7), channel_id=1, source_target_pairs={{0,4},{4,0},{1,5},{5,1},{2,6},{6,2},{3,7},{7,3},{8,12},{12,8},{9,1... | collective-permute-start | bytes 392 | tf_op jit(solution)/shard_map/ppermute | solution.py:223
  1.1 1.5 %collective-permute-start = (bf16[32,768]{1,0:T(8,128)(2,1)}, bf16[32,768]{1,0:T(8,128)(2,1)S(1)}, u32[]{:S(2)}, u32[]{:S(2)}) collective-permute-start(bf16[32,768]{1,0:T(8,128)(2,1)} %param.5), channel_id=1, source_target_pairs={{0,4},{4,0},{1,5},{5,1},{2,6},{6,2},{3,7},{7,3},{8,12},{12,8},{9,1... | collective-permute-start | bytes 147464 | tf_op jit(solution)/shard_map/ppermute | solution.py:223
  1.2 1.5 %collective-permute-start.1 = (bf16[32,768]{1,0:T(8,128)(2,1)}, bf16[32,768]{1,0:T(8,128)(2,1)S(1)}, u32[]{:S(2)}, u32[]{:S(2)}) collective-permute-start(bf16[32,768]{1,0:T(8,128)(2,1)} %param.6), channel_id=1, source_target_pairs={{0,4},{4,0},{1,5},{5,1},{2,6},{6,2},{3,7},{7,3},{8,12},{12,8},{9,1... | collective-permute-start | bytes 147464 | tf_op jit(solution)/shard_map/ppermute | solution.py:223
  1.7 0.9 %copy-start = (f32[256]{0:T(256)S(1)}, f32[256]{0:T(256)}, u32[]{:S(2)}) copy-start(f32[256]{0:T(256)} %param.8) | copy-start | bytes 3076
  1.7 0.9 %copy-start.1 = (f32[32]{0:T(128)S(1)}, f32[32]{0:T(128)}, u32[]{:S(2)}) copy-start(f32[32]{0:T(128)} %param.7) | copy-start | bytes 388
  2.9 6.5 %collective-permute-start.5 = (bf16[400,128]{1,0:T(8,128)(2,1)S(1)}, bf16[400,128]{1,0:T(8,128)(2,1)S(1)}, u32[]{:S(2)}, u32[]{:S(2)}) collective-permute-start(bf16[400,128]{1,0:T(8,128)(2,1)S(1)} %get-tuple-element.10.refs_0_), channel_id=1, source_target_pairs={{24,0},{7,4},{25,1},{6,5},{26,2},{5,6},{27,3},{4,7},{16,8},{15,12}... | collective-permute-start | bytes 307208 | tf_op jit(solution)/shard_map/ppermute | solution.py:245
  6.7 4.7 %collective-permute-start.4 = (bf16[400,128]{1,0:T(8,128)(2,1)S(1)}, bf16[400,128]{1,0:T(8,128)(2,1)S(1)}, u32[]{:S(2)}, u32[]{:S(2)}) collective-permute-start(bf16[400,128]{1,0:T(8,128)(2,1)S(1)} %get-tuple-element.10.refs_0_), channel_id=1, source_target_pairs={{16,0},{6,4},{17,1},{7,5},{18,2},{4,6},{19,3},{5,7},{24,8},{14,12}... | collective-permute-start | bytes 307208 | tf_op jit(solution)/shard_map/ppermute | solution.py:245
  7.3 5.1 %collective-permute-start.3 = (bf16[400,128]{1,0:T(8,128)(2,1)S(1)}, bf16[400,128]{1,0:T(8,128)(2,1)S(1)}, u32[]{:S(2)}, u32[]{:S(2)}) collective-permute-start(bf16[400,128]{1,0:T(8,128)(2,1)S(1)} %get-tuple-element.10.refs_0_), channel_id=1, source_target_pairs={{8,0},{5,4},{9,1},{4,5},{10,2},{7,6},{11,3},{6,7},{0,8},{13,12},{1... | collective-permute-start | bytes 307208 | tf_op jit(solution)/shard_map/ppermute | solution.py:245
  9.4 3.7 %collective-permute-start.8 = (bf16[400,128]{1,0:T(8,128)(2,1)S(1)}, bf16[400,128]{1,0:T(8,128)(2,1)S(1)}, u32[]{:S(2)}, u32[]{:S(2)}) collective-permute-start(bf16[400,128]{1,0:T(8,128)(2,1)S(1)} %collective-permute-done.5.refs_3_), channel_id=1, source_target_pairs={{0,4},{4,0},{1,5},{5,1},{2,6},{6,2},{3,7},{7,3},{8,12},{12,8},{9,1... | collective-permute-start | bytes 307208 | tf_op jit(solution)/shard_map/ppermute | solution.py:223
  11.4 1.9 %collective-permute-start.7 = (bf16[400,128]{1,0:T(8,128)(2,1)S(1)}, bf16[400,128]{1,0:T(8,128)(2,1)S(1)}, u32[]{:S(2)}, u32[]{:S(2)}) collective-permute-start(bf16[400,128]{1,0:T(8,128)(2,1)S(1)} %collective-permute-done.4.refs_2_), channel_id=1, source_target_pairs={{0,4},{4,0},{1,5},{5,1},{2,6},{6,2},{3,7},{7,3},{8,12},{12,8},{9,1... | collective-permute-start | bytes 307208 | tf_op jit(solution)/shard_map/ppermute | solution.py:223
  12.4 1.3 %collective-permute-start.6 = (bf16[400,128]{1,0:T(8,128)(2,1)S(1)}, bf16[400,128]{1,0:T(8,128)(2,1)S(1)}, u32[]{:S(2)}, u32[]{:S(2)}) collective-permute-start(bf16[400,128]{1,0:T(8,128)(2,1)S(1)} %collective-permute-done.3.refs_1_), channel_id=1, source_target_pairs={{0,4},{4,0},{1,5},{5,1},{2,6},{6,2},{3,7},{7,3},{8,12},{12,8},{9,1... | collective-permute-start | bytes 307208 | tf_op jit(solution)/shard_map/ppermute | solution.py:223
  14.8 5.6 %collective-permute-start.11 = (f16[392,128]{1,0:T(8,128)(2,1)S(1)}, f16[392,128]{1,0:T(8,128)(2,1)S(1)}, u32[]{:S(2)}, u32[]{:S(2)}) collective-permute-start(f16[392,128]{1,0:T(8,128)(2,1)S(1)} %convert_element_type.22), channel_id=1, source_target_pairs={{0,24},{4,7},{1,25},{5,6},{2,26},{6,5},{3,27},{7,4},{8,16},{12,15}... | collective-permute-start | bytes 301064 | tf_op jit(solution)/shard_map/ppermute | solution.py:261
  17.3 4.6 %collective-permute-start.10 = (f16[392,128]{1,0:T(8,128)(2,1)S(1)}, f16[392,128]{1,0:T(8,128)(2,1)S(1)}, u32[]{:S(2)}, u32[]{:S(2)}) collective-permute-start(f16[392,128]{1,0:T(8,128)(2,1)S(1)} %convert_element_type.20), channel_id=1, source_target_pairs={{0,16},{4,6},{1,17},{5,7},{2,18},{6,4},{3,19},{7,5},{8,24},{12,14}... | collective-permute-start | bytes 301064 | tf_op jit(solution)/shard_map/ppermute | solution.py:261
  17.8 4.7 %collective-permute-start.9 = (f16[392,128]{1,0:T(8,128)(2,1)S(1)}, f16[392,128]{1,0:T(8,128)(2,1)S(1)}, u32[]{:S(2)}, u32[]{:S(2)}) collective-permute-start(f16[392,128]{1,0:T(8,128)(2,1)S(1)} %convert_element_type.18), channel_id=1, source_target_pairs={{0,8},{4,5},{1,9},{5,4},{2,10},{6,7},{3,11},{7,6},{8,0},{12,13},{9... | collective-permute-start | bytes 301064 | tf_op jit(solution)/shard_map/ppermute | solution.py:261
  22.6 1.4 %collective-permute-start.12 = (f32[32,768]{1,0:T(8,128)S(1)}, f32[32,768]{1,0:T(8,128)S(1)}, u32[]{:S(2)}, u32[]{:S(2)}) collective-permute-start(f32[32,768]{1,0:T(8,128)S(1)} %get-tuple-element.17), channel_id=1, source_target_pairs={{0,4},{4,0},{1,5},{5,1},{2,6},{6,2},{3,7},{7,3},{8,12},{12,8},{9,1... | collective-permute-start | bytes 294920 | tf_op jit(solution)/shard_map/ppermute | solution.py:223

commit v4 on v3

--- a/solution.py
+++ b/solution.py
@@ -12,8 +12,6 @@
 LANES = 128
 NORM_ROWS = 16
 SIZE_ROWS = 8
-ORDER = ((3, 2, 1), (3, 2, 1))
-BACK_ORDER = ((1, 2, 3), (1, 2, 3))
 
 
 def peer(index, step, count):
@@ -92,16 +90,35 @@
     out_ref[2 * rows * (width // LANES) :] = tail.astype(jnp.bfloat16)
 
 
-def read_block(ref, rows):
-    chunks = (ref.shape[0] - NORM_ROWS) // (2 * rows)
-    block = jnp.concatenate(
-        [ref[2 * rows * i : 2 * rows * (i + 1)] for i in range(chunks)], axis=1
-    )
-    tail = ref[2 * rows * chunks :].astype(jnp.float32)
-    norms = [
-        column(tail[i : i + 1] + tail[i + 1 : i + 2] + tail[i + 2 : i + 3], 0, rows) for i in (0, 3)
-    ]
-    return block, jnp.concatenate(norms, axis=0)
+def read_rows(refs, rows):
+    size = 2 * rows
+    chunks = (refs[0].shape[0] - NORM_ROWS) // size
+    parts = [[ref[size * i : size * (i + 1)] for i in range(chunks)] for ref in refs]
+    return jnp.concatenate([jnp.concatenate(part, axis=1) for part in parts], axis=0)
+
+
+def read_norms(refs):
+    norms = []
+    for ref in refs:
+        tail = ref[ref.shape[0] - NORM_ROWS :].astype(jnp.float32)
+        norms += [tail[i : i + 1] + tail[i + 1 : i + 2] + tail[i + 2 : i + 3] for i in (0, 3)]
+    return norms
+
+
+def norm_column(refs, rows):
+    return jnp.concatenate([column(norm, 0, rows) for norm in read_norms(refs)], axis=0)
+
+
+def norm_row(refs, rows):
+    norms, per_row = read_norms(refs), LANES // rows
+    lane = lax.broadcasted_iota(jnp.int32, (1, LANES), 1)
+    pieces = []
+    for start in range(0, len(norms), per_row):
+        piece = norms[start]
+        for i, norm in enumerate(norms[start + 1 : start + per_row], 1):
+            piece = jnp.where(lane >= i * rows, pltpu.roll(norm, i * rows, 1), piece)
+        pieces.append(piece)
+    return jnp.concatenate(pieces, axis=1)[:, : len(norms) * rows]
 
 
 def pack_kernel(
@@ -126,81 +143,116 @@
     )
 
 
-def row_numbers(plan, slab, blk, role, rows, place):
+def row_numbers(plan, slab, blk, role, rows, steps, place):
     chip = slab >> 1
     number = place
-    for step in range(plan.group_size):
+    for i, step in enumerate(steps):
         for other in (0, 1):
             core = role ^ other
             p_shard = blk * (2 * plan.chip_count) + 2 * peer(chip, step, plan.chip_count) + core
             q_shard = (2 * chip + core) * plan.blk_count + peer(blk, step, plan.blk_count)
             p_base = p_shard * rows if step < plan.chip_count else -(1 << 24)
             q_base = q_shard * rows if step < plan.blk_count else -(1 << 25)
-            start = (2 * step + other) * rows
+            start = (2 * i + other) * rows
             base = jnp.where(role == 0, p_base, q_base) - start
             number = jnp.where(place >= start, place + base, number)
     return number
 
 
-def tile_kernel(plan, rows, slab_ref, blk_ref, loss_ref, *refs):
-    count = plan.group_size
-    a_refs, b_refs, out_refs = refs[:count], refs[count : 2 * count], refs[2 * count :]
-    a, a_norm = (jnp.concatenate(x, axis=0) for x in zip(*(read_block(r, rows) for r in a_refs)))
-    b, b_norm = (jnp.concatenate(x, axis=0) for x in zip(*(read_block(r, rows) for r in b_refs)))
-    b_norm = as_row(b_norm, b_norm.shape[0])
+def gradient(plan, rows, scalars, a_steps, a_refs, a_norm, b_steps, b_refs):
+    slab, blk = (ref[0] for ref in scalars)
+    a, b = read_rows(a_refs, rows), read_rows(b_refs, rows)
     scale = 2.0 / math.sqrt(a.shape[1])
     scores = scale * lax.dot_general(
         a, b, (((1,), (1,)), ((), ())), preferred_element_type=jnp.float32
     )
-    slab, blk = slab_ref[0], blk_ref[0]
     role = slab & 1
     numbers = functools.partial(row_numbers, plan, slab, blk, rows=rows)
-    a_number = numbers(role, place=lax.broadcasted_iota(jnp.int32, (a.shape[0], 1), 0))
-    b_number = numbers(1 - role, place=lax.broadcasted_iota(jnp.int32, (1, b.shape[0]), 1))
-    paired = (a_number == b_number).astype(jnp.float32)
-    weights = (0.5 * loss_ref[0]) * (
-        jnp.exp(scores - a_norm) + jnp.exp(scores - b_norm) - 2.0 * paired
+    a_place = lax.broadcasted_iota(jnp.int32, (a.shape[0], 1), 0)
+    b_place = lax.broadcasted_iota(jnp.int32, (1, b.shape[0]), 1)
+    a_number = numbers(role, steps=a_steps, place=a_place)
+    b_number = numbers(1 - role, steps=b_steps, place=b_place)
+    weights = (0.5 * scale) * (
+        jnp.exp(scores - a_norm)
+        + jnp.exp(scores - norm_row(b_refs, rows))
+        - 2.0 * (a_number == b_number).astype(jnp.float32)
     )
     high = weights.astype(jnp.bfloat16)
     low = (weights - high.astype(jnp.float32)).astype(jnp.bfloat16)
-    total = jnp.dot(high, b, preferred_element_type=jnp.float32) + jnp.dot(
-        low, b, preferred_element_type=jnp.float32
-    )
-    total = scale * total
-    out_refs[0][...] = total[: 2 * rows]
-    for i in range(1, count):
-        write_partial(out_refs[i], total[2 * rows * i : 2 * rows * (i + 1)])
+    return jnp.dot(
+        jnp.concatenate([high, low], axis=1),
+        jnp.concatenate([b, b], axis=0),
+        preferred_element_type=jnp.float32,
+    )
+
+
+def early_kernel(plan, rows, a_steps, b_steps, *refs):
+    scalars, refs, (out_ref, norm_ref) = refs[:2], refs[2:-2], refs[-2:]
+    a_refs, b_refs = refs[: len(a_steps)], refs[len(a_steps) :]
+    a_norm = norm_column(a_refs, rows)
+    out_ref[...] = gradient(plan, rows, scalars, a_steps, a_refs, a_norm, b_steps, b_refs)
+    norm_ref[...] = jnp.broadcast_to(a_norm, norm_ref.shape)
+
+
+def late_kernel(plan, rows, a_steps, b_steps, *refs):
+    scalars, (early_ref, norm_ref), refs = refs[:2], refs[2:4], refs[4:]
+    n = len(a_steps)
+    a_refs, b_refs, out_refs = refs[:n], refs[n : n + len(b_steps)], refs[n + len(b_steps) :]
+    total = early_ref[...] + gradient(
+        plan, rows, scalars, a_steps, a_refs, norm_ref[:, 0:1], b_steps, b_refs
+    )
+    for i, out_ref in enumerate(out_refs):
+        write_partial(out_ref, total[2 * rows * i : 2 * rows * (i + 1)])
+
+
+def own_kernel(plan, rows, steps, *refs):
+    scalars, loss_ref, refs, (out_ref, size_ref) = refs[:2], refs[2], refs[3:-2], refs[-2:]
+    a_refs, b_refs = refs[:1], refs[1:]
+    a_norm = norm_column(a_refs, rows)
+    size_ref[...] = jnp.full(size_ref.shape, loss_ref[0], jnp.float32)
+    out_ref[...] = gradient(plan, rows, scalars, steps[:1], a_refs, a_norm, steps, b_refs)
+
+
+def tiles(block):
+    rows, width = block.shape
+    return [
+        block[:, i : i + LANES].reshape(rows // SIZE_ROWS, SIZE_ROWS, LANES)
+        for i in range(0, width, LANES)
+    ]
 
 
 def write_partial(ref, block):
-    rows, width = block.shape
-    largest = jnp.maximum(jnp.max(jnp.abs(block), keepdims=True), 1e-30)
-    power = jnp.ceil(jnp.log2(largest)) - 10.0
-    block = block * jnp.exp2(-power)
-    for chunk in range(width // LANES):
-        ref[chunk * rows : (chunk + 1) * rows] = block[:, chunk * LANES : (chunk + 1) * LANES]
-    ref[rows * (width // LANES) :] = jnp.broadcast_to(power, (SIZE_ROWS, LANES))
-
-
-def sum_kernel(own_ref, *refs):
+    rows = block.shape[0]
+    chunks = tiles(block)
+    largest = functools.reduce(
+        jnp.maximum, [jnp.max(jnp.abs(chunk), axis=0, keepdims=True) for chunk in chunks]
+    )
+    power = jnp.ceil(jnp.log2(jnp.maximum(largest, 1e-30))) - 10.0
+    factor = jnp.exp2(-power)
+    for i, chunk in enumerate(chunks):
+        ref[i * rows : (i + 1) * rows] = (chunk * factor).reshape(rows, LANES)
+    ref[len(chunks) * rows :] = power[0]
+
+
+def sum_kernel(loss_ref, own_ref, *refs):
     partial_refs, (keep_ref, give_ref) = refs[:-2], refs[-2:]
     rows, width = own_ref.shape
     tail = rows * (width // LANES)
-    factors = [jnp.exp2(ref[tail : tail + 1]) for ref in partial_refs]
-    for chunk in range(width // LANES):
-        lanes = slice(chunk * LANES, (chunk + 1) * LANES)
-        total = own_ref[:, lanes]
+    loss = loss_ref[...]
+    factors = [jnp.exp2(ref[tail:])[None] for ref in partial_refs]
+    for i, total in enumerate(tiles(own_ref[...])):
         for ref, factor in zip(partial_refs, factors):
-            total = total + ref[chunk * rows : (chunk + 1) * rows] * factor
-        keep_ref[:, lanes] = total[: rows // 2]
-        give_ref[:, lanes] = total[rows // 2 :]
+            total = total + tiles(ref[i * rows : (i + 1) * rows])[0] * factor
+        total = (total * loss[None]).reshape(rows, LANES)
+        keep_ref[:, i * LANES : (i + 1) * LANES] = total[: rows // 2]
+        give_ref[:, i * LANES : (i + 1) * LANES] = total[rows // 2 :]
 
 
 VMEM = pl.BlockSpec(memory_space=pltpu.VMEM)
 SMEM = pl.BlockSpec(memory_space=pltpu.SMEM)
 
 
-def call(kernel, name, scalars, arrays, out_shape, mebibytes):
+def call(kernel, name, scalars, arrays, out_shape, mebibytes, flops=0):
     return pl.pallas_call(
         kernel,
         out_shape=out_shape,
@@ -208,6 +260,7 @@
         out_specs=[VMEM] * len(out_shape),
         name=name,
         compiler_params=pltpu.CompilerParams(vmem_limit_bytes=mebibytes * 1024 * 1024),
+        cost_estimate=pl.CostEstimate(flops=flops, bytes_accessed=0, transcendentals=0),
     )(*(x.reshape(1) for x in scalars), *arrays)
 
 
@@ -245,23 +298,51 @@
         a_parts.append(lax.ppermute(mine, AXES, back))
         b_parts.append(swapped(a_parts[-1]))
 
-    whole = jax.ShapeDtypeStruct((2 * rows, width), jnp.float32)
+    scalars = (slab, blk)
+    steps = list(range(count))
+    last = steps[1:3]
+    soon = [i for i in steps if i not in last]
+    a_others = a_parts[1:]
+    other_rows = 2 * rows * (count - 1)
+    early = call(
+        functools.partial(early_kernel, plan, rows, steps[1:], soon),
+        "early",
+        scalars,
+        (*a_others, *(b_parts[i] for i in soon)),
+        [
+            jax.ShapeDtypeStruct((other_rows, width), jnp.float32),
+            jax.ShapeDtypeStruct((other_rows, LANES), jnp.float32),
+        ],
+        3 * count,
+        flops=10**9,
+    )
+    partials = call(
+        functools.partial(late_kernel, plan, rows, steps[1:], last),
+        "late",
+        scalars,
+        (*early, *a_others, *(b_parts[i] for i in last)),
+        [jax.ShapeDtypeStruct((chunk_rows + SIZE_ROWS, LANES), jnp.float32)] * (count - 1),
+        3 * count,
+    )
+    own, loss = call(
+        functools.partial(own_kernel, plan, rows, steps),
+        "own",
+        (*scalars, loss_cotangent),
+        (mine, *b_parts),
+        [
+            jax.ShapeDtypeStruct((2 * rows, width), jnp.float32),
+            jax.ShapeDtypeStruct((SIZE_ROWS, LANES), jnp.float32),
+        ],
+        3 * count,
+        flops=10**9,
+    )
     half = jax.ShapeDtypeStruct((rows, width), jnp.float32)
-    partial = jax.ShapeDtypeStruct((chunk_rows + SIZE_ROWS, LANES), jnp.float32)
-    own, *partials = call(
-        functools.partial(tile_kernel, plan, rows),
-        "tile",
-        (slab, blk, loss_cotangent),
-        (*a_parts, *b_parts),
-        [whole] + [partial] * (count - 1),
-        3 * count,
-    )
 
     arrived = [
         lax.ppermute(x.astype(jnp.float16), AXES, plan.group_pairs(1 + i)).astype(jnp.float32)
         for i, x in enumerate(partials)
     ]
-    keep, give = call(sum_kernel, "sum", (), (own, *arrived), [half, half], 2 * count)
+    keep, give = call(sum_kernel, "sum", (), (loss, own, *arrived), [half, half], 2 * count)
     got = swapped(give)
     return jnp.where(core == 1, keep, got), jnp.where(core == 1, got, keep)
 

time: 24.8 us -> 24.4 us (0.984)
  waiting for transfers between devices: 9.58 us -> 8.36 us
  Pallas kernels: 1.22 us -> 2 us
    ppermute x3, waiting for transfers between devices: 4.06 us -> 2.73 us  [local(): lax.ppermute(x.astype(jnp.float16), AXES, plan.group_pairs(1 + i))]
    pallas_call x3 -> x5, Pallas kernels: 1.22 us -> 2 us  [call(): pl.pallas_call(kernel, out_shape=out_shape, in_specs=[SMEM] * len(scalars...]
  transfers between devices with their start and end apart: 13 -> 13, of which waited for: 9 -> 9; matrix products, arithmetic and copies ran while one was open for 4% -> 4% of each run, Pallas kernels for 0% -> 5%
where the time goes in v4:
time: 24.4 us; the launch traced here: 24.2 us
  starting transfers between devices  10.8 us (44%)
  waiting for transfers between devices  8.36 us (34%)
  Pallas kernels  2 us (8%)
  other arithmetic  1.72 us (7%)
  between operations  1.38 us (6%)
    ppermute x3, starting transfers between devices, local(): a_parts.append(lax.ppermute(mine, AXES, back))  4.5 us
    ppermute x3, starting transfers between devices, local(): lax.ppermute(x.astype(jnp.float16), AXES, plan.group_pairs(1 + i))  3.62 us
    ppermute x3, waiting for transfers between devices, local(): a_parts.append(lax.ppermute(mine, AXES, back))  3.47 us
    ppermute x3, waiting for transfers between devices, local(): lax.ppermute(x.astype(jnp.float16), AXES, plan.group_pairs(1 + i))  2.73 us
    ppermute x7, starting transfers between devices, swapped(): return lax.ppermute(block, AXES, plan.core_pairs())  2.64 us
    ppermute x7, waiting for transfers between devices, swapped(): return lax.ppermute(block, AXES, plan.core_pairs())  2.16 us
    pallas_call x5, Pallas kernels, call(): pl.pallas_call(kernel, out_shape=out_shape, in_specs=[SMEM] * len(scalars...  2 us
    select_n x1, other arithmetic, local(): jnp.where(core == 1, passages, queries)  0.86 us
  transfers between devices with their start and end apart: 13, of which 9 were waited for; matrix products, arithmetic and copies ran while one was open for 4% of the time, Pallas kernels for 5%

profile of v4, /device:TPU:0, one launch (start us, length us, event | category | flops | bytes accessed | tf_op | source)
XLA Modules:
  0.0 24.2 jit_solution(2103221095826034273)
XLA Ops:
  0.6 0.5 %collective-permute-start.2 = (f32[32]{0:T(128)}, f32[32]{0:T(128)S(1)}, u32[]{:S(2)}, u32[]{:S(2)}) collective-permute-start(f32[32]{0:T(128)} %param.7), channel_id=1, source_target_pairs={{0,4},{4,0},{1,5},{5,1},{2,6},{6,2},{3,7},{7,3},{8,12},{12,8},{9,1... | collective-permute-start | bytes 392 | tf_op jit(solution)/shard_map/ppermute | solution.py:276
  1.1 0.1 collective-permute-start
  1.2 0.4 %collective-permute-start.1 = (bf16[32,768]{1,0:T(8,128)(2,1)}, bf16[32,768]{1,0:T(8,128)(2,1)S(1)}, u32[]{:S(2)}, u32[]{:S(2)}) collective-permute-start(bf16[32,768]{1,0:T(8,128)(2,1)} %param.6), channel_id=1, source_target_pairs={{0,4},{4,0},{1,5},{5,1},{2,6},{6,2},{3,7},{7,3},{8,12},{12,8},{9,1... | collective-permute-start | bytes 147464 | tf_op jit(solution)/shard_map/ppermute | solution.py:276
  1.7 0.0 copy-start
  1.7 0.0 copy-start.1
  1.7 0.9 %broadcast_select_fusion.2 = (bf16[32,768]{1,0:T(8,128)(2,1)S(1)}, bf16[32,768]{1,0:T(8,128)(2,1)S(1)}) fusion(bf16[32,768]{1,0:T(8,128)(2,1)} %param.6, bf16[32,768]{1,0:T(8,128)(2,1)} %param.5, pred[]{:T(512)S(6)} %eq.2), kind=kLoop, calls=%fused_computation.2 | loop fusion | flops 49152 | bytes 196609 | tf_op jit(solution)/shard_map/jit(_where)/select_n | solution.py:285
  2.5 0.0 copy-done
  2.5 0.0 copy-done.1
  2.5 0.1 pad_maximum_fusion
  2.6 0.0 collective-permute-done.2
  2.6 0.0 collective-permute-done.got_q_ref
  2.6 0.1 collective-permute-done.1.got_p_ref
  2.8 0.1 pack.1
  2.9 3.9 %collective-permute-start.7 = (bf16[400,128]{1,0:T(8,128)(2,1)S(1)}, bf16[400,128]{1,0:T(8,128)(2,1)S(1)}, u32[]{:S(2)}, u32[]{:S(2)}) collective-permute-start(bf16[400,128]{1,0:T(8,128)(2,1)S(1)} %get-tuple-element.13.refs_3_), channel_id=1, source_target_pairs={{24,0},{7,4},{25,1},{6,5},{26,2},{5,6},{27,3},{4,7},{16,8},{15,12}... | collective-permute-start | bytes 307208 | tf_op jit(solution)/shard_map/ppermute | solution.py:298
  6.7 0.5 %collective-permute-start.5 = (bf16[400,128]{1,0:T(8,128)(2,1)S(1)}, bf16[400,128]{1,0:T(8,128)(2,1)S(1)}, u32[]{:S(2)}, u32[]{:S(2)}) collective-permute-start(bf16[400,128]{1,0:T(8,128)(2,1)S(1)} %get-tuple-element.13.refs_3_), channel_id=1, source_target_pairs={{16,0},{6,4},{17,1},{7,5},{18,2},{4,6},{19,3},{5,7},{24,8},{14,12}... | collective-permute-start | bytes 307208 | tf_op jit(solution)/shard_map/ppermute | solution.py:298
  7.3 0.1 collective-permute-start.3
  7.4 2.0 %collective-permute-done.7.refs_4_.refs_6_ = bf16[400,128]{1,0:T(8,128)(2,1)S(1)} collective-permute-done((bf16[400,128]{1,0:T(8,128)(2,1)S(1)}, bf16[400,128]{1,0:T(8,128)(2,1)S(1)}, u32[]{:S(2)}, u32[]{:S(2)}) %collective-permute-start.7) | collective-permute-done | bytes 102432 | tf_op jit(solution)/shard_map/ppermute | solution.py:298
  9.4 0.6 %collective-permute-start.8 = (bf16[400,128]{1,0:T(8,128)(2,1)S(1)}, bf16[400,128]{1,0:T(8,128)(2,1)S(1)}, u32[]{:S(2)}, u32[]{:S(2)}) collective-permute-start(bf16[400,128]{1,0:T(8,128)(2,1)S(1)} %collective-permute-done.7.refs_4_.refs_6_), channel_id=1, source_target_pairs={{0,4},{4,0},{1,5},{5,1},{2,6},{6,2},{3,7},{7,3},{8,12},{12,8},{9,1... | collective-permute-start | bytes 307208 | tf_op jit(solution)/shard_map/ppermute | solution.py:276
  9.9 1.5 %collective-permute-done.5.refs_3_.refs_5_ = bf16[400,128]{1,0:T(8,128)(2,1)S(1)} collective-permute-done((bf16[400,128]{1,0:T(8,128)(2,1)S(1)}, bf16[400,128]{1,0:T(8,128)(2,1)S(1)}, u32[]{:S(2)}, u32[]{:S(2)}) %collective-permute-start.5) | collective-permute-done | bytes 102432 | tf_op jit(solution)/shard_map/ppermute | solution.py:298
  11.4 1.0 %collective-permute-start.6 = (bf16[400,128]{1,0:T(8,128)(2,1)S(1)}, bf16[400,128]{1,0:T(8,128)(2,1)S(1)}, u32[]{:S(2)}, u32[]{:S(2)}) collective-permute-start(bf16[400,128]{1,0:T(8,128)(2,1)S(1)} %collective-permute-done.5.refs_3_.refs_5_), channel_id=1, source_target_pairs={{0,4},{4,0},{1,5},{5,1},{2,6},{6,2},{3,7},{7,3},{8,12},{12,8},{9,1... | collective-permute-start | bytes 307208 | tf_op jit(solution)/shard_map/ppermute | solution.py:276
  12.4 0.0 collective-permute-done.3.refs_2_.refs_4_
  12.4 0.0 collective-permute-start.4
  12.4 0.0 collective-permute-done.8.refs_7_.refs_6_
  12.4 0.5 %early.1 = (f32[192,768]{1,0:T(8,128)S(1)}, f32[192,128]{1,0:T(8,128)S(1)}) custom-call(s32[1]{0:T(128)} %bitcast.slab_ref.refs_0_, s32[1]{0:T(128)} %bitcast.1.refs_1_, bf16[400,128]{1,0:T(8,128)(2,1)S(1)} %collective-permute-done.3.refs_2_.refs_4_, bf16[400,128]{1,0:T(8,128)(2,1)S(1)} %collective-permute-done.5.refs_3_.refs_5_, ...), custom_call_target="tpu_custom_call" | custom-call | flops 1000000000 | tf_op jit(solution)/shard_map/early/pallas_call | solution.py:256
  12.9 0.4 %collective-permute-done.6.refs_6_.refs_8_ = bf16[400,128]{1,0:T(8,128)(2,1)S(1)} collective-permute-done((bf16[400,128]{1,0:T(8,128)(2,1)S(1)}, bf16[400,128]{1,0:T(8,128)(2,1)S(1)}, u32[]{:S(2)}, u32[]{:S(2)}) %collective-permute-start.6) | collective-permute-done | bytes 102432 | tf_op jit(solution)/shard_map/ppermute | solution.py:276
  13.3 0.4 %collective-permute-done.4.refs_5_.refs_7_ = bf16[400,128]{1,0:T(8,128)(2,1)S(1)} collective-permute-done((bf16[400,128]{1,0:T(8,128)(2,1)S(1)}, bf16[400,128]{1,0:T(8,128)(2,1)S(1)}, u32[]{:S(2)}, u32[]{:S(2)}) %collective-permute-start.4) | collective-permute-done | bytes 102432 | tf_op jit(solution)/shard_map/ppermute | solution.py:276
  13.7 0.6 %late.1 = (f32[392,128]{1,0:T(8,128)S(1)}, f32[392,128]{1,0:T(8,128)S(1)}, f32[392,128]{1,0:T(8,128)S(1)}) custom-call(s32[1]{0:T(128)} %bitcast.slab_ref.refs_0_, s32[1]{0:T(128)} %bitcast.1.refs_1_, f32[192,768]{1,0:T(8,128)S(1)} %get-tuple-element.17.refs_2_, f32[192,128]{1,0:T(8,128)S(1)} %get-tuple-element.18.refs_3_, ...), custom_call_target="tpu_custom_call" | custom-call | tf_op jit(solution)/shard_map/late/pallas_call | solution.py:256
  14.3 2.5 %collective-permute-start.11 = (f16[392,128]{1,0:T(8,128)(2,1)S(1)}, f16[392,128]{1,0:T(8,128)(2,1)S(1)}, u32[]{:S(2)}, u32[]{:S(2)}) collective-permute-start(f16[392,128]{1,0:T(8,128)(2,1)S(1)} %convert_element_type.22), channel_id=1, source_target_pairs={{0,24},{4,7},{1,25},{5,6},{2,26},{6,5},{3,27},{7,4},{8,16},{12,15}... | collective-permute-start | bytes 301064 | tf_op jit(solution)/shard_map/ppermute | solution.py:342
  16.8 0.5 %collective-permute-start.10 = (f16[392,128]{1,0:T(8,128)(2,1)S(1)}, f16[392,128]{1,0:T(8,128)(2,1)S(1)}, u32[]{:S(2)}, u32[]{:S(2)}) collective-permute-start(f16[392,128]{1,0:T(8,128)(2,1)S(1)} %convert_element_type.20), channel_id=1, source_target_pairs={{0,16},{4,6},{1,17},{5,7},{2,18},{6,4},{3,19},{7,5},{8,24},{12,14}... | collective-permute-start | bytes 301064 | tf_op jit(solution)/shard_map/ppermute | solution.py:342
  17.4 0.6 %collective-permute-start.9 = (f16[392,128]{1,0:T(8,128)(2,1)S(1)}, f16[392,128]{1,0:T(8,128)(2,1)S(1)}, u32[]{:S(2)}, u32[]{:S(2)}) collective-permute-start(f16[392,128]{1,0:T(8,128)(2,1)S(1)} %convert_element_type.18), channel_id=1, source_target_pairs={{0,8},{4,5},{1,9},{5,4},{2,10},{6,7},{3,11},{7,6},{8,0},{12,13},{9... | collective-permute-start | bytes 301064 | tf_op jit(solution)/shard_map/ppermute | solution.py:342
  18.6 0.7 %own.1 = (f32[64,768]{1,0:T(8,128)S(1)}, f32[8,128]{1,0:T(8,128)S(1)}) custom-call(s32[1]{0:T(128)} %bitcast.slab_ref.refs_0_, s32[1]{0:T(128)} %bitcast.1.refs_1_, f32[1]{0:T(128)} %bitcast.4.refs_2_, bf16[400,128]{1,0:T(8,128)(2,1)S(1)} %get-tuple-element.13.refs_3_, bf16[400,128]{1,0:T(8,128)(2,1)S(1)} %get-tuple-element.14.refs_4_.refs_5_, ...), custom_call_target="tpu_custom_call" | custom-call | flops 1000000000 | tf_op jit(solution)/shard_map/own/pallas_call | solution.py:256
  19.3 0.6 %collective-permute-done.11 = f16[392,128]{1,0:T(8,128)(2,1)S(1)} collective-permute-done((f16[392,128]{1,0:T(8,128)(2,1)S(1)}, f16[392,128]{1,0:T(8,128)(2,1)S(1)}, u32[]{:S(2)}, u32[]{:S(2)}) %collective-permute-start.11) | collective-permute-done | bytes 100384 | tf_op jit(solution)/shard_map/ppermute | solution.py:342
  19.9 1.5 %collective-permute-done.10 = f16[392,128]{1,0:T(8,128)(2,1)S(1)} collective-permute-done((f16[392,128]{1,0:T(8,128)(2,1)S(1)}, f16[392,128]{1,0:T(8,128)(2,1)S(1)}, u32[]{:S(2)}, u32[]{:S(2)}) %collective-permute-start.10) | collective-permute-done | bytes 100384 | tf_op jit(solution)/shard_map/ppermute | solution.py:342
  21.5 0.6 %collective-permute-done.9 = f16[392,128]{1,0:T(8,128)(2,1)S(1)} collective-permute-done((f16[392,128]{1,0:T(8,128)(2,1)S(1)}, f16[392,128]{1,0:T(8,128)(2,1)S(1)}, u32[]{:S(2)}, u32[]{:S(2)}) %collective-permute-start.9) | collective-permute-done | bytes 100384 | tf_op jit(solution)/shard_map/ppermute | solution.py:342
  22.1 0.1 sum.1
  22.2 0.1 collective-permute-start.12
  22.2 1.3 %collective-permute-done.12 = f32[32,768]{1,0:T(8,128)S(1)} collective-permute-done((f32[32,768]{1,0:T(8,128)S(1)}, f32[32,768]{1,0:T(8,128)S(1)}, u32[]{:S(2)}, u32[]{:S(2)}) %collective-permute-start.12) | collective-permute-done | bytes 98336 | tf_op jit(solution)/shard_map/ppermute | solution.py:276
  23.5 0.7 %broadcast_select_fusion = (f32[32,768]{1,0:T(8,128)}, f32[32,768]{1,0:T(8,128)}) fusion(f32[32,768]{1,0:T(8,128)S(1)} %collective-permute-done.12, f32[32,768]{1,0:T(8,128)S(1)} %get-tuple-element.22, pred[]{:T(512)S(6)} %eq.2), kind=kLoop, calls=%fused_computation | loop fusion | flops 49152 | bytes 393217 | tf_op jit(solution)/shard_map/jit(_where)/select_n | solution.py:347
  (7 shorter events, 0.1 us)
Async XLA Ops:
  0.6 2.0 %collective-permute-start.2 = (f32[32]{0:T(128)}, f32[32]{0:T(128)S(1)}, u32[]{:S(2)}, u32[]{:S(2)}) collective-permute-start(f32[32]{0:T(128)} %param.7), channel_id=1, source_target_pairs={{0,4},{4,0},{1,5},{5,1},{2,6},{6,2},{3,7},{7,3},{8,12},{12,8},{9,1... | collective-permute-start | bytes 392 | tf_op jit(solution)/shard_map/ppermute | solution.py:276
  1.1 1.5 %collective-permute-start = (bf16[32,768]{1,0:T(8,128)(2,1)}, bf16[32,768]{1,0:T(8,128)(2,1)S(1)}, u32[]{:S(2)}, u32[]{:S(2)}) collective-permute-start(bf16[32,768]{1,0:T(8,128)(2,1)} %param.5), channel_id=1, source_target_pairs={{0,4},{4,0},{1,5},{5,1},{2,6},{6,2},{3,7},{7,3},{8,12},{12,8},{9,1... | collective-permute-start | bytes 147464 | tf_op jit(solution)/shard_map/ppermute | solution.py:276
  1.2 1.5 %collective-permute-start.1 = (bf16[32,768]{1,0:T(8,128)(2,1)}, bf16[32,768]{1,0:T(8,128)(2,1)S(1)}, u32[]{:S(2)}, u32[]{:S(2)}) collective-permute-start(bf16[32,768]{1,0:T(8,128)(2,1)} %param.6), channel_id=1, source_target_pairs={{0,4},{4,0},{1,5},{5,1},{2,6},{6,2},{3,7},{7,3},{8,12},{12,8},{9,1... | collective-permute-start | bytes 147464 | tf_op jit(solution)/shard_map/ppermute | solution.py:276
  1.7 0.9 %copy-start = (f32[256]{0:T(256)S(1)}, f32[256]{0:T(256)}, u32[]{:S(2)}) copy-start(f32[256]{0:T(256)} %param.8) | copy-start | bytes 3076
  1.7 0.9 %copy-start.1 = (f32[32]{0:T(128)S(1)}, f32[32]{0:T(128)}, u32[]{:S(2)}) copy-start(f32[32]{0:T(128)} %param.7) | copy-start | bytes 388
  2.9 6.5 %collective-permute-start.7 = (bf16[400,128]{1,0:T(8,128)(2,1)S(1)}, bf16[400,128]{1,0:T(8,128)(2,1)S(1)}, u32[]{:S(2)}, u32[]{:S(2)}) collective-permute-start(bf16[400,128]{1,0:T(8,128)(2,1)S(1)} %get-tuple-element.13.refs_3_), channel_id=1, source_target_pairs={{24,0},{7,4},{25,1},{6,5},{26,2},{5,6},{27,3},{4,7},{16,8},{15,12}... | collective-permute-start | bytes 307208 | tf_op jit(solution)/shard_map/ppermute | solution.py:298
  6.7 4.7 %collective-permute-start.5 = (bf16[400,128]{1,0:T(8,128)(2,1)S(1)}, bf16[400,128]{1,0:T(8,128)(2,1)S(1)}, u32[]{:S(2)}, u32[]{:S(2)}) collective-permute-start(bf16[400,128]{1,0:T(8,128)(2,1)S(1)} %get-tuple-element.13.refs_3_), channel_id=1, source_target_pairs={{16,0},{6,4},{17,1},{7,5},{18,2},{4,6},{19,3},{5,7},{24,8},{14,12}... | collective-permute-start | bytes 307208 | tf_op jit(solution)/shard_map/ppermute | solution.py:298
  7.3 5.1 %collective-permute-start.3 = (bf16[400,128]{1,0:T(8,128)(2,1)S(1)}, bf16[400,128]{1,0:T(8,128)(2,1)S(1)}, u32[]{:S(2)}, u32[]{:S(2)}) collective-permute-start(bf16[400,128]{1,0:T(8,128)(2,1)S(1)} %get-tuple-element.13.refs_3_), channel_id=1, source_target_pairs={{8,0},{5,4},{9,1},{4,5},{10,2},{7,6},{11,3},{6,7},{0,8},{13,12},{1... | collective-permute-start | bytes 307208 | tf_op jit(solution)/shard_map/ppermute | solution.py:298
  9.4 3.0 %collective-permute-start.8 = (bf16[400,128]{1,0:T(8,128)(2,1)S(1)}, bf16[400,128]{1,0:T(8,128)(2,1)S(1)}, u32[]{:S(2)}, u32[]{:S(2)}) collective-permute-start(bf16[400,128]{1,0:T(8,128)(2,1)S(1)} %collective-permute-done.7.refs_4_.refs_6_), channel_id=1, source_target_pairs={{0,4},{4,0},{1,5},{5,1},{2,6},{6,2},{3,7},{7,3},{8,12},{12,8},{9,1... | collective-permute-start | bytes 307208 | tf_op jit(solution)/shard_map/ppermute | solution.py:276
  11.4 1.9 %collective-permute-start.6 = (bf16[400,128]{1,0:T(8,128)(2,1)S(1)}, bf16[400,128]{1,0:T(8,128)(2,1)S(1)}, u32[]{:S(2)}, u32[]{:S(2)}) collective-permute-start(bf16[400,128]{1,0:T(8,128)(2,1)S(1)} %collective-permute-done.5.refs_3_.refs_5_), channel_id=1, source_target_pairs={{0,4},{4,0},{1,5},{5,1},{2,6},{6,2},{3,7},{7,3},{8,12},{12,8},{9,1... | collective-permute-start | bytes 307208 | tf_op jit(solution)/shard_map/ppermute | solution.py:276
  12.4 1.3 %collective-permute-start.4 = (bf16[400,128]{1,0:T(8,128)(2,1)S(1)}, bf16[400,128]{1,0:T(8,128)(2,1)S(1)}, u32[]{:S(2)}, u32[]{:S(2)}) collective-permute-start(bf16[400,128]{1,0:T(8,128)(2,1)S(1)} %collective-permute-done.3.refs_2_.refs_4_), channel_id=1, source_target_pairs={{0,4},{4,0},{1,5},{5,1},{2,6},{6,2},{3,7},{7,3},{8,12},{12,8},{9,1... | collective-permute-start | bytes 307208 | tf_op jit(solution)/shard_map/ppermute | solution.py:276
  14.3 5.6 %collective-permute-start.11 = (f16[392,128]{1,0:T(8,128)(2,1)S(1)}, f16[392,128]{1,0:T(8,128)(2,1)S(1)}, u32[]{:S(2)}, u32[]{:S(2)}) collective-permute-start(f16[392,128]{1,0:T(8,128)(2,1)S(1)} %convert_element_type.22), channel_id=1, source_target_pairs={{0,24},{4,7},{1,25},{5,6},{2,26},{6,5},{3,27},{7,4},{8,16},{12,15}... | collective-permute-start | bytes 301064 | tf_op jit(solution)/shard_map/ppermute | solution.py:342
  16.8 4.6 %collective-permute-start.10 = (f16[392,128]{1,0:T(8,128)(2,1)S(1)}, f16[392,128]{1,0:T(8,128)(2,1)S(1)}, u32[]{:S(2)}, u32[]{:S(2)}) collective-permute-start(f16[392,128]{1,0:T(8,128)(2,1)S(1)} %convert_element_type.20), channel_id=1, source_target_pairs={{0,16},{4,6},{1,17},{5,7},{2,18},{6,4},{3,19},{7,5},{8,24},{12,14}... | collective-permute-start | bytes 301064 | tf_op jit(solution)/shard_map/ppermute | solution.py:342
  17.4 4.7 %collective-permute-start.9 = (f16[392,128]{1,0:T(8,128)(2,1)S(1)}, f16[392,128]{1,0:T(8,128)(2,1)S(1)}, u32[]{:S(2)}, u32[]{:S(2)}) collective-permute-start(f16[392,128]{1,0:T(8,128)(2,1)S(1)} %convert_element_type.18), channel_id=1, source_target_pairs={{0,8},{4,5},{1,9},{5,4},{2,10},{6,7},{3,11},{7,6},{8,0},{12,13},{9... | collective-permute-start | bytes 301064 | tf_op jit(solution)/shard_map/ppermute | solution.py:342
  22.2 1.4 %collective-permute-start.12 = (f32[32,768]{1,0:T(8,128)S(1)}, f32[32,768]{1,0:T(8,128)S(1)}, u32[]{:S(2)}, u32[]{:S(2)}) collective-permute-start(f32[32,768]{1,0:T(8,128)S(1)} %get-tuple-element.23), channel_id=1, source_target_pairs={{0,4},{4,0},{1,5},{5,1},{2,6},{6,2},{3,7},{7,3},{8,12},{12,8},{9,1... | collective-permute-start | bytes 294920 | tf_op jit(solution)/shard_map/ppermute | solution.py:276

commit v5 on v4

--- a/solution.py
+++ b/solution.py
@@ -11,6 +11,8 @@
 AXES = ("slab", "blk")
 LANES = 128
 NORM_ROWS = 16
+FIRST_STEPS = ((1, 3, 2), (2, 1, 3))
+PIECES = 1
 SIZE_ROWS = 8
 
 
@@ -25,6 +27,12 @@
         self.blk_count = blk_count
         self.chip_count = slab_count // 2
         self.group_size = max(self.chip_count, blk_count)
+
+    def step(self, role, turn):
+        steps = FIRST_STEPS[role]
+        if turn == 0 or self.group_size <= len(steps):
+            return turn
+        return steps[turn - 1] if turn <= len(steps) else turn
 
     def device(self, chip, core, blk):
         return (2 * chip + core) * self.blk_count + blk
@@ -41,15 +49,16 @@
             for core in (0, 1)
         ]
 
-    def group_pairs(self, step):
+    def group_pairs(self, turn, across=False):
         pairs = []
+        p_step, q_step = self.step(0, turn), self.step(1, turn)
         for chip, blk in self.each():
-            if step < self.chip_count:
-                other = peer(chip, step, self.chip_count)
-                pairs.append((self.device(chip, 0, blk), self.device(other, 0, blk)))
-            if step < self.blk_count:
-                other = peer(blk, step, self.blk_count)
-                pairs.append((self.device(chip, 1, blk), self.device(chip, 1, other)))
+            if p_step < self.chip_count:
+                other = peer(chip, p_step, self.chip_count)
+                pairs.append((self.device(chip, 0, blk), self.device(other, int(across), blk)))
+            if q_step < self.blk_count:
+                other = peer(blk, q_step, self.blk_count)
+                pairs.append((self.device(chip, 1, blk), self.device(chip, 1 - across, other)))
         return pairs
 
 
@@ -143,23 +152,24 @@
     )
 
 
-def row_numbers(plan, slab, blk, role, rows, steps, place):
+def row_numbers(plan, slab, blk, role, rows, turns, place):
     chip = slab >> 1
     number = place
-    for i, step in enumerate(steps):
+    for i, turn in enumerate(turns):
+        p_step, q_step = plan.step(0, turn), plan.step(1, turn)
         for other in (0, 1):
             core = role ^ other
-            p_shard = blk * (2 * plan.chip_count) + 2 * peer(chip, step, plan.chip_count) + core
-            q_shard = (2 * chip + core) * plan.blk_count + peer(blk, step, plan.blk_count)
-            p_base = p_shard * rows if step < plan.chip_count else -(1 << 24)
-            q_base = q_shard * rows if step < plan.blk_count else -(1 << 25)
+            p_shard = blk * (2 * plan.chip_count) + 2 * peer(chip, p_step, plan.chip_count) + core
+            q_shard = (2 * chip + core) * plan.blk_count + peer(blk, q_step, plan.blk_count)
+            p_base = p_shard * rows if p_step < plan.chip_count else -(1 << 24)
+            q_base = q_shard * rows if q_step < plan.blk_count else -(1 << 25)
             start = (2 * i + other) * rows
             base = jnp.where(role == 0, p_base, q_base) - start
             number = jnp.where(place >= start, place + base, number)
     return number
 
 
-def gradient(plan, rows, scalars, a_steps, a_refs, a_norm, b_steps, b_refs):
+def gradient(plan, rows, scalars, a_turns, a_refs, a_norm, b_turns, b_refs):
     slab, blk = (ref[0] for ref in scalars)
     a, b = read_rows(a_refs, rows), read_rows(b_refs, rows)
     scale = 2.0 / math.sqrt(a.shape[1])
@@ -170,8 +180,8 @@
     numbers = functools.partial(row_numbers, plan, slab, blk, rows=rows)
     a_place = lax.broadcasted_iota(jnp.int32, (a.shape[0], 1), 0)
     b_place = lax.broadcasted_iota(jnp.int32, (1, b.shape[0]), 1)
-    a_number = numbers(role, steps=a_steps, place=a_place)
-    b_number = numbers(1 - role, steps=b_steps, place=b_place)
+    a_number = numbers(role, turns=a_turns, place=a_place)
+    b_number = numbers(1 - role, turns=b_turns, place=b_place)
     weights = (0.5 * scale) * (
         jnp.exp(scores - a_norm)
         + jnp.exp(scores - norm_row(b_refs, rows))
@@ -186,31 +196,31 @@
     )
 
 
-def early_kernel(plan, rows, a_steps, b_steps, *refs):
-    scalars, refs, (out_ref, norm_ref) = refs[:2], refs[2:-2], refs[-2:]
-    a_refs, b_refs = refs[: len(a_steps)], refs[len(a_steps) :]
+def early_kernel(plan, rows, a_turns, b_turns, *refs):
+    scalars, refs, (out_ref, norm_ref) = refs[:2], refs[3:-2], refs[-2:]
+    a_refs, b_refs = refs[: len(a_turns)], refs[len(a_turns) :]
     a_norm = norm_column(a_refs, rows)
-    out_ref[...] = gradient(plan, rows, scalars, a_steps, a_refs, a_norm, b_steps, b_refs)
+    out_ref[...] = gradient(plan, rows, scalars, a_turns, a_refs, a_norm, b_turns, b_refs)
     norm_ref[...] = jnp.broadcast_to(a_norm, norm_ref.shape)
 
 
-def late_kernel(plan, rows, a_steps, b_steps, *refs):
+def late_kernel(plan, rows, a_turns, b_turns, *refs):
     scalars, (early_ref, norm_ref), refs = refs[:2], refs[2:4], refs[4:]
-    n = len(a_steps)
-    a_refs, b_refs, out_refs = refs[:n], refs[n : n + len(b_steps)], refs[n + len(b_steps) :]
+    n = len(a_turns)
+    a_refs, b_refs, out_refs = refs[:n], refs[n : n + len(b_turns)], refs[n + len(b_turns) :]
     total = early_ref[...] + gradient(
-        plan, rows, scalars, a_steps, a_refs, norm_ref[:, 0:1], b_steps, b_refs
-    )
-    for i, out_ref in enumerate(out_refs):
+        plan, rows, scalars, a_turns, a_refs, norm_ref[:, 0:1], b_turns, b_refs
+    )
+    write_partial(out_refs[0], total[:rows])
+    write_partial(out_refs[1], total[rows : 2 * rows])
+    for i, out_ref in enumerate(out_refs[2:], 1):
         write_partial(out_ref, total[2 * rows * i : 2 * rows * (i + 1)])
 
 
-def own_kernel(plan, rows, steps, *refs):
-    scalars, loss_ref, refs, (out_ref, size_ref) = refs[:2], refs[2], refs[3:-2], refs[-2:]
-    a_refs, b_refs = refs[:1], refs[1:]
+def own_kernel(plan, rows, turns, *refs):
+    scalars, a_refs, b_refs, out_ref = refs[:2], refs[2:3], refs[3:-1], refs[-1]
     a_norm = norm_column(a_refs, rows)
-    size_ref[...] = jnp.full(size_ref.shape, loss_ref[0], jnp.float32)
-    out_ref[...] = gradient(plan, rows, scalars, steps[:1], a_refs, a_norm, steps, b_refs)
+    out_ref[...] = gradient(plan, rows, scalars, turns[:1], a_refs, a_norm, turns, b_refs)
 
 
 def tiles(block):
@@ -234,18 +244,49 @@
     ref[len(chunks) * rows :] = power[0]
 
 
+def spread_kernel(value_ref, out_ref):
+    out_ref[...] = jnp.full(out_ref.shape, value_ref[0], jnp.float32)
+
+
 def sum_kernel(loss_ref, own_ref, *refs):
-    partial_refs, (keep_ref, give_ref) = refs[:-2], refs[-2:]
+    partial_refs, (keep_ref, *give_refs) = refs[: -1 - PIECES], refs[-1 - PIECES :]
     rows, width = own_ref.shape
     tail = rows * (width // LANES)
     loss = loss_ref[...]
     factors = [jnp.exp2(ref[tail:])[None] for ref in partial_refs]
+    gives = []
     for i, total in enumerate(tiles(own_ref[...])):
         for ref, factor in zip(partial_refs, factors):
             total = total + tiles(ref[i * rows : (i + 1) * rows])[0] * factor
         total = (total * loss[None]).reshape(rows, LANES)
         keep_ref[:, i * LANES : (i + 1) * LANES] = total[: rows // 2]
-        give_ref[:, i * LANES : (i + 1) * LANES] = total[rows // 2 :]
+        gives.append(total[rows // 2 :])
+    size = rows // 2 // PIECES
+    for i, give_ref in enumerate(give_refs):
+        write_partial(
+            give_ref, jnp.concatenate([give[i * size : (i + 1) * size] for give in gives], axis=1)
+        )
+
+
+def end_kernel(loss_ref, keep_ref, *refs):
+    got_refs, last_refs, (keep_out, got_out) = refs[:PIECES], refs[PIECES:-2], refs[-2:]
+    rows, width = keep_ref.shape
+    tail, size = rows * (width // LANES), rows // PIECES
+    loss = loss_ref[...]
+    factors = [(jnp.exp2(ref[tail:]) * loss)[None] for ref in last_refs]
+    got_factors = [jnp.exp2(ref[size * (width // LANES) :])[None] for ref in got_refs]
+    for i, keep in enumerate(tiles(keep_ref[...])):
+        lanes = slice(i * LANES, (i + 1) * LANES)
+        got = jnp.concatenate(
+            [
+                tiles(ref[i * size : (i + 1) * size])[0] * factor
+                for ref, factor in zip(got_refs, got_factors)
+            ],
+            axis=0,
+        )
+        for total, ref, factor, out_ref in zip((keep, got), last_refs, factors, (keep_out, got_out)):
+            total = total + tiles(ref[i * rows : (i + 1) * rows])[0] * factor
+            out_ref[:, lanes] = total.reshape(rows, LANES)
 
 
 VMEM = pl.BlockSpec(memory_space=pltpu.VMEM)
@@ -292,23 +333,33 @@
         4,
     )
 
+    (loss,) = call(
+        spread_kernel,
+        "spread",
+        (loss_cotangent,),
+        (),
+        [jax.ShapeDtypeStruct((SIZE_ROWS, LANES), jnp.float32)],
+        1,
+        flops=10**9,
+    )
+
     a_parts, b_parts = [mine], [others]
-    for step in range(1, count):
-        back = [(to, at) for at, to in plan.group_pairs(step)]
+    for turn in range(1, count):
+        back = [(to, at) for at, to in plan.group_pairs(turn)]
         a_parts.append(lax.ppermute(mine, AXES, back))
         b_parts.append(swapped(a_parts[-1]))
 
     scalars = (slab, blk)
-    steps = list(range(count))
-    last = steps[1:3]
-    soon = [i for i in steps if i not in last]
+    turns = list(range(count))
+    last = turns[1:3]
+    soon = [i for i in turns if i not in last]
     a_others = a_parts[1:]
     other_rows = 2 * rows * (count - 1)
     early = call(
-        functools.partial(early_kernel, plan, rows, steps[1:], soon),
+        functools.partial(early_kernel, plan, rows, turns[1:], soon),
         "early",
         scalars,
-        (*a_others, *(b_parts[i] for i in soon)),
+        (loss, *a_others, *(b_parts[i] for i in soon)),
         [
             jax.ShapeDtypeStruct((other_rows, width), jnp.float32),
             jax.ShapeDtypeStruct((other_rows, LANES), jnp.float32),
@@ -317,33 +368,37 @@
         flops=10**9,
     )
     partials = call(
-        functools.partial(late_kernel, plan, rows, steps[1:], last),
+        functools.partial(late_kernel, plan, rows, turns[1:], last),
         "late",
         scalars,
         (*early, *a_others, *(b_parts[i] for i in last)),
-        [jax.ShapeDtypeStruct((chunk_rows + SIZE_ROWS, LANES), jnp.float32)] * (count - 1),
+        [jax.ShapeDtypeStruct((chunk_rows // 2 + SIZE_ROWS, LANES), jnp.float32)] * 2
+        + [jax.ShapeDtypeStruct((chunk_rows + SIZE_ROWS, LANES), jnp.float32)] * (count - 2),
         3 * count,
     )
-    own, loss = call(
-        functools.partial(own_kernel, plan, rows, steps),
+    (own,) = call(
+        functools.partial(own_kernel, plan, rows, turns),
         "own",
-        (*scalars, loss_cotangent),
+        scalars,
         (mine, *b_parts),
-        [
-            jax.ShapeDtypeStruct((2 * rows, width), jnp.float32),
-            jax.ShapeDtypeStruct((SIZE_ROWS, LANES), jnp.float32),
-        ],
+        [jax.ShapeDtypeStruct((2 * rows, width), jnp.float32)],
         3 * count,
         flops=10**9,
     )
     half = jax.ShapeDtypeStruct((rows, width), jnp.float32)
 
-    arrived = [
-        lax.ppermute(x.astype(jnp.float16), AXES, plan.group_pairs(1 + i)).astype(jnp.float32)
-        for i, x in enumerate(partials)
-    ]
-    keep, give = call(sum_kernel, "sum", (), (loss, own, *arrived), [half, half], 2 * count)
-    got = swapped(give)
+    def crossed(partial, turn, across=False):
+        pairs = plan.group_pairs(turn, across)
+        return lax.ppermute(partial.astype(jnp.float16), AXES, pairs).astype(jnp.float32)
+
+    arrived = [crossed(x, turn) for turn, x in enumerate(partials[2:], 2)]
+    last = [crossed(partials[0], 1), crossed(partials[1], 1, True)]
+    piece = jax.ShapeDtypeStruct((chunk_rows // 2 // PIECES + SIZE_ROWS, LANES), jnp.float32)
+    keep, *gives = call(
+        sum_kernel, "sum", (), (loss, own, *arrived), [half] + [piece] * PIECES, 2 * count
+    )
+    gots = [swapped(give.astype(jnp.float16)).astype(jnp.float32) for give in gives]
+    keep, got = call(end_kernel, "end", (), (loss, keep, *gots, *last), [half, half], 4)
     return jnp.where(core == 1, keep, got), jnp.where(core == 1, got, keep)
 
 

time: 24.4 us -> 23.9 us (0.980)
  waiting for transfers between devices: 8.36 us -> 5.56 us
  starting transfers between devices: 10.8 us -> 12.9 us
    ppermute x3, waiting for transfers between devices: 3.47 us -> 1.89 us  [local(): a_parts.append(lax.ppermute(mine, AXES, back))]
    ppermute x3 -> x4, starting transfers between devices: 3.62 us -> 4.82 us  [crossed(): lax.ppermute(partial.astype(jnp.float16), AXES, pairs).astype(jnp.float32)]
    ppermute x7, waiting for transfers between devices: 2.16 us -> 1.18 us  [swapped(): return lax.ppermute(block, AXES, plan.core_pairs())]
    ppermute x7, starting transfers between devices: 2.64 us -> 3.59 us  [swapped(): return lax.ppermute(block, AXES, plan.core_pairs())]
    ppermute x3 -> x4, waiting for transfers between devices: 2.73 us -> 2.49 us  [crossed(): lax.ppermute(partial.astype(jnp.float16), AXES, pairs).astype(jnp.float32)]
    pallas_call x5 -> x7, Pallas kernels: 2 us -> 2.02 us  [call(): pl.pallas_call(kernel, out_shape=out_shape, in_specs=[SMEM] * len(scalars...]
  transfers between devices with their start and end apart: 13 -> 14, of which waited for: 9 -> 9; matrix products, arithmetic and copies ran while one was open for 4% -> 4% of each run, Pallas kernels for 5% -> 5%
where the time goes in v5:
time: 23.9 us; the launch traced here: 23.7 us
  starting transfers between devices  12.9 us (54%)
  waiting for transfers between devices  5.56 us (23%)
  Pallas kernels  2.02 us (8%)
  other arithmetic  1.75 us (7%)
  between operations  1.43 us (6%)
    ppermute x4, starting transfers between devices, crossed(): lax.ppermute(partial.astype(jnp.float16), AXES, pairs).astype(jnp.float32)  4.82 us
    ppermute x3, starting transfers between devices, local(): a_parts.append(lax.ppermute(mine, AXES, back))  4.47 us
    ppermute x7, starting transfers between devices, swapped(): return lax.ppermute(block, AXES, plan.core_pairs())  3.59 us
    ppermute x4, waiting for transfers between devices, crossed(): lax.ppermute(partial.astype(jnp.float16), AXES, pairs).astype(jnp.float32)  2.49 us
    pallas_call x7, Pallas kernels, call(): pl.pallas_call(kernel, out_shape=out_shape, in_specs=[SMEM] * len(scalars...  2.02 us
    ppermute x3, waiting for transfers between devices, local(): a_parts.append(lax.ppermute(mine, AXES, back))  1.89 us
    ppermute x7, waiting for transfers between devices, swapped(): return lax.ppermute(block, AXES, plan.core_pairs())  1.18 us
    select_n x1, other arithmetic, local(): jnp.where(core == 1, passages, queries)  0.86 us
  transfers between devices with their start and end apart: 14, of which 9 were waited for; matrix products, arithmetic and copies ran while one was open for 4% of the time, Pallas kernels for 5%

profile of v5, /device:TPU:0, one launch (start us, length us, event | category | flops | bytes accessed | tf_op | source)
XLA Modules:
  0.0 23.7 jit_solution(14334773659700657151)
XLA Ops:
  0.6 0.5 %collective-permute-start.2 = (f32[32]{0:T(128)}, f32[32]{0:T(128)S(1)}, u32[]{:S(2)}, u32[]{:S(2)}) collective-permute-start(f32[32]{0:T(128)} %param.7), channel_id=1, source_target_pairs={{0,4},{4,0},{1,5},{5,1},{2,6},{6,2},{3,7},{7,3},{8,12},{12,8},{9,1... | collective-permute-start | bytes 392 | tf_op jit(solution)/shard_map/ppermute | solution.py:317
  1.1 0.1 collective-permute-start
  1.2 0.4 %collective-permute-start.1 = (bf16[32,768]{1,0:T(8,128)(2,1)}, bf16[32,768]{1,0:T(8,128)(2,1)S(1)}, u32[]{:S(2)}, u32[]{:S(2)}) collective-permute-start(bf16[32,768]{1,0:T(8,128)(2,1)} %param.6), channel_id=1, source_target_pairs={{0,4},{4,0},{1,5},{5,1},{2,6},{6,2},{3,7},{7,3},{8,12},{12,8},{9,1... | collective-permute-start | bytes 147464 | tf_op jit(solution)/shard_map/ppermute | solution.py:317
  1.7 0.0 copy-start
  1.7 0.0 copy-start.1
  1.7 0.9 %broadcast_select_fusion.2 = (bf16[32,768]{1,0:T(8,128)(2,1)S(1)}, bf16[32,768]{1,0:T(8,128)(2,1)S(1)}) fusion(bf16[32,768]{1,0:T(8,128)(2,1)} %param.6, bf16[32,768]{1,0:T(8,128)(2,1)} %param.5, pred[]{:T(512)S(6)} %eq.2), kind=kLoop, calls=%fused_computation.2 | loop fusion | flops 49152 | bytes 196609 | tf_op jit(solution)/shard_map/jit(_where)/select_n | solution.py:326
  2.5 0.0 copy-done
  2.5 0.0 copy-done.1
  2.5 0.1 pad_maximum_fusion
  2.6 0.0 collective-permute-done.2
  2.6 0.0 collective-permute-done.got_q_ref
  2.6 0.1 collective-permute-done.1.got_p_ref
  2.8 0.1 pack.1
  2.9 2.9 %collective-permute-start.7 = (bf16[400,128]{1,0:T(8,128)(2,1)S(1)}, bf16[400,128]{1,0:T(8,128)(2,1)S(1)}, u32[]{:S(2)}, u32[]{:S(2)}) collective-permute-start(bf16[400,128]{1,0:T(8,128)(2,1)S(1)} %get-tuple-element.14.refs_2_), channel_id=1, source_target_pairs={{16,0},{7,4},{17,1},{6,5},{18,2},{5,6},{19,3},{4,7},{24,8},{15,12}... | collective-permute-start | bytes 307208 | tf_op jit(solution)/shard_map/ppermute | solution.py:349
  5.8 1.4 %collective-permute-start.5 = (bf16[400,128]{1,0:T(8,128)(2,1)S(1)}, bf16[400,128]{1,0:T(8,128)(2,1)S(1)}, u32[]{:S(2)}, u32[]{:S(2)}) collective-permute-start(bf16[400,128]{1,0:T(8,128)(2,1)S(1)} %get-tuple-element.14.refs_2_), channel_id=1, source_target_pairs={{24,0},{5,4},{25,1},{4,5},{26,2},{7,6},{27,3},{6,7},{16,8},{13,12}... | collective-permute-start | bytes 307208 | tf_op jit(solution)/shard_map/ppermute | solution.py:349
  7.3 0.1 collective-permute-start.3
  7.4 1.1 %collective-permute-done.7.refs_5_.refs_6_ = bf16[400,128]{1,0:T(8,128)(2,1)S(1)} collective-permute-done((bf16[400,128]{1,0:T(8,128)(2,1)S(1)}, bf16[400,128]{1,0:T(8,128)(2,1)S(1)}, u32[]{:S(2)}, u32[]{:S(2)}) %collective-permute-start.7) | collective-permute-done | bytes 102432 | tf_op jit(solution)/shard_map/ppermute | solution.py:349
  8.5 1.5 %collective-permute-start.8 = (bf16[400,128]{1,0:T(8,128)(2,1)S(1)}, bf16[400,128]{1,0:T(8,128)(2,1)S(1)}, u32[]{:S(2)}, u32[]{:S(2)}) collective-permute-start(bf16[400,128]{1,0:T(8,128)(2,1)S(1)} %collective-permute-done.7.refs_5_.refs_6_), channel_id=1, source_target_pairs={{0,4},{4,0},{1,5},{5,1},{2,6},{6,2},{3,7},{7,3},{8,12},{12,8},{9,1... | collective-permute-start | bytes 307208 | tf_op jit(solution)/shard_map/ppermute | solution.py:317
  10.6 0.8 %collective-permute-done.5.refs_4_.refs_5_ = bf16[400,128]{1,0:T(8,128)(2,1)S(1)} collective-permute-done((bf16[400,128]{1,0:T(8,128)(2,1)S(1)}, bf16[400,128]{1,0:T(8,128)(2,1)S(1)}, u32[]{:S(2)}, u32[]{:S(2)}) %collective-permute-start.5) | collective-permute-done | bytes 102432 | tf_op jit(solution)/shard_map/ppermute | solution.py:349
  11.4 1.0 %collective-permute-start.6 = (bf16[400,128]{1,0:T(8,128)(2,1)S(1)}, bf16[400,128]{1,0:T(8,128)(2,1)S(1)}, u32[]{:S(2)}, u32[]{:S(2)}) collective-permute-start(bf16[400,128]{1,0:T(8,128)(2,1)S(1)} %collective-permute-done.5.refs_4_.refs_5_), channel_id=1, source_target_pairs={{0,4},{4,0},{1,5},{5,1},{2,6},{6,2},{3,7},{7,3},{8,12},{12,8},{9,1... | collective-permute-start | bytes 307208 | tf_op jit(solution)/shard_map/ppermute | solution.py:317
  12.4 0.0 collective-permute-done.3.refs_3_.refs_4_
  12.4 0.0 collective-permute-start.4
  12.4 0.0 collective-permute-done.8.refs_6_.refs_7_
  12.4 0.5 %early.1 = (f32[192,768]{1,0:T(8,128)S(1)}, f32[192,128]{1,0:T(8,128)S(1)}) custom-call(s32[1]{0:T(128)} %bitcast.1.slab_ref.refs_0_, s32[1]{0:T(128)} %bitcast.2.refs_1_, f32[8,128]{1,0:T(8,128)S(1)} %spread.1.refs_2_.loss_ref, bf16[400,128]{1,0:T(8,128)(2,1)S(1)} %collective-permute-done.3.refs_3_.refs_4_, ...), custom_call_target="tpu_custom_call" | custom-call | flops 1000000000 | tf_op jit(solution)/shard_map/early/pallas_call | solution.py:297
  13.0 0.4 %collective-permute-done.6.refs_5_.refs_8_ = bf16[400,128]{1,0:T(8,128)(2,1)S(1)} collective-permute-done((bf16[400,128]{1,0:T(8,128)(2,1)S(1)}, bf16[400,128]{1,0:T(8,128)(2,1)S(1)}, u32[]{:S(2)}, u32[]{:S(2)}) %collective-permute-start.6) | collective-permute-done | bytes 102432 | tf_op jit(solution)/shard_map/ppermute | solution.py:317
  13.3 0.4 %collective-permute-done.4.refs_4_.refs_7_ = bf16[400,128]{1,0:T(8,128)(2,1)S(1)} collective-permute-done((bf16[400,128]{1,0:T(8,128)(2,1)S(1)}, bf16[400,128]{1,0:T(8,128)(2,1)S(1)}, u32[]{:S(2)}, u32[]{:S(2)}) %collective-permute-start.4) | collective-permute-done | bytes 102432 | tf_op jit(solution)/shard_map/ppermute | solution.py:317
  13.7 0.6 %late.1 = (f32[200,128]{1,0:T(8,128)S(1)}, f32[200,128]{1,0:T(8,128)S(1)}, f32[392,128]{1,0:T(8,128)S(1)}, f32[392,128]{1,0:T(8,128)S(1)}) custom-call(s32[1]{0:T(128)} %bitcast.1.slab_ref.refs_0_, s32[1]{0:T(128)} %bitcast.2.refs_1_, f32[192,768]{1,0:T(8,128)S(1)} %get-tuple-element.16.refs_2_, f32[192,128]{1,0:T(8,128)S(1)} %get-tuple-element.17.refs_3_, ...), custom_call_target="tpu_custom_call" | custom-call | tf_op jit(solution)/shard_map/late/pallas_call | solution.py:297
  14.3 1.6 %collective-permute-start.10 = (f16[392,128]{1,0:T(8,128)(2,1)S(1)}, f16[392,128]{1,0:T(8,128)(2,1)S(1)}, u32[]{:S(2)}, u32[]{:S(2)}) collective-permute-start(f16[392,128]{1,0:T(8,128)(2,1)S(1)} %convert_element_type.32), channel_id=1, source_target_pairs={{0,16},{4,7},{1,17},{5,6},{2,18},{6,5},{3,19},{7,4},{8,24},{12,15}... | collective-permute-start | bytes 301064 | tf_op jit(solution)/shard_map/ppermute | solution.py:392
  15.9 1.5 %collective-permute-start.9 = (f16[392,128]{1,0:T(8,128)(2,1)S(1)}, f16[392,128]{1,0:T(8,128)(2,1)S(1)}, u32[]{:S(2)}, u32[]{:S(2)}) collective-permute-start(f16[392,128]{1,0:T(8,128)(2,1)S(1)} %convert_element_type.30), channel_id=1, source_target_pairs={{0,24},{4,5},{1,25},{5,4},{2,26},{6,7},{3,27},{7,6},{8,16},{12,13}... | collective-permute-start | bytes 301064 | tf_op jit(solution)/shard_map/ppermute | solution.py:392
  17.4 1.0 %collective-permute-start.13 = (f16[200,128]{1,0:T(8,128)(2,1)S(1)}, f16[200,128]{1,0:T(8,128)(2,1)S(1)}, u32[]{:S(2)}, u32[]{:S(2)}) collective-permute-start(f16[200,128]{1,0:T(8,128)(2,1)S(1)} %convert_element_type.38), channel_id=1, source_target_pairs={{0,12},{4,2},{1,13},{5,3},{2,14},{6,0},{3,15},{7,1},{8,4},{12,10},... | collective-permute-start | bytes 153608 | tf_op jit(solution)/shard_map/ppermute | solution.py:392
  18.5 0.7 %collective-permute-start.12 = (f16[200,128]{1,0:T(8,128)(2,1)S(1)}, f16[200,128]{1,0:T(8,128)(2,1)S(1)}, u32[]{:S(2)}, u32[]{:S(2)}) collective-permute-start(f16[200,128]{1,0:T(8,128)(2,1)S(1)} %convert_element_type.36), channel_id=1, source_target_pairs={{0,8},{4,6},{1,9},{5,7},{2,10},{6,4},{3,11},{7,5},{8,0},{12,14},{9... | collective-permute-start | bytes 153608 | tf_op jit(solution)/shard_map/ppermute | solution.py:392
  19.2 0.7 %own.1.own_ref = f32[64,768]{1,0:T(8,128)S(1)} custom-call(s32[1]{0:T(128)} %bitcast.1.slab_ref.refs_0_, s32[1]{0:T(128)} %bitcast.2.refs_1_, bf16[400,128]{1,0:T(8,128)(2,1)S(1)} %get-tuple-element.14.refs_2_, bf16[400,128]{1,0:T(8,128)(2,1)S(1)} %get-tuple-element.15.refs_3_.refs_6_, bf16[400,128]{1,0:T(8,128)(2,1)S(1)} %collective-permute-done.4.refs_4_.refs_7_, ...), custom_call_target="tpu_custom_call" | custom-call | flops 1000000000 | tf_op jit(solution)/shard_map/own/pallas_call | solution.py:297
  19.9 0.0 collective-permute-done.10
  19.9 1.6 %collective-permute-done.9 = f16[392,128]{1,0:T(8,128)(2,1)S(1)} collective-permute-done((f16[392,128]{1,0:T(8,128)(2,1)S(1)}, f16[392,128]{1,0:T(8,128)(2,1)S(1)}, u32[]{:S(2)}, u32[]{:S(2)}) %collective-permute-start.9) | collective-permute-done | bytes 100384 | tf_op jit(solution)/shard_map/ppermute | solution.py:392
  21.5 0.1 sum.1
  21.6 0.1 collective-permute-start.11
  21.7 0.2 collective-permute-done.13
  21.9 0.6 %collective-permute-done.12 = f16[200,128]{1,0:T(8,128)(2,1)S(1)} collective-permute-done((f16[200,128]{1,0:T(8,128)(2,1)S(1)}, f16[200,128]{1,0:T(8,128)(2,1)S(1)}, u32[]{:S(2)}, u32[]{:S(2)}) %collective-permute-start.12) | collective-permute-done | bytes 51232 | tf_op jit(solution)/shard_map/ppermute | solution.py:392
  22.6 0.3 %collective-permute-done.11 = f16[200,128]{1,0:T(8,128)(2,1)S(1)} collective-permute-done((f16[200,128]{1,0:T(8,128)(2,1)S(1)}, f16[200,128]{1,0:T(8,128)(2,1)S(1)}, u32[]{:S(2)}, u32[]{:S(2)}) %collective-permute-start.11) | collective-permute-done | bytes 51232 | tf_op jit(solution)/shard_map/ppermute | solution.py:317
  23.0 0.7 %broadcast_select_fusion = (f32[32,768]{1,0:T(8,128)}, f32[32,768]{1,0:T(8,128)}) fusion(f32[32,768]{1,0:T(8,128)S(1)} %get-tuple-element.25, f32[32,768]{1,0:T(8,128)S(1)} %get-tuple-element.24, pred[]{:T(512)S(6)} %eq.2), kind=kLoop, calls=%fused_computation | loop fusion | flops 49152 | bytes 393217 | tf_op jit(solution)/shard_map/jit(_where)/select_n | solution.py:402
  (13 shorter events, 0.2 us)
Async XLA Ops:
  0.6 2.0 %collective-permute-start.2 = (f32[32]{0:T(128)}, f32[32]{0:T(128)S(1)}, u32[]{:S(2)}, u32[]{:S(2)}) collective-permute-start(f32[32]{0:T(128)} %param.7), channel_id=1, source_target_pairs={{0,4},{4,0},{1,5},{5,1},{2,6},{6,2},{3,7},{7,3},{8,12},{12,8},{9,1... | collective-permute-start | bytes 392 | tf_op jit(solution)/shard_map/ppermute | solution.py:317
  1.1 1.5 %collective-permute-start = (bf16[32,768]{1,0:T(8,128)(2,1)}, bf16[32,768]{1,0:T(8,128)(2,1)S(1)}, u32[]{:S(2)}, u32[]{:S(2)}) collective-permute-start(bf16[32,768]{1,0:T(8,128)(2,1)} %param.5), channel_id=1, source_target_pairs={{0,4},{4,0},{1,5},{5,1},{2,6},{6,2},{3,7},{7,3},{8,12},{12,8},{9,1... | collective-permute-start | bytes 147464 | tf_op jit(solution)/shard_map/ppermute | solution.py:317
  1.2 1.5 %collective-permute-start.1 = (bf16[32,768]{1,0:T(8,128)(2,1)}, bf16[32,768]{1,0:T(8,128)(2,1)S(1)}, u32[]{:S(2)}, u32[]{:S(2)}) collective-permute-start(bf16[32,768]{1,0:T(8,128)(2,1)} %param.6), channel_id=1, source_target_pairs={{0,4},{4,0},{1,5},{5,1},{2,6},{6,2},{3,7},{7,3},{8,12},{12,8},{9,1... | collective-permute-start | bytes 147464 | tf_op jit(solution)/shard_map/ppermute | solution.py:317
  1.7 0.9 %copy-start = (f32[256]{0:T(256)S(1)}, f32[256]{0:T(256)}, u32[]{:S(2)}) copy-start(f32[256]{0:T(256)} %param.8) | copy-start | bytes 3076
  1.7 0.9 %copy-start.1 = (f32[32]{0:T(128)S(1)}, f32[32]{0:T(128)}, u32[]{:S(2)}) copy-start(f32[32]{0:T(128)} %param.7) | copy-start | bytes 388
  2.9 5.6 %collective-permute-start.7 = (bf16[400,128]{1,0:T(8,128)(2,1)S(1)}, bf16[400,128]{1,0:T(8,128)(2,1)S(1)}, u32[]{:S(2)}, u32[]{:S(2)}) collective-permute-start(bf16[400,128]{1,0:T(8,128)(2,1)S(1)} %get-tuple-element.14.refs_2_), channel_id=1, source_target_pairs={{16,0},{7,4},{17,1},{6,5},{18,2},{5,6},{19,3},{4,7},{24,8},{15,12}... | collective-permute-start | bytes 307208 | tf_op jit(solution)/shard_map/ppermute | solution.py:349
  5.8 5.6 %collective-permute-start.5 = (bf16[400,128]{1,0:T(8,128)(2,1)S(1)}, bf16[400,128]{1,0:T(8,128)(2,1)S(1)}, u32[]{:S(2)}, u32[]{:S(2)}) collective-permute-start(bf16[400,128]{1,0:T(8,128)(2,1)S(1)} %get-tuple-element.14.refs_2_), channel_id=1, source_target_pairs={{24,0},{5,4},{25,1},{4,5},{26,2},{7,6},{27,3},{6,7},{16,8},{13,12}... | collective-permute-start | bytes 307208 | tf_op jit(solution)/shard_map/ppermute | solution.py:349
  7.3 5.1 %collective-permute-start.3 = (bf16[400,128]{1,0:T(8,128)(2,1)S(1)}, bf16[400,128]{1,0:T(8,128)(2,1)S(1)}, u32[]{:S(2)}, u32[]{:S(2)}) collective-permute-start(bf16[400,128]{1,0:T(8,128)(2,1)S(1)} %get-tuple-element.14.refs_2_), channel_id=1, source_target_pairs={{8,0},{6,4},{9,1},{7,5},{10,2},{4,6},{11,3},{5,7},{0,8},{14,12},{1... | collective-permute-start | bytes 307208 | tf_op jit(solution)/shard_map/ppermute | solution.py:349
  8.5 3.9 %collective-permute-start.8 = (bf16[400,128]{1,0:T(8,128)(2,1)S(1)}, bf16[400,128]{1,0:T(8,128)(2,1)S(1)}, u32[]{:S(2)}, u32[]{:S(2)}) collective-permute-start(bf16[400,128]{1,0:T(8,128)(2,1)S(1)} %collective-permute-done.7.refs_5_.refs_6_), channel_id=1, source_target_pairs={{0,4},{4,0},{1,5},{5,1},{2,6},{6,2},{3,7},{7,3},{8,12},{12,8},{9,1... | collective-permute-start | bytes 307208 | tf_op jit(solution)/shard_map/ppermute | solution.py:317
  11.4 2.0 %collective-permute-start.6 = (bf16[400,128]{1,0:T(8,128)(2,1)S(1)}, bf16[400,128]{1,0:T(8,128)(2,1)S(1)}, u32[]{:S(2)}, u32[]{:S(2)}) collective-permute-start(bf16[400,128]{1,0:T(8,128)(2,1)S(1)} %collective-permute-done.5.refs_4_.refs_5_), channel_id=1, source_target_pairs={{0,4},{4,0},{1,5},{5,1},{2,6},{6,2},{3,7},{7,3},{8,12},{12,8},{9,1... | collective-permute-start | bytes 307208 | tf_op jit(solution)/shard_map/ppermute | solution.py:317
  12.4 1.3 %collective-permute-start.4 = (bf16[400,128]{1,0:T(8,128)(2,1)S(1)}, bf16[400,128]{1,0:T(8,128)(2,1)S(1)}, u32[]{:S(2)}, u32[]{:S(2)}) collective-permute-start(bf16[400,128]{1,0:T(8,128)(2,1)S(1)} %collective-permute-done.3.refs_3_.refs_4_), channel_id=1, source_target_pairs={{0,4},{4,0},{1,5},{5,1},{2,6},{6,2},{3,7},{7,3},{8,12},{12,8},{9,1... | collective-permute-start | bytes 307208 | tf_op jit(solution)/shard_map/ppermute | solution.py:317
  14.3 5.6 %collective-permute-start.10 = (f16[392,128]{1,0:T(8,128)(2,1)S(1)}, f16[392,128]{1,0:T(8,128)(2,1)S(1)}, u32[]{:S(2)}, u32[]{:S(2)}) collective-permute-start(f16[392,128]{1,0:T(8,128)(2,1)S(1)} %convert_element_type.32), channel_id=1, source_target_pairs={{0,16},{4,7},{1,17},{5,6},{2,18},{6,5},{3,19},{7,4},{8,24},{12,15}... | collective-permute-start | bytes 301064 | tf_op jit(solution)/shard_map/ppermute | solution.py:392
  15.9 5.6 %collective-permute-start.9 = (f16[392,128]{1,0:T(8,128)(2,1)S(1)}, f16[392,128]{1,0:T(8,128)(2,1)S(1)}, u32[]{:S(2)}, u32[]{:S(2)}) collective-permute-start(f16[392,128]{1,0:T(8,128)(2,1)S(1)} %convert_element_type.30), channel_id=1, source_target_pairs={{0,24},{4,5},{1,25},{5,4},{2,26},{6,7},{3,27},{7,6},{8,16},{12,13}... | collective-permute-start | bytes 301064 | tf_op jit(solution)/shard_map/ppermute | solution.py:392
  17.4 4.5 %collective-permute-start.13 = (f16[200,128]{1,0:T(8,128)(2,1)S(1)}, f16[200,128]{1,0:T(8,128)(2,1)S(1)}, u32[]{:S(2)}, u32[]{:S(2)}) collective-permute-start(f16[200,128]{1,0:T(8,128)(2,1)S(1)} %convert_element_type.38), channel_id=1, source_target_pairs={{0,12},{4,2},{1,13},{5,3},{2,14},{6,0},{3,15},{7,1},{8,4},{12,10},... | collective-permute-start | bytes 153608 | tf_op jit(solution)/shard_map/ppermute | solution.py:392
  18.5 4.1 %collective-permute-start.12 = (f16[200,128]{1,0:T(8,128)(2,1)S(1)}, f16[200,128]{1,0:T(8,128)(2,1)S(1)}, u32[]{:S(2)}, u32[]{:S(2)}) collective-permute-start(f16[200,128]{1,0:T(8,128)(2,1)S(1)} %convert_element_type.36), channel_id=1, source_target_pairs={{0,8},{4,6},{1,9},{5,7},{2,10},{6,4},{3,11},{7,5},{8,0},{12,14},{9... | collective-permute-start | bytes 153608 | tf_op jit(solution)/shard_map/ppermute | solution.py:392
  21.6 1.3 %collective-permute-start.11 = (f16[200,128]{1,0:T(8,128)(2,1)S(1)}, f16[200,128]{1,0:T(8,128)(2,1)S(1)}, u32[]{:S(2)}, u32[]{:S(2)}) collective-permute-start(f16[200,128]{1,0:T(8,128)(2,1)S(1)} %convert_element_type.34), channel_id=1, source_target_pairs={{0,4},{4,0},{1,5},{5,1},{2,6},{6,2},{3,7},{7,3},{8,12},{12,8},{9,1... | collective-permute-start | bytes 153608 | tf_op jit(solution)/shard_map/ppermute | solution.py:317

commit v6 on v5

--- a/solution.py
+++ b/solution.py
@@ -11,8 +11,7 @@
 AXES = ("slab", "blk")
 LANES = 128
 NORM_ROWS = 16
-FIRST_STEPS = ((1, 3, 2), (2, 1, 3))
-PIECES = 1
+FIRST_STEPS = ((1, 2, 3), (1, 2, 3))
 SIZE_ROWS = 8
 
 
@@ -189,6 +188,9 @@
     )
     high = weights.astype(jnp.bfloat16)
     low = (weights - high.astype(jnp.float32)).astype(jnp.bfloat16)
+    if b.shape[0] >= 256:
+        both = jnp.dot(jnp.concatenate([high, low], axis=0), b, preferred_element_type=jnp.float32)
+        return both[: a.shape[0]] + both[a.shape[0] :]
     return jnp.dot(
         jnp.concatenate([high, low], axis=1),
         jnp.concatenate([b, b], axis=0),
@@ -214,7 +216,7 @@
     write_partial(out_refs[0], total[:rows])
     write_partial(out_refs[1], total[rows : 2 * rows])
     for i, out_ref in enumerate(out_refs[2:], 1):
-        write_partial(out_ref, total[2 * rows * i : 2 * rows * (i + 1)])
+        write_partial(out_ref, total[2 * rows * i : 2 * rows * (i + 1)], 2)
 
 
 def own_kernel(plan, rows, turns, *refs):
@@ -231,8 +233,8 @@
     ]
 
 
-def write_partial(ref, block):
-    rows = block.shape[0]
+def write_partial(ref, block, parts=1):
+    size = block.shape[0] // parts
     chunks = tiles(block)
     largest = functools.reduce(
         jnp.maximum, [jnp.max(jnp.abs(chunk), axis=0, keepdims=True) for chunk in chunks]
@@ -240,53 +242,59 @@
     power = jnp.ceil(jnp.log2(jnp.maximum(largest, 1e-30))) - 10.0
     factor = jnp.exp2(-power)
     for i, chunk in enumerate(chunks):
-        ref[i * rows : (i + 1) * rows] = (chunk * factor).reshape(rows, LANES)
-    ref[len(chunks) * rows :] = power[0]
+        chunk = (chunk * factor).reshape(block.shape[0], LANES)
+        for j in range(parts):
+            start = (j * len(chunks) + i) * size
+            ref[start : start + size] = chunk[j * size : (j + 1) * size]
+    start = len(chunks) * block.shape[0]
+    copies = (ref.shape[0] - start) // SIZE_ROWS
+    ref[start:] = jnp.concatenate([power[0]] * copies, axis=0)
 
 
 def spread_kernel(value_ref, out_ref):
     out_ref[...] = jnp.full(out_ref.shape, value_ref[0], jnp.float32)
 
 
-def sum_kernel(loss_ref, own_ref, *refs):
-    partial_refs, (keep_ref, *give_refs) = refs[: -1 - PIECES], refs[-1 - PIECES :]
+def read_partials(refs, rows, start):
+    factors = [jnp.exp2(ref[ref.shape[0] - SIZE_ROWS :])[None] for ref in refs]
+    chunks = (refs[0].shape[0] - SIZE_ROWS - start) // rows
+    for i in range(chunks):
+        yield sum(
+            ref[start + i * rows : start + (i + 1) * rows].reshape(-1, SIZE_ROWS, LANES) * factor
+            for ref, factor in zip(refs, factors)
+        )
+
+
+def sum_kernel(own_ref, *refs):
+    partial_refs, (keep_ref, give_ref) = refs[:-2], refs[-2:]
     rows, width = own_ref.shape
-    tail = rows * (width // LANES)
-    loss = loss_ref[...]
-    factors = [jnp.exp2(ref[tail:])[None] for ref in partial_refs]
+    half = rows // 2
+    chunks = width // LANES
+    own = tiles(own_ref[...])
     gives = []
-    for i, total in enumerate(tiles(own_ref[...])):
-        for ref, factor in zip(partial_refs, factors):
-            total = total + tiles(ref[i * rows : (i + 1) * rows])[0] * factor
-        total = (total * loss[None]).reshape(rows, LANES)
-        keep_ref[:, i * LANES : (i + 1) * LANES] = total[: rows // 2]
-        gives.append(total[rows // 2 :])
-    size = rows // 2 // PIECES
-    for i, give_ref in enumerate(give_refs):
-        write_partial(
-            give_ref, jnp.concatenate([give[i * size : (i + 1) * size] for give in gives], axis=1)
-        )
-
-
-def end_kernel(loss_ref, keep_ref, *refs):
-    got_refs, last_refs, (keep_out, got_out) = refs[:PIECES], refs[PIECES:-2], refs[-2:]
+    first = [0.0] * chunks
+    second = [0.0] * chunks
+    if partial_refs:
+        both = list(read_partials(partial_refs, half, 0))
+        first, second = both[:chunks], both[chunks:]
+    for i, total in enumerate(own):
+        n = half // SIZE_ROWS
+        keep_ref[:, i * LANES : (i + 1) * LANES] = (total[:n] + first[i]).reshape(half, LANES)
+        gives.append((total[n:] + second[i]).reshape(half, LANES))
+    write_partial(give_ref, jnp.concatenate(gives, axis=1))
+
+
+def end_kernel(loss_ref, keep_ref, here_ref, got_ref, there_ref, *refs):
+    last_refs, (keep_out, got_out) = refs[:-2], refs[-2:]
     rows, width = keep_ref.shape
-    tail, size = rows * (width // LANES), rows // PIECES
-    loss = loss_ref[...]
-    factors = [(jnp.exp2(ref[tail:]) * loss)[None] for ref in last_refs]
-    got_factors = [jnp.exp2(ref[size * (width // LANES) :])[None] for ref in got_refs]
-    for i, keep in enumerate(tiles(keep_ref[...])):
+    loss = loss_ref[...][None]
+    here = read_partials([here_ref], rows, 0)
+    keeps = read_partials([last_refs[0]], rows, 0)
+    gots = read_partials([got_ref, there_ref, last_refs[1]], rows, 0)
+    for i, (keep, a, b, got) in enumerate(zip(tiles(keep_ref[...]), here, keeps, gots)):
         lanes = slice(i * LANES, (i + 1) * LANES)
-        got = jnp.concatenate(
-            [
-                tiles(ref[i * size : (i + 1) * size])[0] * factor
-                for ref, factor in zip(got_refs, got_factors)
-            ],
-            axis=0,
-        )
-        for total, ref, factor, out_ref in zip((keep, got), last_refs, factors, (keep_out, got_out)):
-            total = total + tiles(ref[i * rows : (i + 1) * rows])[0] * factor
-            out_ref[:, lanes] = total.reshape(rows, LANES)
+        keep_out[:, lanes] = ((keep + a + b) * loss).reshape(rows, LANES)
+        got_out[:, lanes] = (got * loss).reshape(rows, LANES)
 
 
 VMEM = pl.BlockSpec(memory_space=pltpu.VMEM)
@@ -372,7 +380,10 @@
         "late",
         scalars,
         (*early, *a_others, *(b_parts[i] for i in last)),
-        [jax.ShapeDtypeStruct((chunk_rows // 2 + SIZE_ROWS, LANES), jnp.float32)] * 2
+        [
+            jax.ShapeDtypeStruct((chunk_rows // 2 + n * SIZE_ROWS, LANES), jnp.float32)
+            for n in (1, 3)
+        ]
         + [jax.ShapeDtypeStruct((chunk_rows + SIZE_ROWS, LANES), jnp.float32)] * (count - 2),
         3 * count,
     )
@@ -388,17 +399,22 @@
     half = jax.ShapeDtypeStruct((rows, width), jnp.float32)
 
     def crossed(partial, turn, across=False):
-        pairs = plan.group_pairs(turn, across)
-        return lax.ppermute(partial.astype(jnp.float16), AXES, pairs).astype(jnp.float32)
+        return lax.ppermute(partial.astype(jnp.float16), AXES, plan.group_pairs(turn, across))
+
+    def wide(block):
+        return block.astype(jnp.float32)
 
     arrived = [crossed(x, turn) for turn, x in enumerate(partials[2:], 2)]
-    last = [crossed(partials[0], 1), crossed(partials[1], 1, True)]
-    piece = jax.ShapeDtypeStruct((chunk_rows // 2 // PIECES + SIZE_ROWS, LANES), jnp.float32)
-    keep, *gives = call(
-        sum_kernel, "sum", (), (loss, own, *arrived), [half] + [piece] * PIECES, 2 * count
-    )
-    gots = [swapped(give.astype(jnp.float16)).astype(jnp.float32) for give in gives]
-    keep, got = call(end_kernel, "end", (), (loss, keep, *gots, *last), [half, half], 4)
+    last = [wide(crossed(partials[0], 1)), wide(crossed(partials[1], 1, True))]
+    piece = jax.ShapeDtypeStruct((chunk_rows // 2 + SIZE_ROWS, LANES), jnp.float32)
+    keep, give = call(
+        sum_kernel, "sum", (), (own, *(wide(x) for x in arrived[1:])), [half, piece], 2 * count
+    )
+    got = wide(swapped(give.astype(jnp.float16)))
+    there = wide(swapped(arrived[0][chunk_rows // 2 :]))
+    keep, got = call(
+        end_kernel, "end", (), (loss, keep, wide(arrived[0]), got, there, *last), [half, half], 4
+    )
     return jnp.where(core == 1, keep, got), jnp.where(core == 1, got, keep)
 
 

time: 23.9 us -> 23.9 us (level)
  waiting for transfers between devices: 5.56 us -> 5.93 us
    ppermute x3, waiting for transfers between devices: 1.89 us -> 2.82 us  [local(): a_parts.append(lax.ppermute(mine, AXES, back))]
    ppermute x4, waiting for transfers between devices: 2.49 us -> 1.99 us  [crossed(): lax.ppermute(partial.astype(jnp.float16), AXES, plan.group_pairs(turn, ac...]
    ppermute x4, starting transfers between devices: 4.82 us -> 4.58 us  [crossed(): lax.ppermute(partial.astype(jnp.float16), AXES, plan.group_pairs(turn, ac...]
    ppermute x7 -> x8, waiting for transfers between devices: 1.18 us -> 1.12 us  [swapped(): return lax.ppermute(block, AXES, plan.core_pairs())]
    ppermute x7 -> x8, starting transfers between devices: 3.59 us -> 3.6 us  [swapped(): return lax.ppermute(block, AXES, plan.core_pairs())]
  transfers between devices with their start and end apart: 14 -> 15, of which waited for: 9 -> 8; matrix products, arithmetic and copies ran while one was open for 4% -> 4% of each run, Pallas kernels for 5% -> 5%
where the time goes in v6:
time: 23.9 us; the launch traced here: 23.7 us
  starting transfers between devices  12.7 us (53%)
  waiting for transfers between devices  5.93 us (25%)
  Pallas kernels  1.84 us (8%)
  other arithmetic  1.76 us (7%)
  between operations  1.45 us (6%)
    ppermute x4, starting transfers between devices, crossed(): lax.ppermute(partial.astype(jnp.float16), AXES, plan.group_pairs(turn, ac...  4.58 us
    ppermute x3, starting transfers between devices, local(): a_parts.append(lax.ppermute(mine, AXES, back))  4.5 us
    ppermute x8, starting transfers between devices, swapped(): return lax.ppermute(block, AXES, plan.core_pairs())  3.6 us
    ppermute x3, waiting for transfers between devices, local(): a_parts.append(lax.ppermute(mine, AXES, back))  2.82 us
    ppermute x4, waiting for transfers between devices, crossed(): lax.ppermute(partial.astype(jnp.float16), AXES, plan.group_pairs(turn, ac...  1.99 us
    pallas_call x7, Pallas kernels, call(): pl.pallas_call(kernel, out_shape=out_shape, in_specs=[SMEM] * len(scalars...  1.84 us
    ppermute x8, waiting for transfers between devices, swapped(): return lax.ppermute(block, AXES, plan.core_pairs())  1.12 us
    select_n x1, other arithmetic, local(): jnp.where(core == 1, passages, queries)  0.86 us
  transfers between devices with their start and end apart: 15, of which 8 were waited for; matrix products, arithmetic and copies ran while one was open for 4% of the time, Pallas kernels for 5%

profile of v6, /device:TPU:0, one launch (start us, length us, event | category | flops | bytes accessed | tf_op | source)
XLA Modules:
  0.0 23.7 jit_solution(12381601377244610926)
XLA Ops:
  0.6 0.5 %collective-permute-start.2 = (f32[32]{0:T(128)}, f32[32]{0:T(128)S(1)}, u32[]{:S(2)}, u32[]{:S(2)}) collective-permute-start(f32[32]{0:T(128)} %param.7), channel_id=1, source_target_pairs={{0,4},{4,0},{1,5},{5,1},{2,6},{6,2},{3,7},{7,3},{8,12},{12,8},{9,1... | collective-permute-start | bytes 392 | tf_op jit(solution)/shard_map/ppermute | solution.py:325
  1.1 0.1 collective-permute-start
  1.2 0.4 %collective-permute-start.1 = (bf16[32,768]{1,0:T(8,128)(2,1)}, bf16[32,768]{1,0:T(8,128)(2,1)S(1)}, u32[]{:S(2)}, u32[]{:S(2)}) collective-permute-start(bf16[32,768]{1,0:T(8,128)(2,1)} %param.6), channel_id=1, source_target_pairs={{0,4},{4,0},{1,5},{5,1},{2,6},{6,2},{3,7},{7,3},{8,12},{12,8},{9,1... | collective-permute-start | bytes 147464 | tf_op jit(solution)/shard_map/ppermute | solution.py:325
  1.7 0.0 copy-start
  1.7 0.0 copy-start.1
  1.7 0.9 %broadcast_select_fusion.2 = (bf16[32,768]{1,0:T(8,128)(2,1)S(1)}, bf16[32,768]{1,0:T(8,128)(2,1)S(1)}) fusion(bf16[32,768]{1,0:T(8,128)(2,1)} %param.6, bf16[32,768]{1,0:T(8,128)(2,1)} %param.5, pred[]{:T(512)S(6)} %eq.2), kind=kLoop, calls=%fused_computation.2 | loop fusion | flops 49152 | bytes 196609 | tf_op jit(solution)/shard_map/jit(_where)/select_n | solution.py:334
  2.5 0.0 copy-done
  2.5 0.0 copy-done.1
  2.5 0.1 pad_maximum_fusion
  2.6 0.0 collective-permute-done.2
  2.6 0.0 collective-permute-done.got_q_ref
  2.6 0.1 collective-permute-done.1.got_p_ref
  2.8 0.1 pack.1
  2.9 3.9 %collective-permute-start.7 = (bf16[400,128]{1,0:T(8,128)(2,1)S(1)}, bf16[400,128]{1,0:T(8,128)(2,1)S(1)}, u32[]{:S(2)}, u32[]{:S(2)}) collective-permute-start(bf16[400,128]{1,0:T(8,128)(2,1)S(1)} %get-tuple-element.14.refs_2_), channel_id=1, source_target_pairs={{24,0},{7,4},{25,1},{6,5},{26,2},{5,6},{27,3},{4,7},{16,8},{15,12}... | collective-permute-start | bytes 307208 | tf_op jit(solution)/shard_map/ppermute | solution.py:357
  6.7 0.5 %collective-permute-start.5 = (bf16[400,128]{1,0:T(8,128)(2,1)S(1)}, bf16[400,128]{1,0:T(8,128)(2,1)S(1)}, u32[]{:S(2)}, u32[]{:S(2)}) collective-permute-start(bf16[400,128]{1,0:T(8,128)(2,1)S(1)} %get-tuple-element.14.refs_2_), channel_id=1, source_target_pairs={{16,0},{6,4},{17,1},{7,5},{18,2},{4,6},{19,3},{5,7},{24,8},{14,12}... | collective-permute-start | bytes 307208 | tf_op jit(solution)/shard_map/ppermute | solution.py:357
  7.3 0.1 collective-permute-start.3
  7.4 2.0 %collective-permute-done.7.refs_5_.refs_6_ = bf16[400,128]{1,0:T(8,128)(2,1)S(1)} collective-permute-done((bf16[400,128]{1,0:T(8,128)(2,1)S(1)}, bf16[400,128]{1,0:T(8,128)(2,1)S(1)}, u32[]{:S(2)}, u32[]{:S(2)}) %collective-permute-start.7) | collective-permute-done | bytes 102432 | tf_op jit(solution)/shard_map/ppermute | solution.py:357
  9.4 0.6 %collective-permute-start.8 = (bf16[400,128]{1,0:T(8,128)(2,1)S(1)}, bf16[400,128]{1,0:T(8,128)(2,1)S(1)}, u32[]{:S(2)}, u32[]{:S(2)}) collective-permute-start(bf16[400,128]{1,0:T(8,128)(2,1)S(1)} %collective-permute-done.7.refs_5_.refs_6_), channel_id=1, source_target_pairs={{0,4},{4,0},{1,5},{5,1},{2,6},{6,2},{3,7},{7,3},{8,12},{12,8},{9,1... | collective-permute-start | bytes 307208 | tf_op jit(solution)/shard_map/ppermute | solution.py:325
  10.6 0.8 %collective-permute-done.5.refs_4_.refs_5_ = bf16[400,128]{1,0:T(8,128)(2,1)S(1)} collective-permute-done((bf16[400,128]{1,0:T(8,128)(2,1)S(1)}, bf16[400,128]{1,0:T(8,128)(2,1)S(1)}, u32[]{:S(2)}, u32[]{:S(2)}) %collective-permute-start.5) | collective-permute-done | bytes 102432 | tf_op jit(solution)/shard_map/ppermute | solution.py:357
  11.4 1.0 %collective-permute-start.6 = (bf16[400,128]{1,0:T(8,128)(2,1)S(1)}, bf16[400,128]{1,0:T(8,128)(2,1)S(1)}, u32[]{:S(2)}, u32[]{:S(2)}) collective-permute-start(bf16[400,128]{1,0:T(8,128)(2,1)S(1)} %collective-permute-done.5.refs_4_.refs_5_), channel_id=1, source_target_pairs={{0,4},{4,0},{1,5},{5,1},{2,6},{6,2},{3,7},{7,3},{8,12},{12,8},{9,1... | collective-permute-start | bytes 307208 | tf_op jit(solution)/shard_map/ppermute | solution.py:325
  12.4 0.0 collective-permute-done.3.refs_3_.refs_4_
  12.4 0.0 collective-permute-start.4
  12.4 0.0 collective-permute-done.8.refs_6_.refs_7_
  12.4 0.5 %early.1 = (f32[192,768]{1,0:T(8,128)S(1)}, f32[192,128]{1,0:T(8,128)S(1)}) custom-call(s32[1]{0:T(128)} %bitcast.1.slab_ref.refs_0_, s32[1]{0:T(128)} %bitcast.2.refs_1_, f32[8,128]{1,0:T(8,128)S(1)} %spread.1.refs_2_.loss_ref, bf16[400,128]{1,0:T(8,128)(2,1)S(1)} %collective-permute-done.3.refs_3_.refs_4_, ...), custom_call_target="tpu_custom_call" | custom-call | flops 1000000000 | tf_op jit(solution)/shard_map/early/pallas_call | solution.py:305
  13.0 0.4 %collective-permute-done.6.refs_5_.refs_8_ = bf16[400,128]{1,0:T(8,128)(2,1)S(1)} collective-permute-done((bf16[400,128]{1,0:T(8,128)(2,1)S(1)}, bf16[400,128]{1,0:T(8,128)(2,1)S(1)}, u32[]{:S(2)}, u32[]{:S(2)}) %collective-permute-start.6) | collective-permute-done | bytes 102432 | tf_op jit(solution)/shard_map/ppermute | solution.py:325
  13.3 0.4 %collective-permute-done.4.refs_4_.refs_7_ = bf16[400,128]{1,0:T(8,128)(2,1)S(1)} collective-permute-done((bf16[400,128]{1,0:T(8,128)(2,1)S(1)}, bf16[400,128]{1,0:T(8,128)(2,1)S(1)}, u32[]{:S(2)}, u32[]{:S(2)}) %collective-permute-start.4) | collective-permute-done | bytes 102432 | tf_op jit(solution)/shard_map/ppermute | solution.py:325
  13.7 0.6 %late.1 = (f32[200,128]{1,0:T(8,128)S(1)}, f32[216,128]{1,0:T(8,128)S(1)}, f32[392,128]{1,0:T(8,128)S(1)}, f32[392,128]{1,0:T(8,128)S(1)}) custom-call(s32[1]{0:T(128)} %bitcast.1.slab_ref.refs_0_, s32[1]{0:T(128)} %bitcast.2.refs_1_, f32[192,768]{1,0:T(8,128)S(1)} %get-tuple-element.16.refs_2_, f32[192,128]{1,0:T(8,128)S(1)} %get-tuple-element.17.refs_3_, ...), custom_call_target="tpu_custom_call" | custom-call | tf_op jit(solution)/shard_map/late/pallas_call | solution.py:305
  14.3 1.6 %collective-permute-start.10 = (f16[392,128]{1,0:T(8,128)(2,1)S(1)}, f16[392,128]{1,0:T(8,128)(2,1)S(1)}, u32[]{:S(2)}, u32[]{:S(2)}) collective-permute-start(f16[392,128]{1,0:T(8,128)(2,1)S(1)} %convert_element_type.35), channel_id=1, source_target_pairs={{0,16},{4,6},{1,17},{5,7},{2,18},{6,4},{3,19},{7,5},{8,24},{12,14}... | collective-permute-start | bytes 301064 | tf_op jit(solution)/shard_map/ppermute | solution.py:402
  15.9 1.5 %collective-permute-start.9 = (f16[392,128]{1,0:T(8,128)(2,1)S(1)}, f16[392,128]{1,0:T(8,128)(2,1)S(1)}, u32[]{:S(2)}, u32[]{:S(2)}) collective-permute-start(f16[392,128]{1,0:T(8,128)(2,1)S(1)} %convert_element_type.33), channel_id=1, source_target_pairs={{0,24},{4,7},{1,25},{5,6},{2,26},{6,5},{3,27},{7,4},{8,16},{12,15}... | collective-permute-start | bytes 301064 | tf_op jit(solution)/shard_map/ppermute | solution.py:402
  17.4 0.6 %collective-permute-start.13 = (f16[200,128]{1,0:T(8,128)(2,1)S(1)}, f16[200,128]{1,0:T(8,128)(2,1)S(1)}, u32[]{:S(2)}, u32[]{:S(2)}) collective-permute-start(f16[200,128]{1,0:T(8,128)(2,1)S(1)} %convert_element_type.40), channel_id=1, source_target_pairs={{0,8},{4,5},{1,9},{5,4},{2,10},{6,7},{3,11},{7,6},{8,0},{12,13},{9... | collective-permute-start | bytes 153608 | tf_op jit(solution)/shard_map/ppermute | solution.py:402
  18.0 0.9 %collective-permute-start.14 = (f16[216,128]{1,0:T(8,128)(2,1)S(1)}, f16[216,128]{1,0:T(8,128)(2,1)S(1)}, u32[]{:S(2)}, u32[]{:S(2)}) collective-permute-start(f16[216,128]{1,0:T(8,128)(2,1)S(1)} %convert_element_type.42), channel_id=1, source_target_pairs={{0,12},{4,1},{1,13},{5,0},{2,14},{6,3},{3,15},{7,2},{8,4},{12,9},{... | collective-permute-start | bytes 165896 | tf_op jit(solution)/shard_map/ppermute | solution.py:402
  18.9 0.5 %own.1.own_ref = f32[64,768]{1,0:T(8,128)S(1)} custom-call(s32[1]{0:T(128)} %bitcast.1.slab_ref.refs_0_, s32[1]{0:T(128)} %bitcast.2.refs_1_, bf16[400,128]{1,0:T(8,128)(2,1)S(1)} %get-tuple-element.14.refs_2_, bf16[400,128]{1,0:T(8,128)(2,1)S(1)} %get-tuple-element.15.refs_3_.refs_6_, bf16[400,128]{1,0:T(8,128)(2,1)S(1)} %collective-permute-done.4.refs_4_.refs_7_, ...), custom_call_target="tpu_custom_call" | custom-call | flops 1000000000 | tf_op jit(solution)/shard_map/own/pallas_call | solution.py:305
  19.4 0.0 collective-permute-done.10
  19.5 0.6 %collective-permute-start.12 = (f16[200,128]{1,0:T(8,128)(2,1)S(1)}, f16[200,128]{1,0:T(8,128)(2,1)S(1)}, u32[]{:S(2)}, u32[]{:S(2)}) collective-permute-start(f16[200,128]{1,0:T(8,128)(2,1)S(1)} %slice.4), channel_id=1, source_target_pairs={{0,4},{4,0},{1,5},{5,1},{2,6},{6,2},{3,7},{7,3},{8,12},{12,8},{9,1... | collective-permute-start | bytes 153608 | tf_op jit(solution)/shard_map/ppermute | solution.py:325
  20.1 1.4 %collective-permute-done.9 = f16[392,128]{1,0:T(8,128)(2,1)S(1)} collective-permute-done((f16[392,128]{1,0:T(8,128)(2,1)S(1)}, f16[392,128]{1,0:T(8,128)(2,1)S(1)}, u32[]{:S(2)}, u32[]{:S(2)}) %collective-permute-start.9) | collective-permute-done | bytes 100384 | tf_op jit(solution)/shard_map/ppermute | solution.py:402
  21.6 0.4 %collective-permute-start.11 = (f16[200,128]{1,0:T(8,128)(2,1)S(1)}, f16[200,128]{1,0:T(8,128)(2,1)S(1)}, u32[]{:S(2)}, u32[]{:S(2)}) collective-permute-start(f16[200,128]{1,0:T(8,128)(2,1)S(1)} %convert_element_type.37), channel_id=1, source_target_pairs={{0,4},{4,0},{1,5},{5,1},{2,6},{6,2},{3,7},{7,3},{8,12},{12,8},{9,1... | collective-permute-start | bytes 153608 | tf_op jit(solution)/shard_map/ppermute | solution.py:325
  22.0 0.0 collective-permute-done.13
  22.1 0.5 %collective-permute-done.14 = f16[216,128]{1,0:T(8,128)(2,1)S(1)} collective-permute-done((f16[216,128]{1,0:T(8,128)(2,1)S(1)}, f16[216,128]{1,0:T(8,128)(2,1)S(1)}, u32[]{:S(2)}, u32[]{:S(2)}) %collective-permute-start.14) | collective-permute-done | bytes 55328 | tf_op jit(solution)/shard_map/ppermute | solution.py:402
  22.6 0.0 collective-permute-done.12
  22.7 0.3 %collective-permute-done.11 = f16[200,128]{1,0:T(8,128)(2,1)S(1)} collective-permute-done((f16[200,128]{1,0:T(8,128)(2,1)S(1)}, f16[200,128]{1,0:T(8,128)(2,1)S(1)}, u32[]{:S(2)}, u32[]{:S(2)}) %collective-permute-start.11) | collective-permute-done | bytes 51232 | tf_op jit(solution)/shard_map/ppermute | solution.py:325
  22.9 0.1 end.1
  23.0 0.7 %broadcast_select_fusion = (f32[32,768]{1,0:T(8,128)}, f32[32,768]{1,0:T(8,128)}) fusion(f32[32,768]{1,0:T(8,128)S(1)} %get-tuple-element.25, f32[32,768]{1,0:T(8,128)S(1)} %get-tuple-element.24, pred[]{:T(512)S(6)} %eq.2), kind=kLoop, calls=%fused_computation | loop fusion | flops 49152 | bytes 393217 | tf_op jit(solution)/shard_map/jit(_where)/select_n | solution.py:418
  (15 shorter events, 0.2 us)
Async XLA Ops:
  0.6 2.0 %collective-permute-start.2 = (f32[32]{0:T(128)}, f32[32]{0:T(128)S(1)}, u32[]{:S(2)}, u32[]{:S(2)}) collective-permute-start(f32[32]{0:T(128)} %param.7), channel_id=1, source_target_pairs={{0,4},{4,0},{1,5},{5,1},{2,6},{6,2},{3,7},{7,3},{8,12},{12,8},{9,1... | collective-permute-start | bytes 392 | tf_op jit(solution)/shard_map/ppermute | solution.py:325
  1.1 1.5 %collective-permute-start = (bf16[32,768]{1,0:T(8,128)(2,1)}, bf16[32,768]{1,0:T(8,128)(2,1)S(1)}, u32[]{:S(2)}, u32[]{:S(2)}) collective-permute-start(bf16[32,768]{1,0:T(8,128)(2,1)} %param.5), channel_id=1, source_target_pairs={{0,4},{4,0},{1,5},{5,1},{2,6},{6,2},{3,7},{7,3},{8,12},{12,8},{9,1... | collective-permute-start | bytes 147464 | tf_op jit(solution)/shard_map/ppermute | solution.py:325
  1.2 1.5 %collective-permute-start.1 = (bf16[32,768]{1,0:T(8,128)(2,1)}, bf16[32,768]{1,0:T(8,128)(2,1)S(1)}, u32[]{:S(2)}, u32[]{:S(2)}) collective-permute-start(bf16[32,768]{1,0:T(8,128)(2,1)} %param.6), channel_id=1, source_target_pairs={{0,4},{4,0},{1,5},{5,1},{2,6},{6,2},{3,7},{7,3},{8,12},{12,8},{9,1... | collective-permute-start | bytes 147464 | tf_op jit(solution)/shard_map/ppermute | solution.py:325
  1.7 0.9 %copy-start = (f32[256]{0:T(256)S(1)}, f32[256]{0:T(256)}, u32[]{:S(2)}) copy-start(f32[256]{0:T(256)} %param.8) | copy-start | bytes 3076
  1.7 0.9 %copy-start.1 = (f32[32]{0:T(128)S(1)}, f32[32]{0:T(128)}, u32[]{:S(2)}) copy-start(f32[32]{0:T(128)} %param.7) | copy-start | bytes 388
  2.9 6.5 %collective-permute-start.7 = (bf16[400,128]{1,0:T(8,128)(2,1)S(1)}, bf16[400,128]{1,0:T(8,128)(2,1)S(1)}, u32[]{:S(2)}, u32[]{:S(2)}) collective-permute-start(bf16[400,128]{1,0:T(8,128)(2,1)S(1)} %get-tuple-element.14.refs_2_), channel_id=1, source_target_pairs={{24,0},{7,4},{25,1},{6,5},{26,2},{5,6},{27,3},{4,7},{16,8},{15,12}... | collective-permute-start | bytes 307208 | tf_op jit(solution)/shard_map/ppermute | solution.py:357
  6.7 4.7 %collective-permute-start.5 = (bf16[400,128]{1,0:T(8,128)(2,1)S(1)}, bf16[400,128]{1,0:T(8,128)(2,1)S(1)}, u32[]{:S(2)}, u32[]{:S(2)}) collective-permute-start(bf16[400,128]{1,0:T(8,128)(2,1)S(1)} %get-tuple-element.14.refs_2_), channel_id=1, source_target_pairs={{16,0},{6,4},{17,1},{7,5},{18,2},{4,6},{19,3},{5,7},{24,8},{14,12}... | collective-permute-start | bytes 307208 | tf_op jit(solution)/shard_map/ppermute | solution.py:357
  7.3 5.1 %collective-permute-start.3 = (bf16[400,128]{1,0:T(8,128)(2,1)S(1)}, bf16[400,128]{1,0:T(8,128)(2,1)S(1)}, u32[]{:S(2)}, u32[]{:S(2)}) collective-permute-start(bf16[400,128]{1,0:T(8,128)(2,1)S(1)} %get-tuple-element.14.refs_2_), channel_id=1, source_target_pairs={{8,0},{5,4},{9,1},{4,5},{10,2},{7,6},{11,3},{6,7},{0,8},{13,12},{1... | collective-permute-start | bytes 307208 | tf_op jit(solution)/shard_map/ppermute | solution.py:357
  9.4 3.0 %collective-permute-start.8 = (bf16[400,128]{1,0:T(8,128)(2,1)S(1)}, bf16[400,128]{1,0:T(8,128)(2,1)S(1)}, u32[]{:S(2)}, u32[]{:S(2)}) collective-permute-start(bf16[400,128]{1,0:T(8,128)(2,1)S(1)} %collective-permute-done.7.refs_5_.refs_6_), channel_id=1, source_target_pairs={{0,4},{4,0},{1,5},{5,1},{2,6},{6,2},{3,7},{7,3},{8,12},{12,8},{9,1... | collective-permute-start | bytes 307208 | tf_op jit(solution)/shard_map/ppermute | solution.py:325
  11.4 1.9 %collective-permute-start.6 = (bf16[400,128]{1,0:T(8,128)(2,1)S(1)}, bf16[400,128]{1,0:T(8,128)(2,1)S(1)}, u32[]{:S(2)}, u32[]{:S(2)}) collective-permute-start(bf16[400,128]{1,0:T(8,128)(2,1)S(1)} %collective-permute-done.5.refs_4_.refs_5_), channel_id=1, source_target_pairs={{0,4},{4,0},{1,5},{5,1},{2,6},{6,2},{3,7},{7,3},{8,12},{12,8},{9,1... | collective-permute-start | bytes 307208 | tf_op jit(solution)/shard_map/ppermute | solution.py:325
  12.4 1.3 %collective-permute-start.4 = (bf16[400,128]{1,0:T(8,128)(2,1)S(1)}, bf16[400,128]{1,0:T(8,128)(2,1)S(1)}, u32[]{:S(2)}, u32[]{:S(2)}) collective-permute-start(bf16[400,128]{1,0:T(8,128)(2,1)S(1)} %collective-permute-done.3.refs_3_.refs_4_), channel_id=1, source_target_pairs={{0,4},{4,0},{1,5},{5,1},{2,6},{6,2},{3,7},{7,3},{8,12},{12,8},{9,1... | collective-permute-start | bytes 307208 | tf_op jit(solution)/shard_map/ppermute | solution.py:325
  14.3 5.1 %collective-permute-start.10 = (f16[392,128]{1,0:T(8,128)(2,1)S(1)}, f16[392,128]{1,0:T(8,128)(2,1)S(1)}, u32[]{:S(2)}, u32[]{:S(2)}) collective-permute-start(f16[392,128]{1,0:T(8,128)(2,1)S(1)} %convert_element_type.35), channel_id=1, source_target_pairs={{0,16},{4,6},{1,17},{5,7},{2,18},{6,4},{3,19},{7,5},{8,24},{12,14}... | collective-permute-start | bytes 301064 | tf_op jit(solution)/shard_map/ppermute | solution.py:402
  15.9 5.6 %collective-permute-start.9 = (f16[392,128]{1,0:T(8,128)(2,1)S(1)}, f16[392,128]{1,0:T(8,128)(2,1)S(1)}, u32[]{:S(2)}, u32[]{:S(2)}) collective-permute-start(f16[392,128]{1,0:T(8,128)(2,1)S(1)} %convert_element_type.33), channel_id=1, source_target_pairs={{0,24},{4,7},{1,25},{5,6},{2,26},{6,5},{3,27},{7,4},{8,16},{12,15}... | collective-permute-start | bytes 301064 | tf_op jit(solution)/shard_map/ppermute | solution.py:402
  17.4 4.6 %collective-permute-start.13 = (f16[200,128]{1,0:T(8,128)(2,1)S(1)}, f16[200,128]{1,0:T(8,128)(2,1)S(1)}, u32[]{:S(2)}, u32[]{:S(2)}) collective-permute-start(f16[200,128]{1,0:T(8,128)(2,1)S(1)} %convert_element_type.40), channel_id=1, source_target_pairs={{0,8},{4,5},{1,9},{5,4},{2,10},{6,7},{3,11},{7,6},{8,0},{12,13},{9... | collective-permute-start | bytes 153608 | tf_op jit(solution)/shard_map/ppermute | solution.py:402
  18.0 4.6 %collective-permute-start.14 = (f16[216,128]{1,0:T(8,128)(2,1)S(1)}, f16[216,128]{1,0:T(8,128)(2,1)S(1)}, u32[]{:S(2)}, u32[]{:S(2)}) collective-permute-start(f16[216,128]{1,0:T(8,128)(2,1)S(1)} %convert_element_type.42), channel_id=1, source_target_pairs={{0,12},{4,1},{1,13},{5,0},{2,14},{6,3},{3,15},{7,2},{8,4},{12,9},{... | collective-permute-start | bytes 165896 | tf_op jit(solution)/shard_map/ppermute | solution.py:402
  19.5 3.2 %collective-permute-start.12 = (f16[200,128]{1,0:T(8,128)(2,1)S(1)}, f16[200,128]{1,0:T(8,128)(2,1)S(1)}, u32[]{:S(2)}, u32[]{:S(2)}) collective-permute-start(f16[200,128]{1,0:T(8,128)(2,1)S(1)} %slice.4), channel_id=1, source_target_pairs={{0,4},{4,0},{1,5},{5,1},{2,6},{6,2},{3,7},{7,3},{8,12},{12,8},{9,1... | collective-permute-start | bytes 153608 | tf_op jit(solution)/shard_map/ppermute | solution.py:325
  21.6 1.3 %collective-permute-start.11 = (f16[200,128]{1,0:T(8,128)(2,1)S(1)}, f16[200,128]{1,0:T(8,128)(2,1)S(1)}, u32[]{:S(2)}, u32[]{:S(2)}) collective-permute-start(f16[200,128]{1,0:T(8,128)(2,1)S(1)} %convert_element_type.37), channel_id=1, source_target_pairs={{0,4},{4,0},{1,5},{5,1},{2,6},{6,2},{3,7},{7,3},{8,12},{12,8},{9,1... | collective-permute-start | bytes 153608 | tf_op jit(solution)/shard_map/ppermute | solution.py:325

commit v7 on v6

--- a/solution.py
+++ b/solution.py
@@ -11,7 +11,6 @@
 AXES = ("slab", "blk")
 LANES = 128
 NORM_ROWS = 16
-FIRST_STEPS = ((1, 2, 3), (1, 2, 3))
 SIZE_ROWS = 8
 
 
@@ -26,12 +25,6 @@
         self.blk_count = blk_count
         self.chip_count = slab_count // 2
         self.group_size = max(self.chip_count, blk_count)
-
-    def step(self, role, turn):
-        steps = FIRST_STEPS[role]
-        if turn == 0 or self.group_size <= len(steps):
-            return turn
-        return steps[turn - 1] if turn <= len(steps) else turn
 
     def device(self, chip, core, blk):
         return (2 * chip + core) * self.blk_count + blk
@@ -50,13 +43,12 @@
 
     def group_pairs(self, turn, across=False):
         pairs = []
-        p_step, q_step = self.step(0, turn), self.step(1, turn)
         for chip, blk in self.each():
-            if p_step < self.chip_count:
-                other = peer(chip, p_step, self.chip_count)
+            if turn < self.chip_count:
+                other = peer(chip, turn, self.chip_count)
                 pairs.append((self.device(chip, 0, blk), self.device(other, int(across), blk)))
-            if q_step < self.blk_count:
-                other = peer(blk, q_step, self.blk_count)
+            if turn < self.blk_count:
+                other = peer(blk, turn, self.blk_count)
                 pairs.append((self.device(chip, 1, blk), self.device(chip, 1 - across, other)))
         return pairs
 
@@ -155,13 +147,12 @@
     chip = slab >> 1
     number = place
     for i, turn in enumerate(turns):
-        p_step, q_step = plan.step(0, turn), plan.step(1, turn)
         for other in (0, 1):
             core = role ^ other
-            p_shard = blk * (2 * plan.chip_count) + 2 * peer(chip, p_step, plan.chip_count) + core
-            q_shard = (2 * chip + core) * plan.blk_count + peer(blk, q_step, plan.blk_count)
-            p_base = p_shard * rows if p_step < plan.chip_count else -(1 << 24)
-            q_base = q_shard * rows if q_step < plan.blk_count else -(1 << 25)
+            p_shard = blk * (2 * plan.chip_count) + 2 * peer(chip, turn, plan.chip_count) + core
+            q_shard = (2 * chip + core) * plan.blk_count + peer(blk, turn, plan.blk_count)
+            p_base = p_shard * rows if turn < plan.chip_count else -(1 << 24)
+            q_base = q_shard * rows if turn < plan.blk_count else -(1 << 25)
             start = (2 * i + other) * rows
             base = jnp.where(role == 0, p_base, q_base) - start
             number = jnp.where(place >= start, place + base, number)

time: 23.9 us -> 23.9 us (level)
  no operation moved by 1% of the time
where the time goes in v7:
time: 23.9 us; the launch traced here: 23.7 us
  starting transfers between devices  12.7 us (53%)
  waiting for transfers between devices  5.93 us (25%)
  Pallas kernels  1.84 us (8%)
  other arithmetic  1.76 us (7%)
  between operations  1.45 us (6%)
    ppermute x4, starting transfers between devices, crossed(): lax.ppermute(partial.astype(jnp.float16), AXES, plan.group_pairs(turn, ac...  4.58 us
    ppermute x3, starting transfers between devices, local(): a_parts.append(lax.ppermute(mine, AXES, back))  4.5 us
    ppermute x8, starting transfers between devices, swapped(): return lax.ppermute(block, AXES, plan.core_pairs())  3.6 us
    ppermute x3, waiting for transfers between devices, local(): a_parts.append(lax.ppermute(mine, AXES, back))  2.82 us
    ppermute x4, waiting for transfers between devices, crossed(): lax.ppermute(partial.astype(jnp.float16), AXES, plan.group_pairs(turn, ac...  1.99 us
    pallas_call x7, Pallas kernels, call(): pl.pallas_call(kernel, out_shape=out_shape, in_specs=[SMEM] * len(scalars...  1.84 us
    ppermute x8, waiting for transfers between devices, swapped(): return lax.ppermute(block, AXES, plan.core_pairs())  1.12 us
    select_n x1, other arithmetic, local(): jnp.where(core == 1, passages, queries)  0.86 us
  transfers between devices with their start and end apart: 15, of which 8 were waited for; matrix products, arithmetic and copies ran while one was open for 4% of the time, Pallas kernels for 5%

profile of v7, /device:TPU:0, one launch (start us, length us, event | category | flops | bytes accessed | tf_op | source)
XLA Modules:
  0.0 23.7 jit_solution(12381601377244610926)
XLA Ops:
  0.6 0.5 %collective-permute-start.2 = (f32[32]{0:T(128)}, f32[32]{0:T(128)S(1)}, u32[]{:S(2)}, u32[]{:S(2)}) collective-permute-start(f32[32]{0:T(128)} %param.7), channel_id=1, source_target_pairs={{0,4},{4,0},{1,5},{5,1},{2,6},{6,2},{3,7},{7,3},{8,12},{12,8},{9,1... | collective-permute-start | bytes 392 | tf_op jit(solution)/shard_map/ppermute | solution.py:316
  1.1 0.1 collective-permute-start
  1.2 0.4 %collective-permute-start.1 = (bf16[32,768]{1,0:T(8,128)(2,1)}, bf16[32,768]{1,0:T(8,128)(2,1)S(1)}, u32[]{:S(2)}, u32[]{:S(2)}) collective-permute-start(bf16[32,768]{1,0:T(8,128)(2,1)} %param.6), channel_id=1, source_target_pairs={{0,4},{4,0},{1,5},{5,1},{2,6},{6,2},{3,7},{7,3},{8,12},{12,8},{9,1... | collective-permute-start | bytes 147464 | tf_op jit(solution)/shard_map/ppermute | solution.py:316
  1.7 0.0 copy-start
  1.7 0.0 copy-start.1
  1.7 0.9 %broadcast_select_fusion.2 = (bf16[32,768]{1,0:T(8,128)(2,1)S(1)}, bf16[32,768]{1,0:T(8,128)(2,1)S(1)}) fusion(bf16[32,768]{1,0:T(8,128)(2,1)} %param.6, bf16[32,768]{1,0:T(8,128)(2,1)} %param.5, pred[]{:T(512)S(6)} %eq.2), kind=kLoop, calls=%fused_computation.2 | loop fusion | flops 49152 | bytes 196609 | tf_op jit(solution)/shard_map/jit(_where)/select_n | solution.py:325
  2.5 0.0 copy-done
  2.5 0.0 copy-done.1
  2.5 0.1 pad_maximum_fusion
  2.6 0.0 collective-permute-done.2
  2.6 0.0 collective-permute-done.got_q_ref
  2.6 0.1 collective-permute-done.1.got_p_ref
  2.8 0.1 pack.1
  2.9 3.9 %collective-permute-start.7 = (bf16[400,128]{1,0:T(8,128)(2,1)S(1)}, bf16[400,128]{1,0:T(8,128)(2,1)S(1)}, u32[]{:S(2)}, u32[]{:S(2)}) collective-permute-start(bf16[400,128]{1,0:T(8,128)(2,1)S(1)} %get-tuple-element.14.refs_2_), channel_id=1, source_target_pairs={{24,0},{7,4},{25,1},{6,5},{26,2},{5,6},{27,3},{4,7},{16,8},{15,12}... | collective-permute-start | bytes 307208 | tf_op jit(solution)/shard_map/ppermute | solution.py:348
  6.7 0.5 %collective-permute-start.5 = (bf16[400,128]{1,0:T(8,128)(2,1)S(1)}, bf16[400,128]{1,0:T(8,128)(2,1)S(1)}, u32[]{:S(2)}, u32[]{:S(2)}) collective-permute-start(bf16[400,128]{1,0:T(8,128)(2,1)S(1)} %get-tuple-element.14.refs_2_), channel_id=1, source_target_pairs={{16,0},{6,4},{17,1},{7,5},{18,2},{4,6},{19,3},{5,7},{24,8},{14,12}... | collective-permute-start | bytes 307208 | tf_op jit(solution)/shard_map/ppermute | solution.py:348
  7.3 0.1 collective-permute-start.3
  7.4 2.0 %collective-permute-done.7.refs_5_.refs_6_ = bf16[400,128]{1,0:T(8,128)(2,1)S(1)} collective-permute-done((bf16[400,128]{1,0:T(8,128)(2,1)S(1)}, bf16[400,128]{1,0:T(8,128)(2,1)S(1)}, u32[]{:S(2)}, u32[]{:S(2)}) %collective-permute-start.7) | collective-permute-done | bytes 102432 | tf_op jit(solution)/shard_map/ppermute | solution.py:348
  9.4 0.6 %collective-permute-start.8 = (bf16[400,128]{1,0:T(8,128)(2,1)S(1)}, bf16[400,128]{1,0:T(8,128)(2,1)S(1)}, u32[]{:S(2)}, u32[]{:S(2)}) collective-permute-start(bf16[400,128]{1,0:T(8,128)(2,1)S(1)} %collective-permute-done.7.refs_5_.refs_6_), channel_id=1, source_target_pairs={{0,4},{4,0},{1,5},{5,1},{2,6},{6,2},{3,7},{7,3},{8,12},{12,8},{9,1... | collective-permute-start | bytes 307208 | tf_op jit(solution)/shard_map/ppermute | solution.py:316
  10.6 0.8 %collective-permute-done.5.refs_4_.refs_5_ = bf16[400,128]{1,0:T(8,128)(2,1)S(1)} collective-permute-done((bf16[400,128]{1,0:T(8,128)(2,1)S(1)}, bf16[400,128]{1,0:T(8,128)(2,1)S(1)}, u32[]{:S(2)}, u32[]{:S(2)}) %collective-permute-start.5) | collective-permute-done | bytes 102432 | tf_op jit(solution)/shard_map/ppermute | solution.py:348
  11.4 1.0 %collective-permute-start.6 = (bf16[400,128]{1,0:T(8,128)(2,1)S(1)}, bf16[400,128]{1,0:T(8,128)(2,1)S(1)}, u32[]{:S(2)}, u32[]{:S(2)}) collective-permute-start(bf16[400,128]{1,0:T(8,128)(2,1)S(1)} %collective-permute-done.5.refs_4_.refs_5_), channel_id=1, source_target_pairs={{0,4},{4,0},{1,5},{5,1},{2,6},{6,2},{3,7},{7,3},{8,12},{12,8},{9,1... | collective-permute-start | bytes 307208 | tf_op jit(solution)/shard_map/ppermute | solution.py:316
  12.4 0.0 collective-permute-done.3.refs_3_.refs_4_
  12.4 0.0 collective-permute-start.4
  12.4 0.0 collective-permute-done.8.refs_6_.refs_7_
  12.4 0.5 %early.1 = (f32[192,768]{1,0:T(8,128)S(1)}, f32[192,128]{1,0:T(8,128)S(1)}) custom-call(s32[1]{0:T(128)} %bitcast.1.slab_ref.refs_0_, s32[1]{0:T(128)} %bitcast.2.refs_1_, f32[8,128]{1,0:T(8,128)S(1)} %spread.1.refs_2_.loss_ref, bf16[400,128]{1,0:T(8,128)(2,1)S(1)} %collective-permute-done.3.refs_3_.refs_4_, ...), custom_call_target="tpu_custom_call" | custom-call | flops 1000000000 | tf_op jit(solution)/shard_map/early/pallas_call | solution.py:296
  13.0 0.4 %collective-permute-done.6.refs_5_.refs_8_ = bf16[400,128]{1,0:T(8,128)(2,1)S(1)} collective-permute-done((bf16[400,128]{1,0:T(8,128)(2,1)S(1)}, bf16[400,128]{1,0:T(8,128)(2,1)S(1)}, u32[]{:S(2)}, u32[]{:S(2)}) %collective-permute-start.6) | collective-permute-done | bytes 102432 | tf_op jit(solution)/shard_map/ppermute | solution.py:316
  13.3 0.4 %collective-permute-done.4.refs_4_.refs_7_ = bf16[400,128]{1,0:T(8,128)(2,1)S(1)} collective-permute-done((bf16[400,128]{1,0:T(8,128)(2,1)S(1)}, bf16[400,128]{1,0:T(8,128)(2,1)S(1)}, u32[]{:S(2)}, u32[]{:S(2)}) %collective-permute-start.4) | collective-permute-done | bytes 102432 | tf_op jit(solution)/shard_map/ppermute | solution.py:316
  13.7 0.6 %late.1 = (f32[200,128]{1,0:T(8,128)S(1)}, f32[216,128]{1,0:T(8,128)S(1)}, f32[392,128]{1,0:T(8,128)S(1)}, f32[392,128]{1,0:T(8,128)S(1)}) custom-call(s32[1]{0:T(128)} %bitcast.1.slab_ref.refs_0_, s32[1]{0:T(128)} %bitcast.2.refs_1_, f32[192,768]{1,0:T(8,128)S(1)} %get-tuple-element.16.refs_2_, f32[192,128]{1,0:T(8,128)S(1)} %get-tuple-element.17.refs_3_, ...), custom_call_target="tpu_custom_call" | custom-call | tf_op jit(solution)/shard_map/late/pallas_call | solution.py:296
  14.3 1.6 %collective-permute-start.10 = (f16[392,128]{1,0:T(8,128)(2,1)S(1)}, f16[392,128]{1,0:T(8,128)(2,1)S(1)}, u32[]{:S(2)}, u32[]{:S(2)}) collective-permute-start(f16[392,128]{1,0:T(8,128)(2,1)S(1)} %convert_element_type.35), channel_id=1, source_target_pairs={{0,16},{4,6},{1,17},{5,7},{2,18},{6,4},{3,19},{7,5},{8,24},{12,14}... | collective-permute-start | bytes 301064 | tf_op jit(solution)/shard_map/ppermute | solution.py:393
  15.9 1.5 %collective-permute-start.9 = (f16[392,128]{1,0:T(8,128)(2,1)S(1)}, f16[392,128]{1,0:T(8,128)(2,1)S(1)}, u32[]{:S(2)}, u32[]{:S(2)}) collective-permute-start(f16[392,128]{1,0:T(8,128)(2,1)S(1)} %convert_element_type.33), channel_id=1, source_target_pairs={{0,24},{4,7},{1,25},{5,6},{2,26},{6,5},{3,27},{7,4},{8,16},{12,15}... | collective-permute-start | bytes 301064 | tf_op jit(solution)/shard_map/ppermute | solution.py:393
  17.4 0.6 %collective-permute-start.13 = (f16[200,128]{1,0:T(8,128)(2,1)S(1)}, f16[200,128]{1,0:T(8,128)(2,1)S(1)}, u32[]{:S(2)}, u32[]{:S(2)}) collective-permute-start(f16[200,128]{1,0:T(8,128)(2,1)S(1)} %convert_element_type.40), channel_id=1, source_target_pairs={{0,8},{4,5},{1,9},{5,4},{2,10},{6,7},{3,11},{7,6},{8,0},{12,13},{9... | collective-permute-start | bytes 153608 | tf_op jit(solution)/shard_map/ppermute | solution.py:393
  18.0 0.9 %collective-permute-start.14 = (f16[216,128]{1,0:T(8,128)(2,1)S(1)}, f16[216,128]{1,0:T(8,128)(2,1)S(1)}, u32[]{:S(2)}, u32[]{:S(2)}) collective-permute-start(f16[216,128]{1,0:T(8,128)(2,1)S(1)} %convert_element_type.42), channel_id=1, source_target_pairs={{0,12},{4,1},{1,13},{5,0},{2,14},{6,3},{3,15},{7,2},{8,4},{12,9},{... | collective-permute-start | bytes 165896 | tf_op jit(solution)/shard_map/ppermute | solution.py:393
  18.9 0.5 %own.1.own_ref = f32[64,768]{1,0:T(8,128)S(1)} custom-call(s32[1]{0:T(128)} %bitcast.1.slab_ref.refs_0_, s32[1]{0:T(128)} %bitcast.2.refs_1_, bf16[400,128]{1,0:T(8,128)(2,1)S(1)} %get-tuple-element.14.refs_2_, bf16[400,128]{1,0:T(8,128)(2,1)S(1)} %get-tuple-element.15.refs_3_.refs_6_, bf16[400,128]{1,0:T(8,128)(2,1)S(1)} %collective-permute-done.4.refs_4_.refs_7_, ...), custom_call_target="tpu_custom_call" | custom-call | flops 1000000000 | tf_op jit(solution)/shard_map/own/pallas_call | solution.py:296
  19.4 0.0 collective-permute-done.10
  19.5 0.6 %collective-permute-start.12 = (f16[200,128]{1,0:T(8,128)(2,1)S(1)}, f16[200,128]{1,0:T(8,128)(2,1)S(1)}, u32[]{:S(2)}, u32[]{:S(2)}) collective-permute-start(f16[200,128]{1,0:T(8,128)(2,1)S(1)} %slice.4), channel_id=1, source_target_pairs={{0,4},{4,0},{1,5},{5,1},{2,6},{6,2},{3,7},{7,3},{8,12},{12,8},{9,1... | collective-permute-start | bytes 153608 | tf_op jit(solution)/shard_map/ppermute | solution.py:316
  20.1 1.4 %collective-permute-done.9 = f16[392,128]{1,0:T(8,128)(2,1)S(1)} collective-permute-done((f16[392,128]{1,0:T(8,128)(2,1)S(1)}, f16[392,128]{1,0:T(8,128)(2,1)S(1)}, u32[]{:S(2)}, u32[]{:S(2)}) %collective-permute-start.9) | collective-permute-done | bytes 100384 | tf_op jit(solution)/shard_map/ppermute | solution.py:393
  21.6 0.4 %collective-permute-start.11 = (f16[200,128]{1,0:T(8,128)(2,1)S(1)}, f16[200,128]{1,0:T(8,128)(2,1)S(1)}, u32[]{:S(2)}, u32[]{:S(2)}) collective-permute-start(f16[200,128]{1,0:T(8,128)(2,1)S(1)} %convert_element_type.37), channel_id=1, source_target_pairs={{0,4},{4,0},{1,5},{5,1},{2,6},{6,2},{3,7},{7,3},{8,12},{12,8},{9,1... | collective-permute-start | bytes 153608 | tf_op jit(solution)/shard_map/ppermute | solution.py:316
  22.0 0.0 collective-permute-done.13
  22.1 0.5 %collective-permute-done.14 = f16[216,128]{1,0:T(8,128)(2,1)S(1)} collective-permute-done((f16[216,128]{1,0:T(8,128)(2,1)S(1)}, f16[216,128]{1,0:T(8,128)(2,1)S(1)}, u32[]{:S(2)}, u32[]{:S(2)}) %collective-permute-start.14) | collective-permute-done | bytes 55328 | tf_op jit(solution)/shard_map/ppermute | solution.py:393
  22.6 0.0 collective-permute-done.12
  22.7 0.3 %collective-permute-done.11 = f16[200,128]{1,0:T(8,128)(2,1)S(1)} collective-permute-done((f16[200,128]{1,0:T(8,128)(2,1)S(1)}, f16[200,128]{1,0:T(8,128)(2,1)S(1)}, u32[]{:S(2)}, u32[]{:S(2)}) %collective-permute-start.11) | collective-permute-done | bytes 51232 | tf_op jit(solution)/shard_map/ppermute | solution.py:316
  22.9 0.1 end.1
  23.0 0.7 %broadcast_select_fusion = (f32[32,768]{1,0:T(8,128)}, f32[32,768]{1,0:T(8,128)}) fusion(f32[32,768]{1,0:T(8,128)S(1)} %get-tuple-element.25, f32[32,768]{1,0:T(8,128)S(1)} %get-tuple-element.24, pred[]{:T(512)S(6)} %eq.2), kind=kLoop, calls=%fused_computation | loop fusion | flops 49152 | bytes 393217 | tf_op jit(solution)/shard_map/jit(_where)/select_n | solution.py:409
  (15 shorter events, 0.2 us)
Async XLA Ops:
  0.6 2.0 %collective-permute-start.2 = (f32[32]{0:T(128)}, f32[32]{0:T(128)S(1)}, u32[]{:S(2)}, u32[]{:S(2)}) collective-permute-start(f32[32]{0:T(128)} %param.7), channel_id=1, source_target_pairs={{0,4},{4,0},{1,5},{5,1},{2,6},{6,2},{3,7},{7,3},{8,12},{12,8},{9,1... | collective-permute-start | bytes 392 | tf_op jit(solution)/shard_map/ppermute | solution.py:316
  1.1 1.5 %collective-permute-start = (bf16[32,768]{1,0:T(8,128)(2,1)}, bf16[32,768]{1,0:T(8,128)(2,1)S(1)}, u32[]{:S(2)}, u32[]{:S(2)}) collective-permute-start(bf16[32,768]{1,0:T(8,128)(2,1)} %param.5), channel_id=1, source_target_pairs={{0,4},{4,0},{1,5},{5,1},{2,6},{6,2},{3,7},{7,3},{8,12},{12,8},{9,1... | collective-permute-start | bytes 147464 | tf_op jit(solution)/shard_map/ppermute | solution.py:316
  1.2 1.5 %collective-permute-start.1 = (bf16[32,768]{1,0:T(8,128)(2,1)}, bf16[32,768]{1,0:T(8,128)(2,1)S(1)}, u32[]{:S(2)}, u32[]{:S(2)}) collective-permute-start(bf16[32,768]{1,0:T(8,128)(2,1)} %param.6), channel_id=1, source_target_pairs={{0,4},{4,0},{1,5},{5,1},{2,6},{6,2},{3,7},{7,3},{8,12},{12,8},{9,1... | collective-permute-start | bytes 147464 | tf_op jit(solution)/shard_map/ppermute | solution.py:316
  1.7 0.9 %copy-start = (f32[256]{0:T(256)S(1)}, f32[256]{0:T(256)}, u32[]{:S(2)}) copy-start(f32[256]{0:T(256)} %param.8) | copy-start | bytes 3076
  1.7 0.9 %copy-start.1 = (f32[32]{0:T(128)S(1)}, f32[32]{0:T(128)}, u32[]{:S(2)}) copy-start(f32[32]{0:T(128)} %param.7) | copy-start | bytes 388
  2.9 6.5 %collective-permute-start.7 = (bf16[400,128]{1,0:T(8,128)(2,1)S(1)}, bf16[400,128]{1,0:T(8,128)(2,1)S(1)}, u32[]{:S(2)}, u32[]{:S(2)}) collective-permute-start(bf16[400,128]{1,0:T(8,128)(2,1)S(1)} %get-tuple-element.14.refs_2_), channel_id=1, source_target_pairs={{24,0},{7,4},{25,1},{6,5},{26,2},{5,6},{27,3},{4,7},{16,8},{15,12}... | collective-permute-start | bytes 307208 | tf_op jit(solution)/shard_map/ppermute | solution.py:348
  6.7 4.7 %collective-permute-start.5 = (bf16[400,128]{1,0:T(8,128)(2,1)S(1)}, bf16[400,128]{1,0:T(8,128)(2,1)S(1)}, u32[]{:S(2)}, u32[]{:S(2)}) collective-permute-start(bf16[400,128]{1,0:T(8,128)(2,1)S(1)} %get-tuple-element.14.refs_2_), channel_id=1, source_target_pairs={{16,0},{6,4},{17,1},{7,5},{18,2},{4,6},{19,3},{5,7},{24,8},{14,12}... | collective-permute-start | bytes 307208 | tf_op jit(solution)/shard_map/ppermute | solution.py:348
  7.3 5.1 %collective-permute-start.3 = (bf16[400,128]{1,0:T(8,128)(2,1)S(1)}, bf16[400,128]{1,0:T(8,128)(2,1)S(1)}, u32[]{:S(2)}, u32[]{:S(2)}) collective-permute-start(bf16[400,128]{1,0:T(8,128)(2,1)S(1)} %get-tuple-element.14.refs_2_), channel_id=1, source_target_pairs={{8,0},{5,4},{9,1},{4,5},{10,2},{7,6},{11,3},{6,7},{0,8},{13,12},{1... | collective-permute-start | bytes 307208 | tf_op jit(solution)/shard_map/ppermute | solution.py:348
  9.4 3.0 %collective-permute-start.8 = (bf16[400,128]{1,0:T(8,128)(2,1)S(1)}, bf16[400,128]{1,0:T(8,128)(2,1)S(1)}, u32[]{:S(2)}, u32[]{:S(2)}) collective-permute-start(bf16[400,128]{1,0:T(8,128)(2,1)S(1)} %collective-permute-done.7.refs_5_.refs_6_), channel_id=1, source_target_pairs={{0,4},{4,0},{1,5},{5,1},{2,6},{6,2},{3,7},{7,3},{8,12},{12,8},{9,1... | collective-permute-start | bytes 307208 | tf_op jit(solution)/shard_map/ppermute | solution.py:316
  11.4 1.9 %collective-permute-start.6 = (bf16[400,128]{1,0:T(8,128)(2,1)S(1)}, bf16[400,128]{1,0:T(8,128)(2,1)S(1)}, u32[]{:S(2)}, u32[]{:S(2)}) collective-permute-start(bf16[400,128]{1,0:T(8,128)(2,1)S(1)} %collective-permute-done.5.refs_4_.refs_5_), channel_id=1, source_target_pairs={{0,4},{4,0},{1,5},{5,1},{2,6},{6,2},{3,7},{7,3},{8,12},{12,8},{9,1... | collective-permute-start | bytes 307208 | tf_op jit(solution)/shard_map/ppermute | solution.py:316
  12.4 1.3 %collective-permute-start.4 = (bf16[400,128]{1,0:T(8,128)(2,1)S(1)}, bf16[400,128]{1,0:T(8,128)(2,1)S(1)}, u32[]{:S(2)}, u32[]{:S(2)}) collective-permute-start(bf16[400,128]{1,0:T(8,128)(2,1)S(1)} %collective-permute-done.3.refs_3_.refs_4_), channel_id=1, source_target_pairs={{0,4},{4,0},{1,5},{5,1},{2,6},{6,2},{3,7},{7,3},{8,12},{12,8},{9,1... | collective-permute-start | bytes 307208 | tf_op jit(solution)/shard_map/ppermute | solution.py:316
  14.3 5.1 %collective-permute-start.10 = (f16[392,128]{1,0:T(8,128)(2,1)S(1)}, f16[392,128]{1,0:T(8,128)(2,1)S(1)}, u32[]{:S(2)}, u32[]{:S(2)}) collective-permute-start(f16[392,128]{1,0:T(8,128)(2,1)S(1)} %convert_element_type.35), channel_id=1, source_target_pairs={{0,16},{4,6},{1,17},{5,7},{2,18},{6,4},{3,19},{7,5},{8,24},{12,14}... | collective-permute-start | bytes 301064 | tf_op jit(solution)/shard_map/ppermute | solution.py:393
  15.9 5.6 %collective-permute-start.9 = (f16[392,128]{1,0:T(8,128)(2,1)S(1)}, f16[392,128]{1,0:T(8,128)(2,1)S(1)}, u32[]{:S(2)}, u32[]{:S(2)}) collective-permute-start(f16[392,128]{1,0:T(8,128)(2,1)S(1)} %convert_element_type.33), channel_id=1, source_target_pairs={{0,24},{4,7},{1,25},{5,6},{2,26},{6,5},{3,27},{7,4},{8,16},{12,15}... | collective-permute-start | bytes 301064 | tf_op jit(solution)/shard_map/ppermute | solution.py:393
  17.4 4.6 %collective-permute-start.13 = (f16[200,128]{1,0:T(8,128)(2,1)S(1)}, f16[200,128]{1,0:T(8,128)(2,1)S(1)}, u32[]{:S(2)}, u32[]{:S(2)}) collective-permute-start(f16[200,128]{1,0:T(8,128)(2,1)S(1)} %convert_element_type.40), channel_id=1, source_target_pairs={{0,8},{4,5},{1,9},{5,4},{2,10},{6,7},{3,11},{7,6},{8,0},{12,13},{9... | collective-permute-start | bytes 153608 | tf_op jit(solution)/shard_map/ppermute | solution.py:393
  18.0 4.6 %collective-permute-start.14 = (f16[216,128]{1,0:T(8,128)(2,1)S(1)}, f16[216,128]{1,0:T(8,128)(2,1)S(1)}, u32[]{:S(2)}, u32[]{:S(2)}) collective-permute-start(f16[216,128]{1,0:T(8,128)(2,1)S(1)} %convert_element_type.42), channel_id=1, source_target_pairs={{0,12},{4,1},{1,13},{5,0},{2,14},{6,3},{3,15},{7,2},{8,4},{12,9},{... | collective-permute-start | bytes 165896 | tf_op jit(solution)/shard_map/ppermute | solution.py:393
  19.5 3.2 %collective-permute-start.12 = (f16[200,128]{1,0:T(8,128)(2,1)S(1)}, f16[200,128]{1,0:T(8,128)(2,1)S(1)}, u32[]{:S(2)}, u32[]{:S(2)}) collective-permute-start(f16[200,128]{1,0:T(8,128)(2,1)S(1)} %slice.4), channel_id=1, source_target_pairs={{0,4},{4,0},{1,5},{5,1},{2,6},{6,2},{3,7},{7,3},{8,12},{12,8},{9,1... | collective-permute-start | bytes 153608 | tf_op jit(solution)/shard_map/ppermute | solution.py:316
  21.6 1.3 %collective-permute-start.11 = (f16[200,128]{1,0:T(8,128)(2,1)S(1)}, f16[200,128]{1,0:T(8,128)(2,1)S(1)}, u32[]{:S(2)}, u32[]{:S(2)}) collective-permute-start(f16[200,128]{1,0:T(8,128)(2,1)S(1)} %convert_element_type.37), channel_id=1, source_target_pairs={{0,4},{4,0},{1,5},{5,1},{2,6},{6,2},{3,7},{7,3},{8,12},{12,8},{9,1... | collective-permute-start | bytes 153608 | tf_op jit(solution)/shard_map/ppermute | solution.py:316

commit v8 on v7

--- a/solution.py
+++ b/solution.py
@@ -373,7 +373,7 @@
         (*early, *a_others, *(b_parts[i] for i in last)),
         [
             jax.ShapeDtypeStruct((chunk_rows // 2 + n * SIZE_ROWS, LANES), jnp.float32)
-            for n in (1, 3)
+            for n in (3, 5)
         ]
         + [jax.ShapeDtypeStruct((chunk_rows + SIZE_ROWS, LANES), jnp.float32)] * (count - 2),
         3 * count,
@@ -397,14 +397,14 @@
 
     arrived = [crossed(x, turn) for turn, x in enumerate(partials[2:], 2)]
     last = [wide(crossed(partials[0], 1)), wide(crossed(partials[1], 1, True))]
-    piece = jax.ShapeDtypeStruct((chunk_rows // 2 + SIZE_ROWS, LANES), jnp.float32)
+    piece = jax.ShapeDtypeStruct((chunk_rows // 2 + 2 * SIZE_ROWS, LANES), jnp.float32)
     keep, give = call(
-        sum_kernel, "sum", (), (own, *(wide(x) for x in arrived[1:])), [half, piece], 2 * count
+        sum_kernel, "sum", (), (own, *(wide(x) for x in arrived[:-1])), [half, piece], 2 * count
     )
     got = wide(swapped(give.astype(jnp.float16)))
-    there = wide(swapped(arrived[0][chunk_rows // 2 :]))
+    there = wide(swapped(arrived[-1][chunk_rows // 2 :]))
     keep, got = call(
-        end_kernel, "end", (), (loss, keep, wide(arrived[0]), got, there, *last), [half, half], 4
+        end_kernel, "end", (), (loss, keep, wide(arrived[-1]), got, there, *last), [half, half], 4
     )
     return jnp.where(core == 1, keep, got), jnp.where(core == 1, got, keep)
 

time: 23.9 us -> 23.8 us (level)
  transfers between devices with their start and end apart: 15 -> 15, of which waited for: 8 -> 8; matrix products, arithmetic and copies ran while one was open for 4% -> 5% of each run, Pallas kernels for 5% -> 5%
where the time goes in v8:
time: 23.8 us; the launch traced here: 23.7 us
  starting transfers between devices  12.7 us (53%)
  waiting for transfers between devices  5.88 us (25%)
  Pallas kernels  1.85 us (8%)
  other arithmetic  1.77 us (7%)
  between operations  1.45 us (6%)
    ppermute x4, starting transfers between devices, crossed(): lax.ppermute(partial.astype(jnp.float16), AXES, plan.group_pairs(turn, ac...  4.58 us
    ppermute x3, starting transfers between devices, local(): a_parts.append(lax.ppermute(mine, AXES, back))  4.5 us
    ppermute x8, starting transfers between devices, swapped(): return lax.ppermute(block, AXES, plan.core_pairs())  3.6 us
    ppermute x3, waiting for transfers between devices, local(): a_parts.append(lax.ppermute(mine, AXES, back))  2.82 us
    ppermute x4, waiting for transfers between devices, crossed(): lax.ppermute(partial.astype(jnp.float16), AXES, plan.group_pairs(turn, ac...  2.06 us
    pallas_call x7, Pallas kernels, call(): pl.pallas_call(kernel, out_shape=out_shape, in_specs=[SMEM] * len(scalars...  1.85 us
    ppermute x8, waiting for transfers between devices, swapped(): return lax.ppermute(block, AXES, plan.core_pairs())  1 us
    select_n x1, other arithmetic, local(): jnp.where(core == 1, passages, queries)  0.86 us
  transfers between devices with their start and end apart: 15, of which 8 were waited for; matrix products, arithmetic and copies ran while one was open for 5% of the time, Pallas kernels for 5%

profile of v8, /device:TPU:0, one launch (start us, length us, event | category | flops | bytes accessed | tf_op | source)
XLA Modules:
  0.0 23.7 jit_solution(897865620967194836)
XLA Ops:
  0.6 0.5 %collective-permute-start.2 = (f32[32]{0:T(128)}, f32[32]{0:T(128)S(1)}, u32[]{:S(2)}, u32[]{:S(2)}) collective-permute-start(f32[32]{0:T(128)} %param.7), channel_id=1, source_target_pairs={{0,4},{4,0},{1,5},{5,1},{2,6},{6,2},{3,7},{7,3},{8,12},{12,8},{9,1... | collective-permute-start | bytes 392 | tf_op jit(solution)/shard_map/ppermute | solution.py:316
  1.1 0.1 collective-permute-start
  1.2 0.4 %collective-permute-start.1 = (bf16[32,768]{1,0:T(8,128)(2,1)}, bf16[32,768]{1,0:T(8,128)(2,1)S(1)}, u32[]{:S(2)}, u32[]{:S(2)}) collective-permute-start(bf16[32,768]{1,0:T(8,128)(2,1)} %param.6), channel_id=1, source_target_pairs={{0,4},{4,0},{1,5},{5,1},{2,6},{6,2},{3,7},{7,3},{8,12},{12,8},{9,1... | collective-permute-start | bytes 147464 | tf_op jit(solution)/shard_map/ppermute | solution.py:316
  1.7 0.0 copy-start
  1.7 0.0 copy-start.1
  1.7 0.9 %broadcast_select_fusion.2 = (bf16[32,768]{1,0:T(8,128)(2,1)S(1)}, bf16[32,768]{1,0:T(8,128)(2,1)S(1)}) fusion(bf16[32,768]{1,0:T(8,128)(2,1)} %param.6, bf16[32,768]{1,0:T(8,128)(2,1)} %param.5, pred[]{:T(512)S(6)} %eq.2), kind=kLoop, calls=%fused_computation.2 | loop fusion | flops 49152 | bytes 196609 | tf_op jit(solution)/shard_map/jit(_where)/select_n | solution.py:325
  2.5 0.0 copy-done
  2.5 0.0 copy-done.1
  2.5 0.1 pad_maximum_fusion
  2.6 0.0 collective-permute-done.2
  2.6 0.0 collective-permute-done.got_q_ref
  2.6 0.1 collective-permute-done.1.got_p_ref
  2.8 0.1 pack.1
  2.9 3.9 %collective-permute-start.7 = (bf16[400,128]{1,0:T(8,128)(2,1)S(1)}, bf16[400,128]{1,0:T(8,128)(2,1)S(1)}, u32[]{:S(2)}, u32[]{:S(2)}) collective-permute-start(bf16[400,128]{1,0:T(8,128)(2,1)S(1)} %get-tuple-element.14.refs_2_), channel_id=1, source_target_pairs={{24,0},{7,4},{25,1},{6,5},{26,2},{5,6},{27,3},{4,7},{16,8},{15,12}... | collective-permute-start | bytes 307208 | tf_op jit(solution)/shard_map/ppermute | solution.py:348
  6.7 0.5 %collective-permute-start.5 = (bf16[400,128]{1,0:T(8,128)(2,1)S(1)}, bf16[400,128]{1,0:T(8,128)(2,1)S(1)}, u32[]{:S(2)}, u32[]{:S(2)}) collective-permute-start(bf16[400,128]{1,0:T(8,128)(2,1)S(1)} %get-tuple-element.14.refs_2_), channel_id=1, source_target_pairs={{16,0},{6,4},{17,1},{7,5},{18,2},{4,6},{19,3},{5,7},{24,8},{14,12}... | collective-permute-start | bytes 307208 | tf_op jit(solution)/shard_map/ppermute | solution.py:348
  7.3 0.1 collective-permute-start.3
  7.4 2.0 %collective-permute-done.7.refs_5_.refs_6_ = bf16[400,128]{1,0:T(8,128)(2,1)S(1)} collective-permute-done((bf16[400,128]{1,0:T(8,128)(2,1)S(1)}, bf16[400,128]{1,0:T(8,128)(2,1)S(1)}, u32[]{:S(2)}, u32[]{:S(2)}) %collective-permute-start.7) | collective-permute-done | bytes 102432 | tf_op jit(solution)/shard_map/ppermute | solution.py:348
  9.4 0.6 %collective-permute-start.8 = (bf16[400,128]{1,0:T(8,128)(2,1)S(1)}, bf16[400,128]{1,0:T(8,128)(2,1)S(1)}, u32[]{:S(2)}, u32[]{:S(2)}) collective-permute-start(bf16[400,128]{1,0:T(8,128)(2,1)S(1)} %collective-permute-done.7.refs_5_.refs_6_), channel_id=1, source_target_pairs={{0,4},{4,0},{1,5},{5,1},{2,6},{6,2},{3,7},{7,3},{8,12},{12,8},{9,1... | collective-permute-start | bytes 307208 | tf_op jit(solution)/shard_map/ppermute | solution.py:316
  10.6 0.8 %collective-permute-done.5.refs_4_.refs_5_ = bf16[400,128]{1,0:T(8,128)(2,1)S(1)} collective-permute-done((bf16[400,128]{1,0:T(8,128)(2,1)S(1)}, bf16[400,128]{1,0:T(8,128)(2,1)S(1)}, u32[]{:S(2)}, u32[]{:S(2)}) %collective-permute-start.5) | collective-permute-done | bytes 102432 | tf_op jit(solution)/shard_map/ppermute | solution.py:348
  11.4 1.0 %collective-permute-start.6 = (bf16[400,128]{1,0:T(8,128)(2,1)S(1)}, bf16[400,128]{1,0:T(8,128)(2,1)S(1)}, u32[]{:S(2)}, u32[]{:S(2)}) collective-permute-start(bf16[400,128]{1,0:T(8,128)(2,1)S(1)} %collective-permute-done.5.refs_4_.refs_5_), channel_id=1, source_target_pairs={{0,4},{4,0},{1,5},{5,1},{2,6},{6,2},{3,7},{7,3},{8,12},{12,8},{9,1... | collective-permute-start | bytes 307208 | tf_op jit(solution)/shard_map/ppermute | solution.py:316
  12.4 0.0 collective-permute-done.3.refs_3_.refs_4_
  12.4 0.0 collective-permute-start.4
  12.4 0.0 collective-permute-done.8.refs_6_.refs_7_
  12.4 0.5 %early.1 = (f32[192,768]{1,0:T(8,128)S(1)}, f32[192,128]{1,0:T(8,128)S(1)}) custom-call(s32[1]{0:T(128)} %bitcast.1.slab_ref.refs_0_, s32[1]{0:T(128)} %bitcast.2.refs_1_, f32[8,128]{1,0:T(8,128)S(1)} %spread.1.refs_2_.loss_ref, bf16[400,128]{1,0:T(8,128)(2,1)S(1)} %collective-permute-done.3.refs_3_.refs_4_, ...), custom_call_target="tpu_custom_call" | custom-call | flops 1000000000 | tf_op jit(solution)/shard_map/early/pallas_call | solution.py:296
  13.0 0.4 %collective-permute-done.6.refs_5_.refs_8_ = bf16[400,128]{1,0:T(8,128)(2,1)S(1)} collective-permute-done((bf16[400,128]{1,0:T(8,128)(2,1)S(1)}, bf16[400,128]{1,0:T(8,128)(2,1)S(1)}, u32[]{:S(2)}, u32[]{:S(2)}) %collective-permute-start.6) | collective-permute-done | bytes 102432 | tf_op jit(solution)/shard_map/ppermute | solution.py:316
  13.3 0.4 %collective-permute-done.4.refs_4_.refs_7_ = bf16[400,128]{1,0:T(8,128)(2,1)S(1)} collective-permute-done((bf16[400,128]{1,0:T(8,128)(2,1)S(1)}, bf16[400,128]{1,0:T(8,128)(2,1)S(1)}, u32[]{:S(2)}, u32[]{:S(2)}) %collective-permute-start.4) | collective-permute-done | bytes 102432 | tf_op jit(solution)/shard_map/ppermute | solution.py:316
  13.7 0.6 %late.1 = (f32[216,128]{1,0:T(8,128)S(1)}, f32[232,128]{1,0:T(8,128)S(1)}, f32[392,128]{1,0:T(8,128)S(1)}, f32[392,128]{1,0:T(8,128)S(1)}) custom-call(s32[1]{0:T(128)} %bitcast.1.slab_ref.refs_0_, s32[1]{0:T(128)} %bitcast.2.refs_1_, f32[192,768]{1,0:T(8,128)S(1)} %get-tuple-element.16.refs_2_, f32[192,128]{1,0:T(8,128)S(1)} %get-tuple-element.17.refs_3_, ...), custom_call_target="tpu_custom_call" | custom-call | tf_op jit(solution)/shard_map/late/pallas_call | solution.py:296
  14.3 1.6 %collective-permute-start.9 = (f16[392,128]{1,0:T(8,128)(2,1)S(1)}, f16[392,128]{1,0:T(8,128)(2,1)S(1)}, u32[]{:S(2)}, u32[]{:S(2)}) collective-permute-start(f16[392,128]{1,0:T(8,128)(2,1)S(1)} %convert_element_type.33), channel_id=1, source_target_pairs={{0,16},{4,6},{1,17},{5,7},{2,18},{6,4},{3,19},{7,5},{8,24},{12,14}... | collective-permute-start | bytes 301064 | tf_op jit(solution)/shard_map/ppermute | solution.py:393
  15.9 1.5 %collective-permute-start.10 = (f16[392,128]{1,0:T(8,128)(2,1)S(1)}, f16[392,128]{1,0:T(8,128)(2,1)S(1)}, u32[]{:S(2)}, u32[]{:S(2)}) collective-permute-start(f16[392,128]{1,0:T(8,128)(2,1)S(1)} %convert_element_type.35), channel_id=1, source_target_pairs={{0,24},{4,7},{1,25},{5,6},{2,26},{6,5},{3,27},{7,4},{8,16},{12,15}... | collective-permute-start | bytes 301064 | tf_op jit(solution)/shard_map/ppermute | solution.py:393
  17.4 0.6 %collective-permute-start.13 = (f16[216,128]{1,0:T(8,128)(2,1)S(1)}, f16[216,128]{1,0:T(8,128)(2,1)S(1)}, u32[]{:S(2)}, u32[]{:S(2)}) collective-permute-start(f16[216,128]{1,0:T(8,128)(2,1)S(1)} %convert_element_type.40), channel_id=1, source_target_pairs={{0,8},{4,5},{1,9},{5,4},{2,10},{6,7},{3,11},{7,6},{8,0},{12,13},{9... | collective-permute-start | bytes 165896 | tf_op jit(solution)/shard_map/ppermute | solution.py:393
  18.0 0.9 %collective-permute-start.14 = (f16[232,128]{1,0:T(8,128)(2,1)S(1)}, f16[232,128]{1,0:T(8,128)(2,1)S(1)}, u32[]{:S(2)}, u32[]{:S(2)}) collective-permute-start(f16[232,128]{1,0:T(8,128)(2,1)S(1)} %convert_element_type.42), channel_id=1, source_target_pairs={{0,12},{4,1},{1,13},{5,0},{2,14},{6,3},{3,15},{7,2},{8,4},{12,9},{... | collective-permute-start | bytes 178184 | tf_op jit(solution)/shard_map/ppermute | solution.py:393
  18.9 0.5 %own.1.own_ref = f32[64,768]{1,0:T(8,128)S(1)} custom-call(s32[1]{0:T(128)} %bitcast.1.slab_ref.refs_0_, s32[1]{0:T(128)} %bitcast.2.refs_1_, bf16[400,128]{1,0:T(8,128)(2,1)S(1)} %get-tuple-element.14.refs_2_, bf16[400,128]{1,0:T(8,128)(2,1)S(1)} %get-tuple-element.15.refs_3_.refs_6_, bf16[400,128]{1,0:T(8,128)(2,1)S(1)} %collective-permute-done.4.refs_4_.refs_7_, ...), custom_call_target="tpu_custom_call" | custom-call | flops 1000000000 | tf_op jit(solution)/shard_map/own/pallas_call | solution.py:296
  19.4 0.0 collective-permute-done.9
  19.5 0.6 %collective-permute-start.11 = (f16[208,128]{1,0:T(8,128)(2,1)S(1)}, f16[208,128]{1,0:T(8,128)(2,1)S(1)}, u32[]{:S(2)}, u32[]{:S(2)}) collective-permute-start(f16[208,128]{1,0:T(8,128)(2,1)S(1)} %convert_element_type.37), channel_id=1, source_target_pairs={{0,4},{4,0},{1,5},{5,1},{2,6},{6,2},{3,7},{7,3},{8,12},{12,8},{9,1... | collective-permute-start | bytes 159752 | tf_op jit(solution)/shard_map/ppermute | solution.py:316
  20.1 1.4 %collective-permute-done.10 = f16[392,128]{1,0:T(8,128)(2,1)S(1)} collective-permute-done((f16[392,128]{1,0:T(8,128)(2,1)S(1)}, f16[392,128]{1,0:T(8,128)(2,1)S(1)}, u32[]{:S(2)}, u32[]{:S(2)}) %collective-permute-start.10) | collective-permute-done | bytes 100384 | tf_op jit(solution)/shard_map/ppermute | solution.py:393
  21.5 0.4 %collective-permute-start.12 = (f16[200,128]{1,0:T(8,128)(2,1)S(1)}, f16[200,128]{1,0:T(8,128)(2,1)S(1)}, u32[]{:S(2)}, u32[]{:S(2)}) collective-permute-start(f16[200,128]{1,0:T(8,128)(2,1)S(1)} %slice.4), channel_id=1, source_target_pairs={{0,4},{4,0},{1,5},{5,1},{2,6},{6,2},{3,7},{7,3},{8,12},{12,8},{9,1... | collective-permute-start | bytes 153608 | tf_op jit(solution)/shard_map/ppermute | solution.py:316
  22.0 0.0 collective-permute-done.13
  22.0 0.7 %collective-permute-done.14 = f16[232,128]{1,0:T(8,128)(2,1)S(1)} collective-permute-done((f16[232,128]{1,0:T(8,128)(2,1)S(1)}, f16[232,128]{1,0:T(8,128)(2,1)S(1)}, u32[]{:S(2)}, u32[]{:S(2)}) %collective-permute-start.14) | collective-permute-done | bytes 59424 | tf_op jit(solution)/shard_map/ppermute | solution.py:393
  22.7 0.1 collective-permute-done.12
  22.9 0.0 collective-permute-done.11
  22.9 0.1 end.1
  23.0 0.7 %broadcast_select_fusion = (f32[32,768]{1,0:T(8,128)}, f32[32,768]{1,0:T(8,128)}) fusion(f32[32,768]{1,0:T(8,128)S(1)} %get-tuple-element.25, f32[32,768]{1,0:T(8,128)S(1)} %get-tuple-element.24, pred[]{:T(512)S(6)} %eq.2), kind=kLoop, calls=%fused_computation | loop fusion | flops 49152 | bytes 393217 | tf_op jit(solution)/shard_map/jit(_where)/select_n | solution.py:409
  (15 shorter events, 0.2 us)
Async XLA Ops:
  0.6 2.0 %collective-permute-start.2 = (f32[32]{0:T(128)}, f32[32]{0:T(128)S(1)}, u32[]{:S(2)}, u32[]{:S(2)}) collective-permute-start(f32[32]{0:T(128)} %param.7), channel_id=1, source_target_pairs={{0,4},{4,0},{1,5},{5,1},{2,6},{6,2},{3,7},{7,3},{8,12},{12,8},{9,1... | collective-permute-start | bytes 392 | tf_op jit(solution)/shard_map/ppermute | solution.py:316
  1.1 1.5 %collective-permute-start = (bf16[32,768]{1,0:T(8,128)(2,1)}, bf16[32,768]{1,0:T(8,128)(2,1)S(1)}, u32[]{:S(2)}, u32[]{:S(2)}) collective-permute-start(bf16[32,768]{1,0:T(8,128)(2,1)} %param.5), channel_id=1, source_target_pairs={{0,4},{4,0},{1,5},{5,1},{2,6},{6,2},{3,7},{7,3},{8,12},{12,8},{9,1... | collective-permute-start | bytes 147464 | tf_op jit(solution)/shard_map/ppermute | solution.py:316
  1.2 1.5 %collective-permute-start.1 = (bf16[32,768]{1,0:T(8,128)(2,1)}, bf16[32,768]{1,0:T(8,128)(2,1)S(1)}, u32[]{:S(2)}, u32[]{:S(2)}) collective-permute-start(bf16[32,768]{1,0:T(8,128)(2,1)} %param.6), channel_id=1, source_target_pairs={{0,4},{4,0},{1,5},{5,1},{2,6},{6,2},{3,7},{7,3},{8,12},{12,8},{9,1... | collective-permute-start | bytes 147464 | tf_op jit(solution)/shard_map/ppermute | solution.py:316
  1.7 0.9 %copy-start = (f32[256]{0:T(256)S(1)}, f32[256]{0:T(256)}, u32[]{:S(2)}) copy-start(f32[256]{0:T(256)} %param.8) | copy-start | bytes 3076
  1.7 0.9 %copy-start.1 = (f32[32]{0:T(128)S(1)}, f32[32]{0:T(128)}, u32[]{:S(2)}) copy-start(f32[32]{0:T(128)} %param.7) | copy-start | bytes 388
  2.9 6.5 %collective-permute-start.7 = (bf16[400,128]{1,0:T(8,128)(2,1)S(1)}, bf16[400,128]{1,0:T(8,128)(2,1)S(1)}, u32[]{:S(2)}, u32[]{:S(2)}) collective-permute-start(bf16[400,128]{1,0:T(8,128)(2,1)S(1)} %get-tuple-element.14.refs_2_), channel_id=1, source_target_pairs={{24,0},{7,4},{25,1},{6,5},{26,2},{5,6},{27,3},{4,7},{16,8},{15,12}... | collective-permute-start | bytes 307208 | tf_op jit(solution)/shard_map/ppermute | solution.py:348
  6.7 4.7 %collective-permute-start.5 = (bf16[400,128]{1,0:T(8,128)(2,1)S(1)}, bf16[400,128]{1,0:T(8,128)(2,1)S(1)}, u32[]{:S(2)}, u32[]{:S(2)}) collective-permute-start(bf16[400,128]{1,0:T(8,128)(2,1)S(1)} %get-tuple-element.14.refs_2_), channel_id=1, source_target_pairs={{16,0},{6,4},{17,1},{7,5},{18,2},{4,6},{19,3},{5,7},{24,8},{14,12}... | collective-permute-start | bytes 307208 | tf_op jit(solution)/shard_map/ppermute | solution.py:348
  7.3 5.1 %collective-permute-start.3 = (bf16[400,128]{1,0:T(8,128)(2,1)S(1)}, bf16[400,128]{1,0:T(8,128)(2,1)S(1)}, u32[]{:S(2)}, u32[]{:S(2)}) collective-permute-start(bf16[400,128]{1,0:T(8,128)(2,1)S(1)} %get-tuple-element.14.refs_2_), channel_id=1, source_target_pairs={{8,0},{5,4},{9,1},{4,5},{10,2},{7,6},{11,3},{6,7},{0,8},{13,12},{1... | collective-permute-start | bytes 307208 | tf_op jit(solution)/shard_map/ppermute | solution.py:348
  9.4 3.0 %collective-permute-start.8 = (bf16[400,128]{1,0:T(8,128)(2,1)S(1)}, bf16[400,128]{1,0:T(8,128)(2,1)S(1)}, u32[]{:S(2)}, u32[]{:S(2)}) collective-permute-start(bf16[400,128]{1,0:T(8,128)(2,1)S(1)} %collective-permute-done.7.refs_5_.refs_6_), channel_id=1, source_target_pairs={{0,4},{4,0},{1,5},{5,1},{2,6},{6,2},{3,7},{7,3},{8,12},{12,8},{9,1... | collective-permute-start | bytes 307208 | tf_op jit(solution)/shard_map/ppermute | solution.py:316
  11.4 1.9 %collective-permute-start.6 = (bf16[400,128]{1,0:T(8,128)(2,1)S(1)}, bf16[400,128]{1,0:T(8,128)(2,1)S(1)}, u32[]{:S(2)}, u32[]{:S(2)}) collective-permute-start(bf16[400,128]{1,0:T(8,128)(2,1)S(1)} %collective-permute-done.5.refs_4_.refs_5_), channel_id=1, source_target_pairs={{0,4},{4,0},{1,5},{5,1},{2,6},{6,2},{3,7},{7,3},{8,12},{12,8},{9,1... | collective-permute-start | bytes 307208 | tf_op jit(solution)/shard_map/ppermute | solution.py:316
  12.4 1.3 %collective-permute-start.4 = (bf16[400,128]{1,0:T(8,128)(2,1)S(1)}, bf16[400,128]{1,0:T(8,128)(2,1)S(1)}, u32[]{:S(2)}, u32[]{:S(2)}) collective-permute-start(bf16[400,128]{1,0:T(8,128)(2,1)S(1)} %collective-permute-done.3.refs_3_.refs_4_), channel_id=1, source_target_pairs={{0,4},{4,0},{1,5},{5,1},{2,6},{6,2},{3,7},{7,3},{8,12},{12,8},{9,1... | collective-permute-start | bytes 307208 | tf_op jit(solution)/shard_map/ppermute | solution.py:316
  14.3 5.1 %collective-permute-start.9 = (f16[392,128]{1,0:T(8,128)(2,1)S(1)}, f16[392,128]{1,0:T(8,128)(2,1)S(1)}, u32[]{:S(2)}, u32[]{:S(2)}) collective-permute-start(f16[392,128]{1,0:T(8,128)(2,1)S(1)} %convert_element_type.33), channel_id=1, source_target_pairs={{0,16},{4,6},{1,17},{5,7},{2,18},{6,4},{3,19},{7,5},{8,24},{12,14}... | collective-permute-start | bytes 301064 | tf_op jit(solution)/shard_map/ppermute | solution.py:393
  15.9 5.6 %collective-permute-start.10 = (f16[392,128]{1,0:T(8,128)(2,1)S(1)}, f16[392,128]{1,0:T(8,128)(2,1)S(1)}, u32[]{:S(2)}, u32[]{:S(2)}) collective-permute-start(f16[392,128]{1,0:T(8,128)(2,1)S(1)} %convert_element_type.35), channel_id=1, source_target_pairs={{0,24},{4,7},{1,25},{5,6},{2,26},{6,5},{3,27},{7,4},{8,16},{12,15}... | collective-permute-start | bytes 301064 | tf_op jit(solution)/shard_map/ppermute | solution.py:393
  17.4 4.5 %collective-permute-start.13 = (f16[216,128]{1,0:T(8,128)(2,1)S(1)}, f16[216,128]{1,0:T(8,128)(2,1)S(1)}, u32[]{:S(2)}, u32[]{:S(2)}) collective-permute-start(f16[216,128]{1,0:T(8,128)(2,1)S(1)} %convert_element_type.40), channel_id=1, source_target_pairs={{0,8},{4,5},{1,9},{5,4},{2,10},{6,7},{3,11},{7,6},{8,0},{12,13},{9... | collective-permute-start | bytes 165896 | tf_op jit(solution)/shard_map/ppermute | solution.py:393
  18.0 4.6 %collective-permute-start.14 = (f16[232,128]{1,0:T(8,128)(2,1)S(1)}, f16[232,128]{1,0:T(8,128)(2,1)S(1)}, u32[]{:S(2)}, u32[]{:S(2)}) collective-permute-start(f16[232,128]{1,0:T(8,128)(2,1)S(1)} %convert_element_type.42), channel_id=1, source_target_pairs={{0,12},{4,1},{1,13},{5,0},{2,14},{6,3},{3,15},{7,2},{8,4},{12,9},{... | collective-permute-start | bytes 178184 | tf_op jit(solution)/shard_map/ppermute | solution.py:393
  19.5 3.3 %collective-permute-start.11 = (f16[208,128]{1,0:T(8,128)(2,1)S(1)}, f16[208,128]{1,0:T(8,128)(2,1)S(1)}, u32[]{:S(2)}, u32[]{:S(2)}) collective-permute-start(f16[208,128]{1,0:T(8,128)(2,1)S(1)} %convert_element_type.37), channel_id=1, source_target_pairs={{0,4},{4,0},{1,5},{5,1},{2,6},{6,2},{3,7},{7,3},{8,12},{12,8},{9,1... | collective-permute-start | bytes 159752 | tf_op jit(solution)/shard_map/ppermute | solution.py:316
  21.5 1.3 %collective-permute-start.12 = (f16[200,128]{1,0:T(8,128)(2,1)S(1)}, f16[200,128]{1,0:T(8,128)(2,1)S(1)}, u32[]{:S(2)}, u32[]{:S(2)}) collective-permute-start(f16[200,128]{1,0:T(8,128)(2,1)S(1)} %slice.4), channel_id=1, source_target_pairs={{0,4},{4,0},{1,5},{5,1},{2,6},{6,2},{3,7},{7,3},{8,12},{12,8},{9,1... | collective-permute-start | bytes 153608 | tf_op jit(solution)/shard_map/ppermute | solution.py:316

commit v9 on v8

--- a/solution.py
+++ b/solution.py
@@ -121,10 +121,14 @@
     return jnp.concatenate(pieces, axis=1)[:, : len(norms) * rows]
 
 
+def mark_kernel(slab_ref, out_ref):
+    out_ref[...] = jnp.full(out_ref.shape, slab_ref[0], jnp.int32)
+
+
 def pack_kernel(
-    slab_ref, role_ref, other_ref, got_q_ref, got_p_ref, norm_ref, got_norm_ref, a_ref, b_ref
+    slab_ref, _, q_ref, p_ref, norm_ref, got_q_ref, got_p_ref, got_norm_ref, a_ref, b_ref
 ):
-    rows = role_ref.shape[0]
+    rows = q_ref.shape[0]
     slab = slab_ref[0]
     pick = functools.partial(jnp.where, (slab & 1) == 1)
     own_q = column(norm_ref[...], 0, rows)
@@ -133,12 +137,12 @@
     got_p = column(norm_ref[...], (1 + (slab ^ 1)) * rows, rows)
     write_block(
         a_ref,
-        (role_ref[...], pick(got_q_ref[...], got_p_ref[...])),
+        (pick(q_ref[...], p_ref[...]), pick(got_q_ref[...], got_p_ref[...])),
         (pick(own_q, own_p), pick(got_q, got_p)),
     )
     write_block(
         b_ref,
-        (pick(got_p_ref[...], got_q_ref[...]), other_ref[...]),
+        (pick(got_p_ref[...], got_q_ref[...]), pick(p_ref[...], q_ref[...])),
         (pick(got_p, got_q), pick(own_p, own_q)),
     )
 
@@ -316,16 +320,20 @@
         return lax.ppermute(block, AXES, plan.core_pairs())
 
     packed = jax.ShapeDtypeStruct((chunk_rows + NORM_ROWS, LANES), jnp.bfloat16)
+    (mark,) = call(
+        mark_kernel, "mark", (slab,), (), [jax.ShapeDtypeStruct((8, LANES), jnp.int32)], 1, flops=4*10**9
+    )
     mine, others = call(
         pack_kernel,
         "pack",
         (slab,),
         (
-            jnp.where(core == 1, queries, passages),
-            jnp.where(core == 1, passages, queries),
+            mark,
+            queries,
+            passages,
+            jnp.concatenate([query_lognorm, passage_lognorm]).reshape(1, -1),
             swapped(queries),
             swapped(passages),
-            jnp.concatenate([query_lognorm, passage_lognorm]).reshape(1, -1),
             swapped(query_lognorm).reshape(1, -1),
         ),
         [packed, packed],

time: 23.8 us -> 23.7 us (level)
  other arithmetic: 1.77 us -> 0.91 us
  local copies, waits for them, and re-layouts: 0.03 us -> 0.69 us
    select_n x1 -> x0, other arithmetic: 0.86 us -> none  [local(): jnp.where(core == 1, passages, queries)]
    unnamed x4 -> x8, local copies, waits for them, and re-layouts: 0.01 us -> 0.67 us
    pallas_call x7 -> x8, Pallas kernels: 1.85 us -> 1.83 us  [call(): pl.pallas_call(kernel, out_shape=out_shape, in_specs=[SMEM] * len(scalars...]
  transfers between devices with their start and end apart: 15 -> 15, of which waited for: 8 -> 7; matrix products, arithmetic and copies ran while one was open for 5% -> 1% of each run, Pallas kernels for 5% -> 5%
where the time goes in v9:
time: 23.7 us; the launch traced here: 23.5 us
  starting transfers between devices  12.7 us (54%)
  waiting for transfers between devices  5.91 us (25%)
  Pallas kernels  1.83 us (8%)
  between operations  1.45 us (6%)
  other arithmetic  0.91 us (4%)
  local copies, waits for them, and re-layouts  0.69 us (3%)
    ppermute x4, starting transfers between devices, crossed(): lax.ppermute(partial.astype(jnp.float16), AXES, plan.group_pairs(turn, ac...  4.71 us
    ppermute x3, starting transfers between devices, local(): a_parts.append(lax.ppermute(mine, AXES, back))  4.45 us
    ppermute x8, starting transfers between devices, swapped(): return lax.ppermute(block, AXES, plan.core_pairs())  3.58 us
    ppermute x3, waiting for transfers between devices, local(): a_parts.append(lax.ppermute(mine, AXES, back))  2.77 us
    ppermute x4, waiting for transfers between devices, crossed(): lax.ppermute(partial.astype(jnp.float16), AXES, plan.group_pairs(turn, ac...  2.16 us
    pallas_call x8, Pallas kernels, call(): pl.pallas_call(kernel, out_shape=out_shape, in_specs=[SMEM] * len(scalars...  1.83 us
    ppermute x8, waiting for transfers between devices, swapped(): return lax.ppermute(block, AXES, plan.core_pairs())  0.98 us
    select_n x1, other arithmetic, local(): return (jnp.where(core == 1, keep, got), jnp.where(core == 1, got, keep))  0.69 us
  transfers between devices with their start and end apart: 15, of which 7 were waited for; matrix products, arithmetic and copies ran while one was open for 1% of the time, Pallas kernels for 5%

profile of v9, /device:TPU:0, one launch (start us, length us, event | category | flops | bytes accessed | tf_op | source)
XLA Modules:
  0.0 23.5 jit_solution(10678272729726560417)
XLA Ops:
  0.6 0.5 %collective-permute-start = (bf16[32,768]{1,0:T(8,128)(2,1)}, bf16[32,768]{1,0:T(8,128)(2,1)S(1)}, u32[]{:S(2)}, u32[]{:S(2)}) collective-permute-start(bf16[32,768]{1,0:T(8,128)(2,1)} %q_ref.1), channel_id=1, source_target_pairs={{0,4},{4,0},{1,5},{5,1},{2,6},{6,2},{3,7},{7,3},{8,12},{12,8},{9,1... | collective-permute-start | bytes 147464 | tf_op jit(solution)/shard_map/ppermute | solution.py:320
  1.1 0.1 collective-permute-start.1
  1.2 0.4 %collective-permute-start.2 = (f32[32]{0:T(128)}, f32[32]{0:T(128)S(1)}, u32[]{:S(2)}, u32[]{:S(2)}) collective-permute-start(f32[32]{0:T(128)} %param.7), channel_id=1, source_target_pairs={{0,4},{4,0},{1,5},{5,1},{2,6},{6,2},{3,7},{7,3},{8,12},{12,8},{9,1... | collective-permute-start | bytes 392 | tf_op jit(solution)/shard_map/ppermute | solution.py:320
  1.7 0.0 copy-start.2
  1.7 0.0 copy-start.3
  1.7 0.0 copy-start
  1.7 0.0 copy-start.1
  1.7 0.7 %copy-done.2 = f32[256]{0:T(256)S(1)} copy-done((f32[256]{0:T(256)S(1)}, f32[256]{0:T(256)}, u32[]{:S(2)}) %copy-start.2) | copy-done | bytes 1048
  2.3 0.0 copy-done.3
  2.3 0.1 pad_maximum_fusion
  2.4 0.2 collective-permute-done.2
  2.6 0.0 collective-permute-done.got_q_ref
  2.6 0.0 collective-permute-done.1.got_p_ref
  2.6 0.0 copy-done
  2.6 0.0 copy-done.1
  2.6 0.1 pack.1
  2.8 3.8 %collective-permute-start.7 = (bf16[400,128]{1,0:T(8,128)(2,1)S(1)}, bf16[400,128]{1,0:T(8,128)(2,1)S(1)}, u32[]{:S(2)}, u32[]{:S(2)}) collective-permute-start(bf16[400,128]{1,0:T(8,128)(2,1)S(1)} %get-tuple-element.14.refs_2_), channel_id=1, source_target_pairs={{24,0},{7,4},{25,1},{6,5},{26,2},{5,6},{27,3},{4,7},{16,8},{15,12}... | collective-permute-start | bytes 307208 | tf_op jit(solution)/shard_map/ppermute | solution.py:356
  6.6 0.5 %collective-permute-start.3 = (bf16[400,128]{1,0:T(8,128)(2,1)S(1)}, bf16[400,128]{1,0:T(8,128)(2,1)S(1)}, u32[]{:S(2)}, u32[]{:S(2)}) collective-permute-start(bf16[400,128]{1,0:T(8,128)(2,1)S(1)} %get-tuple-element.14.refs_2_), channel_id=1, source_target_pairs={{8,0},{5,4},{9,1},{4,5},{10,2},{7,6},{11,3},{6,7},{0,8},{13,12},{1... | collective-permute-start | bytes 307208 | tf_op jit(solution)/shard_map/ppermute | solution.py:356
  7.1 0.1 collective-permute-start.5
  7.2 2.0 %collective-permute-done.7.refs_5_.refs_6_ = bf16[400,128]{1,0:T(8,128)(2,1)S(1)} collective-permute-done((bf16[400,128]{1,0:T(8,128)(2,1)S(1)}, bf16[400,128]{1,0:T(8,128)(2,1)S(1)}, u32[]{:S(2)}, u32[]{:S(2)}) %collective-permute-start.7) | collective-permute-done | bytes 102432 | tf_op jit(solution)/shard_map/ppermute | solution.py:356
  9.2 0.6 %collective-permute-start.8 = (bf16[400,128]{1,0:T(8,128)(2,1)S(1)}, bf16[400,128]{1,0:T(8,128)(2,1)S(1)}, u32[]{:S(2)}, u32[]{:S(2)}) collective-permute-start(bf16[400,128]{1,0:T(8,128)(2,1)S(1)} %collective-permute-done.7.refs_5_.refs_6_), channel_id=1, source_target_pairs={{0,4},{4,0},{1,5},{5,1},{2,6},{6,2},{3,7},{7,3},{8,12},{12,8},{9,1... | collective-permute-start | bytes 307208 | tf_op jit(solution)/shard_map/ppermute | solution.py:320
  10.5 0.8 %collective-permute-done.3.refs_3_.refs_4_ = bf16[400,128]{1,0:T(8,128)(2,1)S(1)} collective-permute-done((bf16[400,128]{1,0:T(8,128)(2,1)S(1)}, bf16[400,128]{1,0:T(8,128)(2,1)S(1)}, u32[]{:S(2)}, u32[]{:S(2)}) %collective-permute-start.3) | collective-permute-done | bytes 102432 | tf_op jit(solution)/shard_map/ppermute | solution.py:356
  11.2 1.0 %collective-permute-start.4 = (bf16[400,128]{1,0:T(8,128)(2,1)S(1)}, bf16[400,128]{1,0:T(8,128)(2,1)S(1)}, u32[]{:S(2)}, u32[]{:S(2)}) collective-permute-start(bf16[400,128]{1,0:T(8,128)(2,1)S(1)} %collective-permute-done.3.refs_3_.refs_4_), channel_id=1, source_target_pairs={{0,4},{4,0},{1,5},{5,1},{2,6},{6,2},{3,7},{7,3},{8,12},{12,8},{9,1... | collective-permute-start | bytes 307208 | tf_op jit(solution)/shard_map/ppermute | solution.py:320
  12.3 0.0 collective-permute-done.5.refs_4_.refs_5_
  12.3 0.0 collective-permute-start.6
  12.3 0.0 collective-permute-done.8.refs_6_.refs_7_
  12.3 0.5 %early.1 = (f32[192,768]{1,0:T(8,128)S(1)}, f32[192,128]{1,0:T(8,128)S(1)}) custom-call(s32[1]{0:T(128)} %bitcast.1.slab_ref.refs_0_, s32[1]{0:T(128)} %bitcast.2.refs_1_, f32[8,128]{1,0:T(8,128)S(1)} %spread.1.refs_2_.loss_ref, bf16[400,128]{1,0:T(8,128)(2,1)S(1)} %collective-permute-done.3.refs_3_.refs_4_, ...), custom_call_target="tpu_custom_call" | custom-call | flops 1000000000 | tf_op jit(solution)/shard_map/early/pallas_call | solution.py:300
  12.8 0.4 %collective-permute-done.4.refs_4_.refs_7_ = bf16[400,128]{1,0:T(8,128)(2,1)S(1)} collective-permute-done((bf16[400,128]{1,0:T(8,128)(2,1)S(1)}, bf16[400,128]{1,0:T(8,128)(2,1)S(1)}, u32[]{:S(2)}, u32[]{:S(2)}) %collective-permute-start.4) | collective-permute-done | bytes 102432 | tf_op jit(solution)/shard_map/ppermute | solution.py:320
  13.2 0.4 %collective-permute-done.6.refs_5_.refs_8_ = bf16[400,128]{1,0:T(8,128)(2,1)S(1)} collective-permute-done((bf16[400,128]{1,0:T(8,128)(2,1)S(1)}, bf16[400,128]{1,0:T(8,128)(2,1)S(1)}, u32[]{:S(2)}, u32[]{:S(2)}) %collective-permute-start.6) | collective-permute-done | bytes 102432 | tf_op jit(solution)/shard_map/ppermute | solution.py:320
  13.6 0.6 %late.1 = (f32[216,128]{1,0:T(8,128)S(1)}, f32[232,128]{1,0:T(8,128)S(1)}, f32[392,128]{1,0:T(8,128)S(1)}, f32[392,128]{1,0:T(8,128)S(1)}) custom-call(s32[1]{0:T(128)} %bitcast.1.slab_ref.refs_0_, s32[1]{0:T(128)} %bitcast.2.refs_1_, f32[192,768]{1,0:T(8,128)S(1)} %get-tuple-element.16.refs_2_, f32[192,128]{1,0:T(8,128)S(1)} %get-tuple-element.17.refs_3_, ...), custom_call_target="tpu_custom_call" | custom-call | tf_op jit(solution)/shard_map/late/pallas_call | solution.py:300
  14.2 1.6 %collective-permute-start.9 = (f16[392,128]{1,0:T(8,128)(2,1)S(1)}, f16[392,128]{1,0:T(8,128)(2,1)S(1)}, u32[]{:S(2)}, u32[]{:S(2)}) collective-permute-start(f16[392,128]{1,0:T(8,128)(2,1)S(1)} %convert_element_type.33), channel_id=1, source_target_pairs={{0,16},{4,6},{1,17},{5,7},{2,18},{6,4},{3,19},{7,5},{8,24},{12,14}... | collective-permute-start | bytes 301064 | tf_op jit(solution)/shard_map/ppermute | solution.py:401
  15.8 1.5 %collective-permute-start.10 = (f16[392,128]{1,0:T(8,128)(2,1)S(1)}, f16[392,128]{1,0:T(8,128)(2,1)S(1)}, u32[]{:S(2)}, u32[]{:S(2)}) collective-permute-start(f16[392,128]{1,0:T(8,128)(2,1)S(1)} %convert_element_type.35), channel_id=1, source_target_pairs={{0,24},{4,7},{1,25},{5,6},{2,26},{6,5},{3,27},{7,4},{8,16},{12,15}... | collective-permute-start | bytes 301064 | tf_op jit(solution)/shard_map/ppermute | solution.py:401
  17.3 0.6 %collective-permute-start.13 = (f16[216,128]{1,0:T(8,128)(2,1)S(1)}, f16[216,128]{1,0:T(8,128)(2,1)S(1)}, u32[]{:S(2)}, u32[]{:S(2)}) collective-permute-start(f16[216,128]{1,0:T(8,128)(2,1)S(1)} %convert_element_type.40), channel_id=1, source_target_pairs={{0,8},{4,5},{1,9},{5,4},{2,10},{6,7},{3,11},{7,6},{8,0},{12,13},{9... | collective-permute-start | bytes 165896 | tf_op jit(solution)/shard_map/ppermute | solution.py:401
  17.9 1.0 %collective-permute-start.14 = (f16[232,128]{1,0:T(8,128)(2,1)S(1)}, f16[232,128]{1,0:T(8,128)(2,1)S(1)}, u32[]{:S(2)}, u32[]{:S(2)}) collective-permute-start(f16[232,128]{1,0:T(8,128)(2,1)S(1)} %convert_element_type.42), channel_id=1, source_target_pairs={{0,12},{4,1},{1,13},{5,0},{2,14},{6,3},{3,15},{7,2},{8,4},{12,9},{... | collective-permute-start | bytes 178184 | tf_op jit(solution)/shard_map/ppermute | solution.py:401
  18.9 0.5 %own.1.own_ref = f32[64,768]{1,0:T(8,128)S(1)} custom-call(s32[1]{0:T(128)} %bitcast.1.slab_ref.refs_0_, s32[1]{0:T(128)} %bitcast.2.refs_1_, bf16[400,128]{1,0:T(8,128)(2,1)S(1)} %get-tuple-element.14.refs_2_, bf16[400,128]{1,0:T(8,128)(2,1)S(1)} %get-tuple-element.15.refs_3_.refs_6_, bf16[400,128]{1,0:T(8,128)(2,1)S(1)} %collective-permute-done.4.refs_4_.refs_7_, ...), custom_call_target="tpu_custom_call" | custom-call | flops 1000000000 | tf_op jit(solution)/shard_map/own/pallas_call | solution.py:300
  19.4 0.0 collective-permute-done.9
  19.5 0.5 %collective-permute-start.11 = (f16[208,128]{1,0:T(8,128)(2,1)S(1)}, f16[208,128]{1,0:T(8,128)(2,1)S(1)}, u32[]{:S(2)}, u32[]{:S(2)}) collective-permute-start(f16[208,128]{1,0:T(8,128)(2,1)S(1)} %convert_element_type.37), channel_id=1, source_target_pairs={{0,4},{4,0},{1,5},{5,1},{2,6},{6,2},{3,7},{7,3},{8,12},{12,8},{9,1... | collective-permute-start | bytes 159752 | tf_op jit(solution)/shard_map/ppermute | solution.py:320
  20.0 1.4 %collective-permute-done.10 = f16[392,128]{1,0:T(8,128)(2,1)S(1)} collective-permute-done((f16[392,128]{1,0:T(8,128)(2,1)S(1)}, f16[392,128]{1,0:T(8,128)(2,1)S(1)}, u32[]{:S(2)}, u32[]{:S(2)}) %collective-permute-start.10) | collective-permute-done | bytes 100384 | tf_op jit(solution)/shard_map/ppermute | solution.py:401
  21.4 0.4 %collective-permute-start.12 = (f16[200,128]{1,0:T(8,128)(2,1)S(1)}, f16[200,128]{1,0:T(8,128)(2,1)S(1)}, u32[]{:S(2)}, u32[]{:S(2)}) collective-permute-start(f16[200,128]{1,0:T(8,128)(2,1)S(1)} %slice.4), channel_id=1, source_target_pairs={{0,4},{4,0},{1,5},{5,1},{2,6},{6,2},{3,7},{7,3},{8,12},{12,8},{9,1... | collective-permute-start | bytes 153608 | tf_op jit(solution)/shard_map/ppermute | solution.py:320
  21.8 0.0 collective-permute-done.13
  21.9 0.8 %collective-permute-done.14 = f16[232,128]{1,0:T(8,128)(2,1)S(1)} collective-permute-done((f16[232,128]{1,0:T(8,128)(2,1)S(1)}, f16[232,128]{1,0:T(8,128)(2,1)S(1)}, u32[]{:S(2)}, u32[]{:S(2)}) %collective-permute-start.14) | collective-permute-done | bytes 59424 | tf_op jit(solution)/shard_map/ppermute | solution.py:401
  22.7 0.0 collective-permute-done.12
  22.7 0.0 collective-permute-done.11
  22.8 0.1 end.1
  22.8 0.7 %broadcast_select_fusion = (f32[32,768]{1,0:T(8,128)}, f32[32,768]{1,0:T(8,128)}) fusion(f32[32,768]{1,0:T(8,128)S(1)} %get-tuple-element.25, f32[32,768]{1,0:T(8,128)S(1)} %get-tuple-element.24, pred[]{:T(512)S(6)} %eq.4), kind=kLoop, calls=%fused_computation | loop fusion | flops 49152 | bytes 393217 | tf_op jit(solution)/shard_map/jit(_where)/select_n | solution.py:417
  (16 shorter events, 0.2 us)
Async XLA Ops:
  0.6 2.0 %collective-permute-start = (bf16[32,768]{1,0:T(8,128)(2,1)}, bf16[32,768]{1,0:T(8,128)(2,1)S(1)}, u32[]{:S(2)}, u32[]{:S(2)}) collective-permute-start(bf16[32,768]{1,0:T(8,128)(2,1)} %q_ref.1), channel_id=1, source_target_pairs={{0,4},{4,0},{1,5},{5,1},{2,6},{6,2},{3,7},{7,3},{8,12},{12,8},{9,1... | collective-permute-start | bytes 147464 | tf_op jit(solution)/shard_map/ppermute | solution.py:320
  1.1 1.5 %collective-permute-start.1 = (bf16[32,768]{1,0:T(8,128)(2,1)}, bf16[32,768]{1,0:T(8,128)(2,1)S(1)}, u32[]{:S(2)}, u32[]{:S(2)}) collective-permute-start(bf16[32,768]{1,0:T(8,128)(2,1)} %p_ref.1), channel_id=1, source_target_pairs={{0,4},{4,0},{1,5},{5,1},{2,6},{6,2},{3,7},{7,3},{8,12},{12,8},{9,1... | collective-permute-start | bytes 147464 | tf_op jit(solution)/shard_map/ppermute | solution.py:320
  1.2 1.4 %collective-permute-start.2 = (f32[32]{0:T(128)}, f32[32]{0:T(128)S(1)}, u32[]{:S(2)}, u32[]{:S(2)}) collective-permute-start(f32[32]{0:T(128)} %param.7), channel_id=1, source_target_pairs={{0,4},{4,0},{1,5},{5,1},{2,6},{6,2},{3,7},{7,3},{8,12},{12,8},{9,1... | collective-permute-start | bytes 392 | tf_op jit(solution)/shard_map/ppermute | solution.py:320
  1.7 0.7 %copy-start.2 = (f32[256]{0:T(256)S(1)}, f32[256]{0:T(256)}, u32[]{:S(2)}) copy-start(f32[256]{0:T(256)} %param.8) | copy-start | bytes 3076
  1.7 0.7 %copy-start.3 = (f32[32]{0:T(128)S(1)}, f32[32]{0:T(128)}, u32[]{:S(2)}) copy-start(f32[32]{0:T(128)} %param.7) | copy-start | bytes 388
  1.7 1.0 %copy-start = (bf16[32,768]{1,0:T(8,128)(2,1)S(1)}, bf16[32,768]{1,0:T(8,128)(2,1)}, u32[]{:S(2)}) copy-start(bf16[32,768]{1,0:T(8,128)(2,1)} %q_ref.1) | copy-start | bytes 147460
  1.7 1.0 %copy-start.1 = (bf16[32,768]{1,0:T(8,128)(2,1)S(1)}, bf16[32,768]{1,0:T(8,128)(2,1)}, u32[]{:S(2)}) copy-start(bf16[32,768]{1,0:T(8,128)(2,1)} %p_ref.1) | copy-start | bytes 147460
  2.8 6.5 %collective-permute-start.7 = (bf16[400,128]{1,0:T(8,128)(2,1)S(1)}, bf16[400,128]{1,0:T(8,128)(2,1)S(1)}, u32[]{:S(2)}, u32[]{:S(2)}) collective-permute-start(bf16[400,128]{1,0:T(8,128)(2,1)S(1)} %get-tuple-element.14.refs_2_), channel_id=1, source_target_pairs={{24,0},{7,4},{25,1},{6,5},{26,2},{5,6},{27,3},{4,7},{16,8},{15,12}... | collective-permute-start | bytes 307208 | tf_op jit(solution)/shard_map/ppermute | solution.py:356
  6.6 4.7 %collective-permute-start.3 = (bf16[400,128]{1,0:T(8,128)(2,1)S(1)}, bf16[400,128]{1,0:T(8,128)(2,1)S(1)}, u32[]{:S(2)}, u32[]{:S(2)}) collective-permute-start(bf16[400,128]{1,0:T(8,128)(2,1)S(1)} %get-tuple-element.14.refs_2_), channel_id=1, source_target_pairs={{8,0},{5,4},{9,1},{4,5},{10,2},{7,6},{11,3},{6,7},{0,8},{13,12},{1... | collective-permute-start | bytes 307208 | tf_op jit(solution)/shard_map/ppermute | solution.py:356
  7.1 5.2 %collective-permute-start.5 = (bf16[400,128]{1,0:T(8,128)(2,1)S(1)}, bf16[400,128]{1,0:T(8,128)(2,1)S(1)}, u32[]{:S(2)}, u32[]{:S(2)}) collective-permute-start(bf16[400,128]{1,0:T(8,128)(2,1)S(1)} %get-tuple-element.14.refs_2_), channel_id=1, source_target_pairs={{16,0},{6,4},{17,1},{7,5},{18,2},{4,6},{19,3},{5,7},{24,8},{14,12}... | collective-permute-start | bytes 307208 | tf_op jit(solution)/shard_map/ppermute | solution.py:356
  9.2 3.1 %collective-permute-start.8 = (bf16[400,128]{1,0:T(8,128)(2,1)S(1)}, bf16[400,128]{1,0:T(8,128)(2,1)S(1)}, u32[]{:S(2)}, u32[]{:S(2)}) collective-permute-start(bf16[400,128]{1,0:T(8,128)(2,1)S(1)} %collective-permute-done.7.refs_5_.refs_6_), channel_id=1, source_target_pairs={{0,4},{4,0},{1,5},{5,1},{2,6},{6,2},{3,7},{7,3},{8,12},{12,8},{9,1... | collective-permute-start | bytes 307208 | tf_op jit(solution)/shard_map/ppermute | solution.py:320
  11.2 2.0 %collective-permute-start.4 = (bf16[400,128]{1,0:T(8,128)(2,1)S(1)}, bf16[400,128]{1,0:T(8,128)(2,1)S(1)}, u32[]{:S(2)}, u32[]{:S(2)}) collective-permute-start(bf16[400,128]{1,0:T(8,128)(2,1)S(1)} %collective-permute-done.3.refs_3_.refs_4_), channel_id=1, source_target_pairs={{0,4},{4,0},{1,5},{5,1},{2,6},{6,2},{3,7},{7,3},{8,12},{12,8},{9,1... | collective-permute-start | bytes 307208 | tf_op jit(solution)/shard_map/ppermute | solution.py:320
  12.3 1.3 %collective-permute-start.6 = (bf16[400,128]{1,0:T(8,128)(2,1)S(1)}, bf16[400,128]{1,0:T(8,128)(2,1)S(1)}, u32[]{:S(2)}, u32[]{:S(2)}) collective-permute-start(bf16[400,128]{1,0:T(8,128)(2,1)S(1)} %collective-permute-done.5.refs_4_.refs_5_), channel_id=1, source_target_pairs={{0,4},{4,0},{1,5},{5,1},{2,6},{6,2},{3,7},{7,3},{8,12},{12,8},{9,1... | collective-permute-start | bytes 307208 | tf_op jit(solution)/shard_map/ppermute | solution.py:320
  14.2 5.3 %collective-permute-start.9 = (f16[392,128]{1,0:T(8,128)(2,1)S(1)}, f16[392,128]{1,0:T(8,128)(2,1)S(1)}, u32[]{:S(2)}, u32[]{:S(2)}) collective-permute-start(f16[392,128]{1,0:T(8,128)(2,1)S(1)} %convert_element_type.33), channel_id=1, source_target_pairs={{0,16},{4,6},{1,17},{5,7},{2,18},{6,4},{3,19},{7,5},{8,24},{12,14}... | collective-permute-start | bytes 301064 | tf_op jit(solution)/shard_map/ppermute | solution.py:401
  15.8 5.6 %collective-permute-start.10 = (f16[392,128]{1,0:T(8,128)(2,1)S(1)}, f16[392,128]{1,0:T(8,128)(2,1)S(1)}, u32[]{:S(2)}, u32[]{:S(2)}) collective-permute-start(f16[392,128]{1,0:T(8,128)(2,1)S(1)} %convert_element_type.35), channel_id=1, source_target_pairs={{0,24},{4,7},{1,25},{5,6},{2,26},{6,5},{3,27},{7,4},{8,16},{12,15}... | collective-permute-start | bytes 301064 | tf_op jit(solution)/shard_map/ppermute | solution.py:401
  17.3 4.6 %collective-permute-start.13 = (f16[216,128]{1,0:T(8,128)(2,1)S(1)}, f16[216,128]{1,0:T(8,128)(2,1)S(1)}, u32[]{:S(2)}, u32[]{:S(2)}) collective-permute-start(f16[216,128]{1,0:T(8,128)(2,1)S(1)} %convert_element_type.40), channel_id=1, source_target_pairs={{0,8},{4,5},{1,9},{5,4},{2,10},{6,7},{3,11},{7,6},{8,0},{12,13},{9... | collective-permute-start | bytes 165896 | tf_op jit(solution)/shard_map/ppermute | solution.py:401
  17.9 4.7 %collective-permute-start.14 = (f16[232,128]{1,0:T(8,128)(2,1)S(1)}, f16[232,128]{1,0:T(8,128)(2,1)S(1)}, u32[]{:S(2)}, u32[]{:S(2)}) collective-permute-start(f16[232,128]{1,0:T(8,128)(2,1)S(1)} %convert_element_type.42), channel_id=1, source_target_pairs={{0,12},{4,1},{1,13},{5,0},{2,14},{6,3},{3,15},{7,2},{8,4},{12,9},{... | collective-permute-start | bytes 178184 | tf_op jit(solution)/shard_map/ppermute | solution.py:401
  19.5 3.2 %collective-permute-start.11 = (f16[208,128]{1,0:T(8,128)(2,1)S(1)}, f16[208,128]{1,0:T(8,128)(2,1)S(1)}, u32[]{:S(2)}, u32[]{:S(2)}) collective-permute-start(f16[208,128]{1,0:T(8,128)(2,1)S(1)} %convert_element_type.37), channel_id=1, source_target_pairs={{0,4},{4,0},{1,5},{5,1},{2,6},{6,2},{3,7},{7,3},{8,12},{12,8},{9,1... | collective-permute-start | bytes 159752 | tf_op jit(solution)/shard_map/ppermute | solution.py:320
  21.4 1.3 %collective-permute-start.12 = (f16[200,128]{1,0:T(8,128)(2,1)S(1)}, f16[200,128]{1,0:T(8,128)(2,1)S(1)}, u32[]{:S(2)}, u32[]{:S(2)}) collective-permute-start(f16[200,128]{1,0:T(8,128)(2,1)S(1)} %slice.4), channel_id=1, source_target_pairs={{0,4},{4,0},{1,5},{5,1},{2,6},{6,2},{3,7},{7,3},{8,12},{12,8},{9,1... | collective-permute-start | bytes 153608 | tf_op jit(solution)/shard_map/ppermute | solution.py:320

commit v10 on v9

--- a/solution.py
+++ b/solution.py
@@ -126,7 +126,7 @@
 
 
 def pack_kernel(
-    slab_ref, _, q_ref, p_ref, norm_ref, got_q_ref, got_p_ref, got_norm_ref, a_ref, b_ref
+    other, slab_ref, _, q_ref, p_ref, norm_ref, got_q_ref, got_p_ref, got_norm_ref, out_ref
 ):
     rows = q_ref.shape[0]
     slab = slab_ref[0]
@@ -135,16 +135,18 @@
     got_q = column(got_norm_ref[...], 0, rows)
     own_p = column(norm_ref[...], (1 + slab) * rows, rows)
     got_p = column(norm_ref[...], (1 + (slab ^ 1)) * rows, rows)
-    write_block(
-        a_ref,
-        (pick(q_ref[...], p_ref[...]), pick(got_q_ref[...], got_p_ref[...])),
-        (pick(own_q, own_p), pick(got_q, got_p)),
-    )
-    write_block(
-        b_ref,
-        (pick(got_p_ref[...], got_q_ref[...]), pick(p_ref[...], q_ref[...])),
-        (pick(got_p, got_q), pick(own_p, own_q)),
-    )
+    if other:
+        write_block(
+            out_ref,
+            (pick(got_p_ref[...], got_q_ref[...]), pick(p_ref[...], q_ref[...])),
+            (pick(got_p, got_q), pick(own_p, own_q)),
+        )
+    else:
+        write_block(
+            out_ref,
+            (pick(q_ref[...], p_ref[...]), pick(got_q_ref[...], got_p_ref[...])),
+            (pick(own_q, own_p), pick(got_q, got_p)),
+        )
 
 
 def row_numbers(plan, slab, blk, role, rows, turns, place):
@@ -323,23 +325,19 @@
     (mark,) = call(
         mark_kernel, "mark", (slab,), (), [jax.ShapeDtypeStruct((8, LANES), jnp.int32)], 1, flops=4*10**9
     )
-    mine, others = call(
-        pack_kernel,
-        "pack",
-        (slab,),
-        (
-            mark,
-            queries,
-            passages,
-            jnp.concatenate([query_lognorm, passage_lognorm]).reshape(1, -1),
-            swapped(queries),
-            swapped(passages),
-            swapped(query_lognorm).reshape(1, -1),
-        ),
-        [packed, packed],
-        4,
-    )
-
+    arrays = (
+        mark,
+        queries,
+        passages,
+        jnp.concatenate([query_lognorm, passage_lognorm]).reshape(1, -1),
+        swapped(queries),
+        swapped(passages),
+        swapped(query_lognorm).reshape(1, -1),
+    )
+    (mine,), (others,) = (
+        call(functools.partial(pack_kernel, other), "pack", (slab,), arrays, [packed], 4)
+        for other in (False, True)
+    )
     (loss,) = call(
         spread_kernel,
         "spread",

time: 23.7 us -> 23.7 us (level)
    pallas_call x8 -> x9, Pallas kernels: 1.83 us -> 1.97 us  [call(): pl.pallas_call(kernel, out_shape=out_shape, in_specs=[SMEM] * len(scalars...]
where the time goes in v10:
time: 23.7 us; the launch traced here: 23.5 us
  starting transfers between devices  12.7 us (54%)
  waiting for transfers between devices  5.79 us (24%)
  Pallas kernels  1.97 us (8%)
  between operations  1.44 us (6%)
  other arithmetic  0.91 us (4%)
  local copies, waits for them, and re-layouts  0.69 us (3%)
    ppermute x4, starting transfers between devices, crossed(): lax.ppermute(partial.astype(jnp.float16), AXES, plan.group_pairs(turn, ac...  4.71 us
    ppermute x3, starting transfers between devices, local(): a_parts.append(lax.ppermute(mine, AXES, back))  4.45 us
    ppermute x8, starting transfers between devices, swapped(): return lax.ppermute(block, AXES, plan.core_pairs())  3.58 us
    ppermute x3, waiting for transfers between devices, local(): a_parts.append(lax.ppermute(mine, AXES, back))  2.77 us
    ppermute x4, waiting for transfers between devices, crossed(): lax.ppermute(partial.astype(jnp.float16), AXES, plan.group_pairs(turn, ac...  2.16 us
    pallas_call x9, Pallas kernels, call(): pl.pallas_call(kernel, out_shape=out_shape, in_specs=[SMEM] * len(scalars...  1.97 us
    ppermute x8, waiting for transfers between devices, swapped(): return lax.ppermute(block, AXES, plan.core_pairs())  0.85 us
    select_n x1, other arithmetic, local(): return (jnp.where(core == 1, keep, got), jnp.where(core == 1, got, keep))  0.69 us
  transfers between devices with their start and end apart: 15, of which 7 were waited for; matrix products, arithmetic and copies ran while one was open for 1% of the time, Pallas kernels for 5%

profile of v10, /device:TPU:0, one launch (start us, length us, event | category | flops | bytes accessed | tf_op | source)
XLA Modules:
  0.0 23.5 jit_solution(18422406031503317030)
XLA Ops:
  0.6 0.5 %collective-permute-start = (bf16[32,768]{1,0:T(8,128)(2,1)}, bf16[32,768]{1,0:T(8,128)(2,1)S(1)}, u32[]{:S(2)}, u32[]{:S(2)}) collective-permute-start(bf16[32,768]{1,0:T(8,128)(2,1)} %q_ref.3), channel_id=1, source_target_pairs={{0,4},{4,0},{1,5},{5,1},{2,6},{6,2},{3,7},{7,3},{8,12},{12,8},{9,1... | collective-permute-start | bytes 147464 | tf_op jit(solution)/shard_map/ppermute | solution.py:322
  1.1 0.1 collective-permute-start.1
  1.2 0.4 %collective-permute-start.2 = (f32[32]{0:T(128)}, f32[32]{0:T(128)S(1)}, u32[]{:S(2)}, u32[]{:S(2)}) collective-permute-start(f32[32]{0:T(128)} %param.7), channel_id=1, source_target_pairs={{0,4},{4,0},{1,5},{5,1},{2,6},{6,2},{3,7},{7,3},{8,12},{12,8},{9,1... | collective-permute-start | bytes 392 | tf_op jit(solution)/shard_map/ppermute | solution.py:322
  1.7 0.0 copy-start.2
  1.7 0.0 copy-start.3
  1.7 0.0 copy-start
  1.7 0.0 copy-start.1
  1.7 0.7 %copy-done.2 = f32[256]{0:T(256)S(1)} copy-done((f32[256]{0:T(256)S(1)}, f32[256]{0:T(256)}, u32[]{:S(2)}) %copy-start.2) | copy-done | bytes 1048
  2.3 0.0 copy-done.3
  2.3 0.1 pad_maximum_fusion
  2.4 0.2 collective-permute-done.2
  2.6 0.0 collective-permute-done.got_q_ref
  2.6 0.0 collective-permute-done.1.got_p_ref
  2.6 0.0 copy-done
  2.6 0.0 copy-done.1
  2.6 0.1 pack.2.refs_2_
  2.8 3.8 %collective-permute-start.7 = (bf16[400,128]{1,0:T(8,128)(2,1)S(1)}, bf16[400,128]{1,0:T(8,128)(2,1)S(1)}, u32[]{:S(2)}, u32[]{:S(2)}) collective-permute-start(bf16[400,128]{1,0:T(8,128)(2,1)S(1)} %pack.2.refs_2_), channel_id=1, source_target_pairs={{24,0},{7,4},{25,1},{6,5},{26,2},{5,6},{27,3},{4,7},{16,8},{15,12}... | collective-permute-start | bytes 307208 | tf_op jit(solution)/shard_map/ppermute | solution.py:354
  6.6 0.5 %collective-permute-start.3 = (bf16[400,128]{1,0:T(8,128)(2,1)S(1)}, bf16[400,128]{1,0:T(8,128)(2,1)S(1)}, u32[]{:S(2)}, u32[]{:S(2)}) collective-permute-start(bf16[400,128]{1,0:T(8,128)(2,1)S(1)} %pack.2.refs_2_), channel_id=1, source_target_pairs={{8,0},{5,4},{9,1},{4,5},{10,2},{7,6},{11,3},{6,7},{0,8},{13,12},{1... | collective-permute-start | bytes 307208 | tf_op jit(solution)/shard_map/ppermute | solution.py:354
  7.1 0.1 collective-permute-start.5
  7.2 2.0 %collective-permute-done.7.refs_5_.refs_6_ = bf16[400,128]{1,0:T(8,128)(2,1)S(1)} collective-permute-done((bf16[400,128]{1,0:T(8,128)(2,1)S(1)}, bf16[400,128]{1,0:T(8,128)(2,1)S(1)}, u32[]{:S(2)}, u32[]{:S(2)}) %collective-permute-start.7) | collective-permute-done | bytes 102432 | tf_op jit(solution)/shard_map/ppermute | solution.py:354
  9.2 0.6 %collective-permute-start.8 = (bf16[400,128]{1,0:T(8,128)(2,1)S(1)}, bf16[400,128]{1,0:T(8,128)(2,1)S(1)}, u32[]{:S(2)}, u32[]{:S(2)}) collective-permute-start(bf16[400,128]{1,0:T(8,128)(2,1)S(1)} %collective-permute-done.7.refs_5_.refs_6_), channel_id=1, source_target_pairs={{0,4},{4,0},{1,5},{5,1},{2,6},{6,2},{3,7},{7,3},{8,12},{12,8},{9,1... | collective-permute-start | bytes 307208 | tf_op jit(solution)/shard_map/ppermute | solution.py:322
  10.5 0.8 %collective-permute-done.3.refs_3_.refs_4_ = bf16[400,128]{1,0:T(8,128)(2,1)S(1)} collective-permute-done((bf16[400,128]{1,0:T(8,128)(2,1)S(1)}, bf16[400,128]{1,0:T(8,128)(2,1)S(1)}, u32[]{:S(2)}, u32[]{:S(2)}) %collective-permute-start.3) | collective-permute-done | bytes 102432 | tf_op jit(solution)/shard_map/ppermute | solution.py:354
  11.2 1.0 %collective-permute-start.4 = (bf16[400,128]{1,0:T(8,128)(2,1)S(1)}, bf16[400,128]{1,0:T(8,128)(2,1)S(1)}, u32[]{:S(2)}, u32[]{:S(2)}) collective-permute-start(bf16[400,128]{1,0:T(8,128)(2,1)S(1)} %collective-permute-done.3.refs_3_.refs_4_), channel_id=1, source_target_pairs={{0,4},{4,0},{1,5},{5,1},{2,6},{6,2},{3,7},{7,3},{8,12},{12,8},{9,1... | collective-permute-start | bytes 307208 | tf_op jit(solution)/shard_map/ppermute | solution.py:322
  12.3 0.0 collective-permute-done.5.refs_4_.refs_5_
  12.3 0.0 collective-permute-start.6
  12.3 0.1 pack.3.refs_3_.refs_6_
  12.4 0.0 collective-permute-done.8.refs_6_.refs_7_
  12.4 0.5 %early.1 = (f32[192,768]{1,0:T(8,128)S(1)}, f32[192,128]{1,0:T(8,128)S(1)}) custom-call(s32[1]{0:T(128)} %bitcast.1.slab_ref.refs_0_, s32[1]{0:T(128)} %bitcast.2.refs_1_, f32[8,128]{1,0:T(8,128)S(1)} %spread.1.refs_2_.loss_ref, bf16[400,128]{1,0:T(8,128)(2,1)S(1)} %collective-permute-done.3.refs_3_.refs_4_, ...), custom_call_target="tpu_custom_call" | custom-call | flops 1000000000 | tf_op jit(solution)/shard_map/early/pallas_call | solution.py:302
  13.0 0.2 %collective-permute-done.4.refs_4_.refs_7_ = bf16[400,128]{1,0:T(8,128)(2,1)S(1)} collective-permute-done((bf16[400,128]{1,0:T(8,128)(2,1)S(1)}, bf16[400,128]{1,0:T(8,128)(2,1)S(1)}, u32[]{:S(2)}, u32[]{:S(2)}) %collective-permute-start.4) | collective-permute-done | bytes 102432 | tf_op jit(solution)/shard_map/ppermute | solution.py:322
  13.2 0.4 %collective-permute-done.6.refs_5_.refs_8_ = bf16[400,128]{1,0:T(8,128)(2,1)S(1)} collective-permute-done((bf16[400,128]{1,0:T(8,128)(2,1)S(1)}, bf16[400,128]{1,0:T(8,128)(2,1)S(1)}, u32[]{:S(2)}, u32[]{:S(2)}) %collective-permute-start.6) | collective-permute-done | bytes 102432 | tf_op jit(solution)/shard_map/ppermute | solution.py:322
  13.6 0.6 %late.1 = (f32[216,128]{1,0:T(8,128)S(1)}, f32[232,128]{1,0:T(8,128)S(1)}, f32[392,128]{1,0:T(8,128)S(1)}, f32[392,128]{1,0:T(8,128)S(1)}) custom-call(s32[1]{0:T(128)} %bitcast.1.slab_ref.refs_0_, s32[1]{0:T(128)} %bitcast.2.refs_1_, f32[192,768]{1,0:T(8,128)S(1)} %get-tuple-element.12.refs_2_, f32[192,128]{1,0:T(8,128)S(1)} %get-tuple-element.13.refs_3_, ...), custom_call_target="tpu_custom_call" | custom-call | tf_op jit(solution)/shard_map/late/pallas_call | solution.py:302
  14.2 1.6 %collective-permute-start.9 = (f16[392,128]{1,0:T(8,128)(2,1)S(1)}, f16[392,128]{1,0:T(8,128)(2,1)S(1)}, u32[]{:S(2)}, u32[]{:S(2)}) collective-permute-start(f16[392,128]{1,0:T(8,128)(2,1)S(1)} %convert_element_type.33), channel_id=1, source_target_pairs={{0,16},{4,6},{1,17},{5,7},{2,18},{6,4},{3,19},{7,5},{8,24},{12,14}... | collective-permute-start | bytes 301064 | tf_op jit(solution)/shard_map/ppermute | solution.py:399
  15.8 1.5 %collective-permute-start.10 = (f16[392,128]{1,0:T(8,128)(2,1)S(1)}, f16[392,128]{1,0:T(8,128)(2,1)S(1)}, u32[]{:S(2)}, u32[]{:S(2)}) collective-permute-start(f16[392,128]{1,0:T(8,128)(2,1)S(1)} %convert_element_type.35), channel_id=1, source_target_pairs={{0,24},{4,7},{1,25},{5,6},{2,26},{6,5},{3,27},{7,4},{8,16},{12,15}... | collective-permute-start | bytes 301064 | tf_op jit(solution)/shard_map/ppermute | solution.py:399
  17.3 0.6 %collective-permute-start.13 = (f16[216,128]{1,0:T(8,128)(2,1)S(1)}, f16[216,128]{1,0:T(8,128)(2,1)S(1)}, u32[]{:S(2)}, u32[]{:S(2)}) collective-permute-start(f16[216,128]{1,0:T(8,128)(2,1)S(1)} %convert_element_type.40), channel_id=1, source_target_pairs={{0,8},{4,5},{1,9},{5,4},{2,10},{6,7},{3,11},{7,6},{8,0},{12,13},{9... | collective-permute-start | bytes 165896 | tf_op jit(solution)/shard_map/ppermute | solution.py:399
  17.9 1.0 %collective-permute-start.14 = (f16[232,128]{1,0:T(8,128)(2,1)S(1)}, f16[232,128]{1,0:T(8,128)(2,1)S(1)}, u32[]{:S(2)}, u32[]{:S(2)}) collective-permute-start(f16[232,128]{1,0:T(8,128)(2,1)S(1)} %convert_element_type.42), channel_id=1, source_target_pairs={{0,12},{4,1},{1,13},{5,0},{2,14},{6,3},{3,15},{7,2},{8,4},{12,9},{... | collective-permute-start | bytes 178184 | tf_op jit(solution)/shard_map/ppermute | solution.py:399
  18.9 0.5 %own.1.own_ref = f32[64,768]{1,0:T(8,128)S(1)} custom-call(s32[1]{0:T(128)} %bitcast.1.slab_ref.refs_0_, s32[1]{0:T(128)} %bitcast.2.refs_1_, bf16[400,128]{1,0:T(8,128)(2,1)S(1)} %pack.2.refs_2_, bf16[400,128]{1,0:T(8,128)(2,1)S(1)} %pack.3.refs_3_.refs_6_, bf16[400,128]{1,0:T(8,128)(2,1)S(1)} %collective-permute-done.4.refs_4_.refs_7_, ...), custom_call_target="tpu_custom_call" | custom-call | flops 1000000000 | tf_op jit(solution)/shard_map/own/pallas_call | solution.py:302
  19.4 0.0 collective-permute-done.9
  19.5 0.5 %collective-permute-start.11 = (f16[208,128]{1,0:T(8,128)(2,1)S(1)}, f16[208,128]{1,0:T(8,128)(2,1)S(1)}, u32[]{:S(2)}, u32[]{:S(2)}) collective-permute-start(f16[208,128]{1,0:T(8,128)(2,1)S(1)} %convert_element_type.37), channel_id=1, source_target_pairs={{0,4},{4,0},{1,5},{5,1},{2,6},{6,2},{3,7},{7,3},{8,12},{12,8},{9,1... | collective-permute-start | bytes 159752 | tf_op jit(solution)/shard_map/ppermute | solution.py:322
  20.0 1.4 %collective-permute-done.10 = f16[392,128]{1,0:T(8,128)(2,1)S(1)} collective-permute-done((f16[392,128]{1,0:T(8,128)(2,1)S(1)}, f16[392,128]{1,0:T(8,128)(2,1)S(1)}, u32[]{:S(2)}, u32[]{:S(2)}) %collective-permute-start.10) | collective-permute-done | bytes 100384 | tf_op jit(solution)/shard_map/ppermute | solution.py:399
  21.4 0.4 %collective-permute-start.12 = (f16[200,128]{1,0:T(8,128)(2,1)S(1)}, f16[200,128]{1,0:T(8,128)(2,1)S(1)}, u32[]{:S(2)}, u32[]{:S(2)}) collective-permute-start(f16[200,128]{1,0:T(8,128)(2,1)S(1)} %slice.4), channel_id=1, source_target_pairs={{0,4},{4,0},{1,5},{5,1},{2,6},{6,2},{3,7},{7,3},{8,12},{12,8},{9,1... | collective-permute-start | bytes 153608 | tf_op jit(solution)/shard_map/ppermute | solution.py:322
  21.8 0.0 collective-permute-done.13
  21.9 0.8 %collective-permute-done.14 = f16[232,128]{1,0:T(8,128)(2,1)S(1)} collective-permute-done((f16[232,128]{1,0:T(8,128)(2,1)S(1)}, f16[232,128]{1,0:T(8,128)(2,1)S(1)}, u32[]{:S(2)}, u32[]{:S(2)}) %collective-permute-start.14) | collective-permute-done | bytes 59424 | tf_op jit(solution)/shard_map/ppermute | solution.py:399
  22.7 0.0 collective-permute-done.12
  22.7 0.0 collective-permute-done.11
  22.8 0.1 end.1
  22.8 0.7 %broadcast_select_fusion = (f32[32,768]{1,0:T(8,128)}, f32[32,768]{1,0:T(8,128)}) fusion(f32[32,768]{1,0:T(8,128)S(1)} %get-tuple-element.21, f32[32,768]{1,0:T(8,128)S(1)} %get-tuple-element.20, pred[]{:T(512)S(6)} %eq.4), kind=kLoop, calls=%fused_computation | loop fusion | flops 49152 | bytes 393217 | tf_op jit(solution)/shard_map/jit(_where)/select_n | solution.py:415
  (16 shorter events, 0.2 us)
Async XLA Ops:
  0.6 2.0 %collective-permute-start = (bf16[32,768]{1,0:T(8,128)(2,1)}, bf16[32,768]{1,0:T(8,128)(2,1)S(1)}, u32[]{:S(2)}, u32[]{:S(2)}) collective-permute-start(bf16[32,768]{1,0:T(8,128)(2,1)} %q_ref.3), channel_id=1, source_target_pairs={{0,4},{4,0},{1,5},{5,1},{2,6},{6,2},{3,7},{7,3},{8,12},{12,8},{9,1... | collective-permute-start | bytes 147464 | tf_op jit(solution)/shard_map/ppermute | solution.py:322
  1.1 1.5 %collective-permute-start.1 = (bf16[32,768]{1,0:T(8,128)(2,1)}, bf16[32,768]{1,0:T(8,128)(2,1)S(1)}, u32[]{:S(2)}, u32[]{:S(2)}) collective-permute-start(bf16[32,768]{1,0:T(8,128)(2,1)} %p_ref.3), channel_id=1, source_target_pairs={{0,4},{4,0},{1,5},{5,1},{2,6},{6,2},{3,7},{7,3},{8,12},{12,8},{9,1... | collective-permute-start | bytes 147464 | tf_op jit(solution)/shard_map/ppermute | solution.py:322
  1.2 1.4 %collective-permute-start.2 = (f32[32]{0:T(128)}, f32[32]{0:T(128)S(1)}, u32[]{:S(2)}, u32[]{:S(2)}) collective-permute-start(f32[32]{0:T(128)} %param.7), channel_id=1, source_target_pairs={{0,4},{4,0},{1,5},{5,1},{2,6},{6,2},{3,7},{7,3},{8,12},{12,8},{9,1... | collective-permute-start | bytes 392 | tf_op jit(solution)/shard_map/ppermute | solution.py:322
  1.7 0.7 %copy-start.2 = (f32[256]{0:T(256)S(1)}, f32[256]{0:T(256)}, u32[]{:S(2)}) copy-start(f32[256]{0:T(256)} %param.8) | copy-start | bytes 3076
  1.7 0.7 %copy-start.3 = (f32[32]{0:T(128)S(1)}, f32[32]{0:T(128)}, u32[]{:S(2)}) copy-start(f32[32]{0:T(128)} %param.7) | copy-start | bytes 388
  1.7 1.0 %copy-start = (bf16[32,768]{1,0:T(8,128)(2,1)S(1)}, bf16[32,768]{1,0:T(8,128)(2,1)}, u32[]{:S(2)}) copy-start(bf16[32,768]{1,0:T(8,128)(2,1)} %q_ref.3) | copy-start | bytes 147460
  1.7 1.0 %copy-start.1 = (bf16[32,768]{1,0:T(8,128)(2,1)S(1)}, bf16[32,768]{1,0:T(8,128)(2,1)}, u32[]{:S(2)}) copy-start(bf16[32,768]{1,0:T(8,128)(2,1)} %p_ref.3) | copy-start | bytes 147460
  2.8 6.5 %collective-permute-start.7 = (bf16[400,128]{1,0:T(8,128)(2,1)S(1)}, bf16[400,128]{1,0:T(8,128)(2,1)S(1)}, u32[]{:S(2)}, u32[]{:S(2)}) collective-permute-start(bf16[400,128]{1,0:T(8,128)(2,1)S(1)} %pack.2.refs_2_), channel_id=1, source_target_pairs={{24,0},{7,4},{25,1},{6,5},{26,2},{5,6},{27,3},{4,7},{16,8},{15,12}... | collective-permute-start | bytes 307208 | tf_op jit(solution)/shard_map/ppermute | solution.py:354
  6.6 4.7 %collective-permute-start.3 = (bf16[400,128]{1,0:T(8,128)(2,1)S(1)}, bf16[400,128]{1,0:T(8,128)(2,1)S(1)}, u32[]{:S(2)}, u32[]{:S(2)}) collective-permute-start(bf16[400,128]{1,0:T(8,128)(2,1)S(1)} %pack.2.refs_2_), channel_id=1, source_target_pairs={{8,0},{5,4},{9,1},{4,5},{10,2},{7,6},{11,3},{6,7},{0,8},{13,12},{1... | collective-permute-start | bytes 307208 | tf_op jit(solution)/shard_map/ppermute | solution.py:354
  7.1 5.2 %collective-permute-start.5 = (bf16[400,128]{1,0:T(8,128)(2,1)S(1)}, bf16[400,128]{1,0:T(8,128)(2,1)S(1)}, u32[]{:S(2)}, u32[]{:S(2)}) collective-permute-start(bf16[400,128]{1,0:T(8,128)(2,1)S(1)} %pack.2.refs_2_), channel_id=1, source_target_pairs={{16,0},{6,4},{17,1},{7,5},{18,2},{4,6},{19,3},{5,7},{24,8},{14,12}... | collective-permute-start | bytes 307208 | tf_op jit(solution)/shard_map/ppermute | solution.py:354
  9.2 3.2 %collective-permute-start.8 = (bf16[400,128]{1,0:T(8,128)(2,1)S(1)}, bf16[400,128]{1,0:T(8,128)(2,1)S(1)}, u32[]{:S(2)}, u32[]{:S(2)}) collective-permute-start(bf16[400,128]{1,0:T(8,128)(2,1)S(1)} %collective-permute-done.7.refs_5_.refs_6_), channel_id=1, source_target_pairs={{0,4},{4,0},{1,5},{5,1},{2,6},{6,2},{3,7},{7,3},{8,12},{12,8},{9,1... | collective-permute-start | bytes 307208 | tf_op jit(solution)/shard_map/ppermute | solution.py:322
  11.2 2.0 %collective-permute-start.4 = (bf16[400,128]{1,0:T(8,128)(2,1)S(1)}, bf16[400,128]{1,0:T(8,128)(2,1)S(1)}, u32[]{:S(2)}, u32[]{:S(2)}) collective-permute-start(bf16[400,128]{1,0:T(8,128)(2,1)S(1)} %collective-permute-done.3.refs_3_.refs_4_), channel_id=1, source_target_pairs={{0,4},{4,0},{1,5},{5,1},{2,6},{6,2},{3,7},{7,3},{8,12},{12,8},{9,1... | collective-permute-start | bytes 307208 | tf_op jit(solution)/shard_map/ppermute | solution.py:322
  12.3 1.3 %collective-permute-start.6 = (bf16[400,128]{1,0:T(8,128)(2,1)S(1)}, bf16[400,128]{1,0:T(8,128)(2,1)S(1)}, u32[]{:S(2)}, u32[]{:S(2)}) collective-permute-start(bf16[400,128]{1,0:T(8,128)(2,1)S(1)} %collective-permute-done.5.refs_4_.refs_5_), channel_id=1, source_target_pairs={{0,4},{4,0},{1,5},{5,1},{2,6},{6,2},{3,7},{7,3},{8,12},{12,8},{9,1... | collective-permute-start | bytes 307208 | tf_op jit(solution)/shard_map/ppermute | solution.py:322
  14.2 5.3 %collective-permute-start.9 = (f16[392,128]{1,0:T(8,128)(2,1)S(1)}, f16[392,128]{1,0:T(8,128)(2,1)S(1)}, u32[]{:S(2)}, u32[]{:S(2)}) collective-permute-start(f16[392,128]{1,0:T(8,128)(2,1)S(1)} %convert_element_type.33), channel_id=1, source_target_pairs={{0,16},{4,6},{1,17},{5,7},{2,18},{6,4},{3,19},{7,5},{8,24},{12,14}... | collective-permute-start | bytes 301064 | tf_op jit(solution)/shard_map/ppermute | solution.py:399
  15.8 5.6 %collective-permute-start.10 = (f16[392,128]{1,0:T(8,128)(2,1)S(1)}, f16[392,128]{1,0:T(8,128)(2,1)S(1)}, u32[]{:S(2)}, u32[]{:S(2)}) collective-permute-start(f16[392,128]{1,0:T(8,128)(2,1)S(1)} %convert_element_type.35), channel_id=1, source_target_pairs={{0,24},{4,7},{1,25},{5,6},{2,26},{6,5},{3,27},{7,4},{8,16},{12,15}... | collective-permute-start | bytes 301064 | tf_op jit(solution)/shard_map/ppermute | solution.py:399
  17.3 4.6 %collective-permute-start.13 = (f16[216,128]{1,0:T(8,128)(2,1)S(1)}, f16[216,128]{1,0:T(8,128)(2,1)S(1)}, u32[]{:S(2)}, u32[]{:S(2)}) collective-permute-start(f16[216,128]{1,0:T(8,128)(2,1)S(1)} %convert_element_type.40), channel_id=1, source_target_pairs={{0,8},{4,5},{1,9},{5,4},{2,10},{6,7},{3,11},{7,6},{8,0},{12,13},{9... | collective-permute-start | bytes 165896 | tf_op jit(solution)/shard_map/ppermute | solution.py:399
  17.9 4.7 %collective-permute-start.14 = (f16[232,128]{1,0:T(8,128)(2,1)S(1)}, f16[232,128]{1,0:T(8,128)(2,1)S(1)}, u32[]{:S(2)}, u32[]{:S(2)}) collective-permute-start(f16[232,128]{1,0:T(8,128)(2,1)S(1)} %convert_element_type.42), channel_id=1, source_target_pairs={{0,12},{4,1},{1,13},{5,0},{2,14},{6,3},{3,15},{7,2},{8,4},{12,9},{... | collective-permute-start | bytes 178184 | tf_op jit(solution)/shard_map/ppermute | solution.py:399
  19.5 3.2 %collective-permute-start.11 = (f16[208,128]{1,0:T(8,128)(2,1)S(1)}, f16[208,128]{1,0:T(8,128)(2,1)S(1)}, u32[]{:S(2)}, u32[]{:S(2)}) collective-permute-start(f16[208,128]{1,0:T(8,128)(2,1)S(1)} %convert_element_type.37), channel_id=1, source_target_pairs={{0,4},{4,0},{1,5},{5,1},{2,6},{6,2},{3,7},{7,3},{8,12},{12,8},{9,1... | collective-permute-start | bytes 159752 | tf_op jit(solution)/shard_map/ppermute | solution.py:322
  21.4 1.3 %collective-permute-start.12 = (f16[200,128]{1,0:T(8,128)(2,1)S(1)}, f16[200,128]{1,0:T(8,128)(2,1)S(1)}, u32[]{:S(2)}, u32[]{:S(2)}) collective-permute-start(f16[200,128]{1,0:T(8,128)(2,1)S(1)} %slice.4), channel_id=1, source_target_pairs={{0,4},{4,0},{1,5},{5,1},{2,6},{6,2},{3,7},{7,3},{8,12},{12,8},{9,1... | collective-permute-start | bytes 153608 | tf_op jit(solution)/shard_map/ppermute | solution.py:322

commit v11 on v9

--- a/solution.py
+++ b/solution.py
@@ -279,8 +279,9 @@
     write_partial(give_ref, jnp.concatenate(gives, axis=1))
 
 
-def end_kernel(loss_ref, keep_ref, here_ref, got_ref, there_ref, *refs):
-    last_refs, (keep_out, got_out) = refs[:-2], refs[-2:]
+def end_kernel(slab_ref, loss_ref, keep_ref, here_ref, got_ref, there_ref, *refs):
+    last_refs, (q_out, p_out) = refs[:-2], refs[-2:]
+    pick = functools.partial(jnp.where, (slab_ref[0] & 1) == 1)
     rows, width = keep_ref.shape
     loss = loss_ref[...][None]
     here = read_partials([here_ref], rows, 0)
@@ -288,8 +289,8 @@
     gots = read_partials([got_ref, there_ref, last_refs[1]], rows, 0)
     for i, (keep, a, b, got) in enumerate(zip(tiles(keep_ref[...]), here, keeps, gots)):
         lanes = slice(i * LANES, (i + 1) * LANES)
-        keep_out[:, lanes] = ((keep + a + b) * loss).reshape(rows, LANES)
-        got_out[:, lanes] = (got * loss).reshape(rows, LANES)
+        keep, got = (((x * loss).reshape(rows, LANES)) for x in (keep + a + b, got))
+        q_out[:, lanes], p_out[:, lanes] = pick(keep, got), pick(got, keep)
 
 
 VMEM = pl.BlockSpec(memory_space=pltpu.VMEM)
@@ -411,10 +412,14 @@
     )
     got = wide(swapped(give.astype(jnp.float16)))
     there = wide(swapped(arrived[-1][chunk_rows // 2 :]))
-    keep, got = call(
-        end_kernel, "end", (), (loss, keep, wide(arrived[-1]), got, there, *last), [half, half], 4
-    )
-    return jnp.where(core == 1, keep, got), jnp.where(core == 1, got, keep)
+    return call(
+        end_kernel,
+        "end",
+        (slab,),
+        (loss, keep, wide(arrived[-1]), got, there, *last),
+        [half, half],
+        4,
+    )
 
 
 def solution(mesh):

time: 23.7 us -> 23.8 us (level)
  other arithmetic: 0.91 us -> 0.21 us
  Pallas kernels: 1.83 us -> 2.51 us
    select_n x1 -> x0, other arithmetic: 0.69 us -> none  [local(): return (jnp.where(core == 1, keep, got), jnp.where(core == 1, got, keep))]
    pallas_call x8, Pallas kernels: 1.83 us -> 2.51 us  [call(): pl.pallas_call(kernel, out_shape=out_shape, in_specs=[SMEM] * len(scalars...]
  transfers between devices with their start and end apart: 15 -> 15, of which waited for: 7 -> 9; matrix products, arithmetic and copies ran while one was open for 1% -> 1% of each run, Pallas kernels for 5% -> 5%
where the time goes in v11:
time: 23.8 us; the launch traced here: 23.6 us
  starting transfers between devices  12.7 us (53%)
  waiting for transfers between devices  6.09 us (26%)
  Pallas kernels  2.51 us (11%)
  between operations  1.44 us (6%)
  local copies, waits for them, and re-layouts  0.69 us (3%)
    ppermute x4, starting transfers between devices, crossed(): lax.ppermute(partial.astype(jnp.float16), AXES, plan.group_pairs(turn, ac...  4.58 us
    ppermute x3, starting transfers between devices, local(): a_parts.append(lax.ppermute(mine, AXES, back))  4.5 us
    ppermute x8, starting transfers between devices, swapped(): return lax.ppermute(block, AXES, plan.core_pairs())  3.6 us
    ppermute x3, waiting for transfers between devices, local(): a_parts.append(lax.ppermute(mine, AXES, back))  2.82 us
    pallas_call x8, Pallas kernels, call(): pl.pallas_call(kernel, out_shape=out_shape, in_specs=[SMEM] * len(scalars...  2.51 us
    ppermute x4, waiting for transfers between devices, crossed(): lax.ppermute(partial.astype(jnp.float16), AXES, plan.group_pairs(turn, ac...  2.06 us
    ppermute x8, waiting for transfers between devices, swapped(): return lax.ppermute(block, AXES, plan.core_pairs())  1.21 us
    unnamed x8, local copies, waits for them, and re-layouts  0.67 us
  transfers between devices with their start and end apart: 15, of which 9 were waited for; matrix products, arithmetic and copies ran while one was open for 1% of the time, Pallas kernels for 5%

profile of v11, /device:TPU:0, one launch (start us, length us, event | category | flops | bytes accessed | tf_op | source)
XLA Modules:
  0.0 23.6 jit_solution(7208963992389420649)
XLA Ops:
  0.6 0.5 %collective-permute-start.2 = (f32[32]{0:T(128)}, f32[32]{0:T(128)S(1)}, u32[]{:S(2)}, u32[]{:S(2)}) collective-permute-start(f32[32]{0:T(128)} %param.7), channel_id=1, source_target_pairs={{0,4},{4,0},{1,5},{5,1},{2,6},{6,2},{3,7},{7,3},{8,12},{12,8},{9,1... | collective-permute-start | bytes 392 | tf_op jit(solution)/shard_map/ppermute | solution.py:321
  1.1 0.1 collective-permute-start
  1.2 0.4 %collective-permute-start.1 = (bf16[32,768]{1,0:T(8,128)(2,1)}, bf16[32,768]{1,0:T(8,128)(2,1)S(1)}, u32[]{:S(2)}, u32[]{:S(2)}) collective-permute-start(bf16[32,768]{1,0:T(8,128)(2,1)} %p_ref.1), channel_id=1, source_target_pairs={{0,4},{4,0},{1,5},{5,1},{2,6},{6,2},{3,7},{7,3},{8,12},{12,8},{9,1... | collective-permute-start | bytes 147464 | tf_op jit(solution)/shard_map/ppermute | solution.py:321
  1.7 0.0 copy-start.2
  1.7 0.0 copy-start.3
  1.7 0.0 copy-start
  1.7 0.0 copy-start.1
  1.7 0.7 %copy-done.2 = f32[256]{0:T(256)S(1)} copy-done((f32[256]{0:T(256)S(1)}, f32[256]{0:T(256)}, u32[]{:S(2)}) %copy-start.2) | copy-done | bytes 1048
  2.3 0.0 copy-done.3
  2.3 0.1 pad_maximum_fusion
  2.4 0.0 collective-permute-done.2
  2.4 0.2 collective-permute-done.got_q_ref
  2.6 0.2 collective-permute-done.1.got_p_ref
  2.8 0.0 copy-done
  2.8 0.0 copy-done.1
  2.8 0.1 pack.1
  2.9 3.9 %collective-permute-start.7 = (bf16[400,128]{1,0:T(8,128)(2,1)S(1)}, bf16[400,128]{1,0:T(8,128)(2,1)S(1)}, u32[]{:S(2)}, u32[]{:S(2)}) collective-permute-start(bf16[400,128]{1,0:T(8,128)(2,1)S(1)} %get-tuple-element.12.refs_2_), channel_id=1, source_target_pairs={{24,0},{7,4},{25,1},{6,5},{26,2},{5,6},{27,3},{4,7},{16,8},{15,12}... | collective-permute-start | bytes 307208 | tf_op jit(solution)/shard_map/ppermute | solution.py:357
  6.7 0.5 %collective-permute-start.5 = (bf16[400,128]{1,0:T(8,128)(2,1)S(1)}, bf16[400,128]{1,0:T(8,128)(2,1)S(1)}, u32[]{:S(2)}, u32[]{:S(2)}) collective-permute-start(bf16[400,128]{1,0:T(8,128)(2,1)S(1)} %get-tuple-element.12.refs_2_), channel_id=1, source_target_pairs={{16,0},{6,4},{17,1},{7,5},{18,2},{4,6},{19,3},{5,7},{24,8},{14,12}... | collective-permute-start | bytes 307208 | tf_op jit(solution)/shard_map/ppermute | solution.py:357
  7.2 0.1 collective-permute-start.3
  7.4 2.0 %collective-permute-done.7.refs_5_.refs_6_ = bf16[400,128]{1,0:T(8,128)(2,1)S(1)} collective-permute-done((bf16[400,128]{1,0:T(8,128)(2,1)S(1)}, bf16[400,128]{1,0:T(8,128)(2,1)S(1)}, u32[]{:S(2)}, u32[]{:S(2)}) %collective-permute-start.7) | collective-permute-done | bytes 102432 | tf_op jit(solution)/shard_map/ppermute | solution.py:357
  9.4 0.6 %collective-permute-start.8 = (bf16[400,128]{1,0:T(8,128)(2,1)S(1)}, bf16[400,128]{1,0:T(8,128)(2,1)S(1)}, u32[]{:S(2)}, u32[]{:S(2)}) collective-permute-start(bf16[400,128]{1,0:T(8,128)(2,1)S(1)} %collective-permute-done.7.refs_5_.refs_6_), channel_id=1, source_target_pairs={{0,4},{4,0},{1,5},{5,1},{2,6},{6,2},{3,7},{7,3},{8,12},{12,8},{9,1... | collective-permute-start | bytes 307208 | tf_op jit(solution)/shard_map/ppermute | solution.py:321
  10.6 0.8 %collective-permute-done.5.refs_4_.refs_5_ = bf16[400,128]{1,0:T(8,128)(2,1)S(1)} collective-permute-done((bf16[400,128]{1,0:T(8,128)(2,1)S(1)}, bf16[400,128]{1,0:T(8,128)(2,1)S(1)}, u32[]{:S(2)}, u32[]{:S(2)}) %collective-permute-start.5) | collective-permute-done | bytes 102432 | tf_op jit(solution)/shard_map/ppermute | solution.py:357
  11.4 1.0 %collective-permute-start.6 = (bf16[400,128]{1,0:T(8,128)(2,1)S(1)}, bf16[400,128]{1,0:T(8,128)(2,1)S(1)}, u32[]{:S(2)}, u32[]{:S(2)}) collective-permute-start(bf16[400,128]{1,0:T(8,128)(2,1)S(1)} %collective-permute-done.5.refs_4_.refs_5_), channel_id=1, source_target_pairs={{0,4},{4,0},{1,5},{5,1},{2,6},{6,2},{3,7},{7,3},{8,12},{12,8},{9,1... | collective-permute-start | bytes 307208 | tf_op jit(solution)/shard_map/ppermute | solution.py:321
  12.4 0.0 collective-permute-done.3.refs_3_.refs_4_
  12.4 0.0 collective-permute-start.4
  12.4 0.0 collective-permute-done.8.refs_6_.refs_7_
  12.4 0.5 %early.1 = (f32[192,768]{1,0:T(8,128)S(1)}, f32[192,128]{1,0:T(8,128)S(1)}) custom-call(s32[1]{0:T(128)} %bitcast.slab_ref.refs_0_, s32[1]{0:T(128)} %bitcast.2.refs_1_, f32[8,128]{1,0:T(8,128)S(1)} %spread.1.refs_2_.loss_ref, bf16[400,128]{1,0:T(8,128)(2,1)S(1)} %collective-permute-done.3.refs_3_.refs_4_, ...), custom_call_target="tpu_custom_call" | custom-call | flops 1000000000 | tf_op jit(solution)/shard_map/early/pallas_call | solution.py:301
  12.9 0.4 %collective-permute-done.6.refs_5_.refs_8_ = bf16[400,128]{1,0:T(8,128)(2,1)S(1)} collective-permute-done((bf16[400,128]{1,0:T(8,128)(2,1)S(1)}, bf16[400,128]{1,0:T(8,128)(2,1)S(1)}, u32[]{:S(2)}, u32[]{:S(2)}) %collective-permute-start.6) | collective-permute-done | bytes 102432 | tf_op jit(solution)/shard_map/ppermute | solution.py:321
  13.3 0.4 %collective-permute-done.4.refs_4_.refs_7_ = bf16[400,128]{1,0:T(8,128)(2,1)S(1)} collective-permute-done((bf16[400,128]{1,0:T(8,128)(2,1)S(1)}, bf16[400,128]{1,0:T(8,128)(2,1)S(1)}, u32[]{:S(2)}, u32[]{:S(2)}) %collective-permute-start.4) | collective-permute-done | bytes 102432 | tf_op jit(solution)/shard_map/ppermute | solution.py:321
  13.7 0.6 %late.1 = (f32[216,128]{1,0:T(8,128)S(1)}, f32[232,128]{1,0:T(8,128)S(1)}, f32[392,128]{1,0:T(8,128)S(1)}, f32[392,128]{1,0:T(8,128)S(1)}) custom-call(s32[1]{0:T(128)} %bitcast.slab_ref.refs_0_, s32[1]{0:T(128)} %bitcast.2.refs_1_, f32[192,768]{1,0:T(8,128)S(1)} %get-tuple-element.14.refs_2_, f32[192,128]{1,0:T(8,128)S(1)} %get-tuple-element.15.refs_3_, ...), custom_call_target="tpu_custom_call" | custom-call | tf_op jit(solution)/shard_map/late/pallas_call | solution.py:301
  14.3 1.6 %collective-permute-start.9 = (f16[392,128]{1,0:T(8,128)(2,1)S(1)}, f16[392,128]{1,0:T(8,128)(2,1)S(1)}, u32[]{:S(2)}, u32[]{:S(2)}) collective-permute-start(f16[392,128]{1,0:T(8,128)(2,1)S(1)} %convert_element_type.33), channel_id=1, source_target_pairs={{0,16},{4,6},{1,17},{5,7},{2,18},{6,4},{3,19},{7,5},{8,24},{12,14}... | collective-permute-start | bytes 301064 | tf_op jit(solution)/shard_map/ppermute | solution.py:402
  15.9 1.5 %collective-permute-start.10 = (f16[392,128]{1,0:T(8,128)(2,1)S(1)}, f16[392,128]{1,0:T(8,128)(2,1)S(1)}, u32[]{:S(2)}, u32[]{:S(2)}) collective-permute-start(f16[392,128]{1,0:T(8,128)(2,1)S(1)} %convert_element_type.35), channel_id=1, source_target_pairs={{0,24},{4,7},{1,25},{5,6},{2,26},{6,5},{3,27},{7,4},{8,16},{12,15}... | collective-permute-start | bytes 301064 | tf_op jit(solution)/shard_map/ppermute | solution.py:402
  17.4 0.6 %collective-permute-start.13 = (f16[216,128]{1,0:T(8,128)(2,1)S(1)}, f16[216,128]{1,0:T(8,128)(2,1)S(1)}, u32[]{:S(2)}, u32[]{:S(2)}) collective-permute-start(f16[216,128]{1,0:T(8,128)(2,1)S(1)} %convert_element_type.40), channel_id=1, source_target_pairs={{0,8},{4,5},{1,9},{5,4},{2,10},{6,7},{3,11},{7,6},{8,0},{12,13},{9... | collective-permute-start | bytes 165896 | tf_op jit(solution)/shard_map/ppermute | solution.py:402
  18.0 0.9 %collective-permute-start.14 = (f16[232,128]{1,0:T(8,128)(2,1)S(1)}, f16[232,128]{1,0:T(8,128)(2,1)S(1)}, u32[]{:S(2)}, u32[]{:S(2)}) collective-permute-start(f16[232,128]{1,0:T(8,128)(2,1)S(1)} %convert_element_type.42), channel_id=1, source_target_pairs={{0,12},{4,1},{1,13},{5,0},{2,14},{6,3},{3,15},{7,2},{8,4},{12,9},{... | collective-permute-start | bytes 178184 | tf_op jit(solution)/shard_map/ppermute | solution.py:402
  18.9 0.5 %own.1.own_ref = f32[64,768]{1,0:T(8,128)S(1)} custom-call(s32[1]{0:T(128)} %bitcast.slab_ref.refs_0_, s32[1]{0:T(128)} %bitcast.2.refs_1_, bf16[400,128]{1,0:T(8,128)(2,1)S(1)} %get-tuple-element.12.refs_2_, bf16[400,128]{1,0:T(8,128)(2,1)S(1)} %get-tuple-element.13.refs_3_.refs_6_, bf16[400,128]{1,0:T(8,128)(2,1)S(1)} %collective-permute-done.4.refs_4_.refs_7_, ...), custom_call_target="tpu_custom_call" | custom-call | flops 1000000000 | tf_op jit(solution)/shard_map/own/pallas_call | solution.py:301
  19.4 0.0 collective-permute-done.9
  19.5 0.6 %collective-permute-start.11 = (f16[208,128]{1,0:T(8,128)(2,1)S(1)}, f16[208,128]{1,0:T(8,128)(2,1)S(1)}, u32[]{:S(2)}, u32[]{:S(2)}) collective-permute-start(f16[208,128]{1,0:T(8,128)(2,1)S(1)} %convert_element_type.37), channel_id=1, source_target_pairs={{0,4},{4,0},{1,5},{5,1},{2,6},{6,2},{3,7},{7,3},{8,12},{12,8},{9,1... | collective-permute-start | bytes 159752 | tf_op jit(solution)/shard_map/ppermute | solution.py:321
  20.1 1.4 %collective-permute-done.10 = f16[392,128]{1,0:T(8,128)(2,1)S(1)} collective-permute-done((f16[392,128]{1,0:T(8,128)(2,1)S(1)}, f16[392,128]{1,0:T(8,128)(2,1)S(1)}, u32[]{:S(2)}, u32[]{:S(2)}) %collective-permute-start.10) | collective-permute-done | bytes 100384 | tf_op jit(solution)/shard_map/ppermute | solution.py:402
  21.5 0.4 %collective-permute-start.12 = (f16[200,128]{1,0:T(8,128)(2,1)S(1)}, f16[200,128]{1,0:T(8,128)(2,1)S(1)}, u32[]{:S(2)}, u32[]{:S(2)}) collective-permute-start(f16[200,128]{1,0:T(8,128)(2,1)S(1)} %slice.4), channel_id=1, source_target_pairs={{0,4},{4,0},{1,5},{5,1},{2,6},{6,2},{3,7},{7,3},{8,12},{12,8},{9,1... | collective-permute-start | bytes 153608 | tf_op jit(solution)/shard_map/ppermute | solution.py:321
  22.0 0.0 collective-permute-done.13
  22.0 0.7 %collective-permute-done.14 = f16[232,128]{1,0:T(8,128)(2,1)S(1)} collective-permute-done((f16[232,128]{1,0:T(8,128)(2,1)S(1)}, f16[232,128]{1,0:T(8,128)(2,1)S(1)}, u32[]{:S(2)}, u32[]{:S(2)}) %collective-permute-start.14) | collective-permute-done | bytes 59424 | tf_op jit(solution)/shard_map/ppermute | solution.py:402
  22.7 0.1 collective-permute-done.12
  22.9 0.0 collective-permute-done.11
  22.9 0.7 %end.1 = (f32[32,768]{1,0:T(8,128)}, f32[32,768]{1,0:T(8,128)}) custom-call(s32[1]{0:T(128)} %bitcast.slab_ref.refs_0_, f32[8,128]{1,0:T(8,128)S(1)} %spread.1.refs_2_.loss_ref, f32[32,768]{1,0:T(8,128)S(1)} %get-tuple-element.17.keep_ref, f32[392,128]{1,0:T(8,128)S(1)} %convert_element_type.36.here_ref, f32[208,128]{1,0:T(8,128)S(1)} %convert_element_type.38.got_ref, ...), custom_call_target="tpu_custom_call" | custom-call | tf_op jit(solution)/shard_map/end/pallas_call | solution.py:301
  (16 shorter events, 0.2 us)
Async XLA Ops:
  0.6 1.8 %collective-permute-start.2 = (f32[32]{0:T(128)}, f32[32]{0:T(128)S(1)}, u32[]{:S(2)}, u32[]{:S(2)}) collective-permute-start(f32[32]{0:T(128)} %param.7), channel_id=1, source_target_pairs={{0,4},{4,0},{1,5},{5,1},{2,6},{6,2},{3,7},{7,3},{8,12},{12,8},{9,1... | collective-permute-start | bytes 392 | tf_op jit(solution)/shard_map/ppermute | solution.py:321
  1.1 1.4 %collective-permute-start = (bf16[32,768]{1,0:T(8,128)(2,1)}, bf16[32,768]{1,0:T(8,128)(2,1)S(1)}, u32[]{:S(2)}, u32[]{:S(2)}) collective-permute-start(bf16[32,768]{1,0:T(8,128)(2,1)} %q_ref.1), channel_id=1, source_target_pairs={{0,4},{4,0},{1,5},{5,1},{2,6},{6,2},{3,7},{7,3},{8,12},{12,8},{9,1... | collective-permute-start | bytes 147464 | tf_op jit(solution)/shard_map/ppermute | solution.py:321
  1.2 1.5 %collective-permute-start.1 = (bf16[32,768]{1,0:T(8,128)(2,1)}, bf16[32,768]{1,0:T(8,128)(2,1)S(1)}, u32[]{:S(2)}, u32[]{:S(2)}) collective-permute-start(bf16[32,768]{1,0:T(8,128)(2,1)} %p_ref.1), channel_id=1, source_target_pairs={{0,4},{4,0},{1,5},{5,1},{2,6},{6,2},{3,7},{7,3},{8,12},{12,8},{9,1... | collective-permute-start | bytes 147464 | tf_op jit(solution)/shard_map/ppermute | solution.py:321
  1.7 0.7 %copy-start.2 = (f32[256]{0:T(256)S(1)}, f32[256]{0:T(256)}, u32[]{:S(2)}) copy-start(f32[256]{0:T(256)} %param.8) | copy-start | bytes 3076
  1.7 0.7 %copy-start.3 = (f32[32]{0:T(128)S(1)}, f32[32]{0:T(128)}, u32[]{:S(2)}) copy-start(f32[32]{0:T(128)} %param.7) | copy-start | bytes 388
  1.7 1.1 %copy-start = (bf16[32,768]{1,0:T(8,128)(2,1)S(1)}, bf16[32,768]{1,0:T(8,128)(2,1)}, u32[]{:S(2)}) copy-start(bf16[32,768]{1,0:T(8,128)(2,1)} %q_ref.1) | copy-start | bytes 147460
  1.7 1.1 %copy-start.1 = (bf16[32,768]{1,0:T(8,128)(2,1)S(1)}, bf16[32,768]{1,0:T(8,128)(2,1)}, u32[]{:S(2)}) copy-start(bf16[32,768]{1,0:T(8,128)(2,1)} %p_ref.1) | copy-start | bytes 147460
  2.9 6.5 %collective-permute-start.7 = (bf16[400,128]{1,0:T(8,128)(2,1)S(1)}, bf16[400,128]{1,0:T(8,128)(2,1)S(1)}, u32[]{:S(2)}, u32[]{:S(2)}) collective-permute-start(bf16[400,128]{1,0:T(8,128)(2,1)S(1)} %get-tuple-element.12.refs_2_), channel_id=1, source_target_pairs={{24,0},{7,4},{25,1},{6,5},{26,2},{5,6},{27,3},{4,7},{16,8},{15,12}... | collective-permute-start | bytes 307208 | tf_op jit(solution)/shard_map/ppermute | solution.py:357
  6.7 4.7 %collective-permute-start.5 = (bf16[400,128]{1,0:T(8,128)(2,1)S(1)}, bf16[400,128]{1,0:T(8,128)(2,1)S(1)}, u32[]{:S(2)}, u32[]{:S(2)}) collective-permute-start(bf16[400,128]{1,0:T(8,128)(2,1)S(1)} %get-tuple-element.12.refs_2_), channel_id=1, source_target_pairs={{16,0},{6,4},{17,1},{7,5},{18,2},{4,6},{19,3},{5,7},{24,8},{14,12}... | collective-permute-start | bytes 307208 | tf_op jit(solution)/shard_map/ppermute | solution.py:357
  7.2 5.1 %collective-permute-start.3 = (bf16[400,128]{1,0:T(8,128)(2,1)S(1)}, bf16[400,128]{1,0:T(8,128)(2,1)S(1)}, u32[]{:S(2)}, u32[]{:S(2)}) collective-permute-start(bf16[400,128]{1,0:T(8,128)(2,1)S(1)} %get-tuple-element.12.refs_2_), channel_id=1, source_target_pairs={{8,0},{5,4},{9,1},{4,5},{10,2},{7,6},{11,3},{6,7},{0,8},{13,12},{1... | collective-permute-start | bytes 307208 | tf_op jit(solution)/shard_map/ppermute | solution.py:357
  9.4 3.0 %collective-permute-start.8 = (bf16[400,128]{1,0:T(8,128)(2,1)S(1)}, bf16[400,128]{1,0:T(8,128)(2,1)S(1)}, u32[]{:S(2)}, u32[]{:S(2)}) collective-permute-start(bf16[400,128]{1,0:T(8,128)(2,1)S(1)} %collective-permute-done.7.refs_5_.refs_6_), channel_id=1, source_target_pairs={{0,4},{4,0},{1,5},{5,1},{2,6},{6,2},{3,7},{7,3},{8,12},{12,8},{9,1... | collective-permute-start | bytes 307208 | tf_op jit(solution)/shard_map/ppermute | solution.py:321
  11.4 1.9 %collective-permute-start.6 = (bf16[400,128]{1,0:T(8,128)(2,1)S(1)}, bf16[400,128]{1,0:T(8,128)(2,1)S(1)}, u32[]{:S(2)}, u32[]{:S(2)}) collective-permute-start(bf16[400,128]{1,0:T(8,128)(2,1)S(1)} %collective-permute-done.5.refs_4_.refs_5_), channel_id=1, source_target_pairs={{0,4},{4,0},{1,5},{5,1},{2,6},{6,2},{3,7},{7,3},{8,12},{12,8},{9,1... | collective-permute-start | bytes 307208 | tf_op jit(solution)/shard_map/ppermute | solution.py:321
  12.4 1.3 %collective-permute-start.4 = (bf16[400,128]{1,0:T(8,128)(2,1)S(1)}, bf16[400,128]{1,0:T(8,128)(2,1)S(1)}, u32[]{:S(2)}, u32[]{:S(2)}) collective-permute-start(bf16[400,128]{1,0:T(8,128)(2,1)S(1)} %collective-permute-done.3.refs_3_.refs_4_), channel_id=1, source_target_pairs={{0,4},{4,0},{1,5},{5,1},{2,6},{6,2},{3,7},{7,3},{8,12},{12,8},{9,1... | collective-permute-start | bytes 307208 | tf_op jit(solution)/shard_map/ppermute | solution.py:321
  14.3 5.1 %collective-permute-start.9 = (f16[392,128]{1,0:T(8,128)(2,1)S(1)}, f16[392,128]{1,0:T(8,128)(2,1)S(1)}, u32[]{:S(2)}, u32[]{:S(2)}) collective-permute-start(f16[392,128]{1,0:T(8,128)(2,1)S(1)} %convert_element_type.33), channel_id=1, source_target_pairs={{0,16},{4,6},{1,17},{5,7},{2,18},{6,4},{3,19},{7,5},{8,24},{12,14}... | collective-permute-start | bytes 301064 | tf_op jit(solution)/shard_map/ppermute | solution.py:402
  15.9 5.6 %collective-permute-start.10 = (f16[392,128]{1,0:T(8,128)(2,1)S(1)}, f16[392,128]{1,0:T(8,128)(2,1)S(1)}, u32[]{:S(2)}, u32[]{:S(2)}) collective-permute-start(f16[392,128]{1,0:T(8,128)(2,1)S(1)} %convert_element_type.35), channel_id=1, source_target_pairs={{0,24},{4,7},{1,25},{5,6},{2,26},{6,5},{3,27},{7,4},{8,16},{12,15}... | collective-permute-start | bytes 301064 | tf_op jit(solution)/shard_map/ppermute | solution.py:402
  17.4 4.5 %collective-permute-start.13 = (f16[216,128]{1,0:T(8,128)(2,1)S(1)}, f16[216,128]{1,0:T(8,128)(2,1)S(1)}, u32[]{:S(2)}, u32[]{:S(2)}) collective-permute-start(f16[216,128]{1,0:T(8,128)(2,1)S(1)} %convert_element_type.40), channel_id=1, source_target_pairs={{0,8},{4,5},{1,9},{5,4},{2,10},{6,7},{3,11},{7,6},{8,0},{12,13},{9... | collective-permute-start | bytes 165896 | tf_op jit(solution)/shard_map/ppermute | solution.py:402
  18.0 4.6 %collective-permute-start.14 = (f16[232,128]{1,0:T(8,128)(2,1)S(1)}, f16[232,128]{1,0:T(8,128)(2,1)S(1)}, u32[]{:S(2)}, u32[]{:S(2)}) collective-permute-start(f16[232,128]{1,0:T(8,128)(2,1)S(1)} %convert_element_type.42), channel_id=1, source_target_pairs={{0,12},{4,1},{1,13},{5,0},{2,14},{6,3},{3,15},{7,2},{8,4},{12,9},{... | collective-permute-start | bytes 178184 | tf_op jit(solution)/shard_map/ppermute | solution.py:402
  19.5 3.3 %collective-permute-start.11 = (f16[208,128]{1,0:T(8,128)(2,1)S(1)}, f16[208,128]{1,0:T(8,128)(2,1)S(1)}, u32[]{:S(2)}, u32[]{:S(2)}) collective-permute-start(f16[208,128]{1,0:T(8,128)(2,1)S(1)} %convert_element_type.37), channel_id=1, source_target_pairs={{0,4},{4,0},{1,5},{5,1},{2,6},{6,2},{3,7},{7,3},{8,12},{12,8},{9,1... | collective-permute-start | bytes 159752 | tf_op jit(solution)/shard_map/ppermute | solution.py:321
  21.5 1.3 %collective-permute-start.12 = (f16[200,128]{1,0:T(8,128)(2,1)S(1)}, f16[200,128]{1,0:T(8,128)(2,1)S(1)}, u32[]{:S(2)}, u32[]{:S(2)}) collective-permute-start(f16[200,128]{1,0:T(8,128)(2,1)S(1)} %slice.4), channel_id=1, source_target_pairs={{0,4},{4,0},{1,5},{5,1},{2,6},{6,2},{3,7},{7,3},{8,12},{12,8},{9,1... | collective-permute-start | bytes 153608 | tf_op jit(solution)/shard_map/ppermute | solution.py:321
